TPU v7x, 128 devices: a whole 4x4x4 slice. The times are simulated.
128 devices in a mesh: row: 16 (over z, y_hi, core), col: 8 (over x, y_lo).
Axes of the slice: x: 4, y: 4 (y_hi: 2, y_lo: 2; y = y_hi * 2 + y_lo), z: 4, core: 2. Of those that a mesh axis runs over, the one named last changes fastest.
Arguments:
- a_blocks: float32 [7168, 128, 128], P(('row', 'col')), may hold values from -0.1875 to 0.1875
- a_pick: int32 [16384], P(('row', 'col')), may hold values from 0 to 56, as said below
- a_place: int32 [7168], P(('row', 'col')), may hold values from 0 to 127, as said below
- b_blocks: float32 [7168, 128, 128], P(('row', 'col')), may hold values from -6 to 6
- b_pick: int32 [16384], P(('row', 'col')), may hold values from 0 to 56, as said below
- b_place: int32 [7168], P(('row', 'col')), may hold values from 0 to 127, as said below
- prod_a: int32 [4, 8192], P(None, ('row', 'col')), may hold values from 0 to 55
- prod_b: int32 [4, 8192], P(None, ('row', 'col')), may hold values from 0 to 55
- prod_c: int32 [4, 8192], P(None, ('row', 'col')), may hold values from 0 to 64, as said below
Outputs:
- c_blocks: float32 [8192, 128, 128], P(('row', 'col'))
Inputs may be any that keep to these rules, and one draw needn't show every extreme that they name: `a_pick`: 56 marks an empty send slot; every source fills 56 slots, at most 1 to any one device, and exactly 1 to some device. `a_place`: each device's list names 56 distinct filled arrived slots. `b_pick`: 56 marks an empty send slot; every source fills 56 slots, at most 1 to any one device, and exactly 1 to some device. `b_place`: each device's list names 56 distinct filled arrived slots. `prod_c`: 64 marks an unused entry; in every step some device uses all 64 entries and every device uses a third of them or more.
All inputs are finite; a program needn't handle non-finite values.
Results may differ from a plain program's by a relative error of at most 0.0003.
Values sent between devices are 32-bit elements; how exact they have to be, the bound alone decides.
No kernel may reach another device: no remote copies, remote signals or barrier semaphores. Data moves between devices by JAX's collectives and lax.ppermute only.
A program may use at most 128 MiB of HBM per device.

v0:
```python
import jax
import jax.numpy as jnp
from jax import lax
from jax.sharding import PartitionSpec as P

CBLK = 64


def from_behind(array, axis, by):
    peers = lax.axis_size(axis)
    return lax.ppermute(array, axis, [(i, (i + by) % peers) for i in range(peers)])


def stack_product(panel_a, panel_b, index_a, index_b, index_c):
    left = jnp.take(panel_a, index_a, axis=0)
    right = jnp.take(panel_b, index_b, axis=0)
    products = jnp.einsum(
        "pij,pjk->pik",
        left,
        right,
        precision=lax.Precision.HIGHEST,
        preferred_element_type=jnp.float32,
    )
    return jax.ops.segment_sum(products, index_c, num_segments=CBLK)


def local(a_blocks, a_pick, a_place, b_blocks, b_pick, b_place, prod_a, prod_b, prod_c):
    grid_rows = lax.axis_size("row")
    grid_cols = lax.axis_size("col")
    devices = grid_rows * grid_cols
    capacity = a_pick.shape[0] // devices
    width = a_blocks.shape[1]
    outgoing = jnp.stack(
        [
            jnp.take(a_blocks, a_pick, axis=0, mode="fill", fill_value=0.0),
            jnp.take(b_blocks, b_pick, axis=0, mode="fill", fill_value=0.0),
        ]
    )
    arrived = lax.all_to_all(
        outgoing.reshape(2, devices, capacity, width, width),
        ("row", "col"),
        split_axis=1,
        concat_axis=1,
        tiled=True,
    )
    arrived = arrived.reshape(2, devices * capacity, width, width)
    panel_a = jnp.take(arrived[0], a_place, axis=0)
    panel_b = jnp.take(arrived[1], b_place, axis=0)
    steps = prod_a.shape[0]
    total = jnp.zeros((CBLK, width, width), jnp.float32)
    for step in range(steps):
        if step > 0:
            panel_a = from_behind(panel_a, "col", -1)
            panel_b = from_behind(panel_b, "row", -1)
        total = total + stack_product(panel_a, panel_b, prod_a[step], prod_b[step], prod_c[step])
    return total


def solution(mesh):
    placed = (
        P(("row", "col"), None, None),
        P(("row", "col")),
        P(("row", "col")),
        P(("row", "col"), None, None),
        P(("row", "col")),
        P(("row", "col")),
        P(None, ("row", "col")),
        P(None, ("row", "col")),
        P(None, ("row", "col")),
    )
    return jax.shard_map(
        local, mesh=mesh, in_specs=placed, out_specs=P(("row", "col"), None, None), check_vma=False
    )
```

profile of v0, /device:TPU:0, one launch (start us, length us, event | category | flops | bytes accessed | tf_op | source)
XLA Modules:
  0.0 769.8 jit_solution(15040684696568830643)
XLA Ops:
  0.0 0.7 compare_select_fusion.10
  0.7 0.7 compare_and_fusion.10
  1.3 0.7 compare_select_fusion.11
  2.0 0.7 compare_and_fusion.11
  2.7 6.3 gather_fusion
  9.0 6.4 gather_fusion.1
  15.4 6.6 select_bitcast_fusion
  22.0 6.0 maximum_bitcast_fusion
  28.0 11.7 %all-to-all-start = ((f32[2,128,1,128,128]{4,3,0,2,1:T(8,128)}), f32[2,128,1,128,128]{4,3,0,2,1:T(8,128)}, u32[]{:S(2)}, u32[]{:S(2)}) async-start(f32[2,128,1,128,128]{4,3,0,2,1:T(8,128)} %maximum_bitcast_fusion), calls=%async_computation | async-start | bytes 33554432 | tf_op jit(solution)/shard_map/all_to_all | solution.py:39
  39.8 228.7 %all-to-all-done = f32[2,128,1,128,128]{4,3,0,2,1:T(8,128)} async-done(((f32[2,128,1,128,128]{4,3,0,2,1:T(8,128)}), f32[2,128,1,128,128]{4,3,0,2,1:T(8,128)}, u32[]{:S(2)}, u32[]{:S(2)}) %all-to-all-start) | async-done | bytes 16777248 | tf_op jit(solution)/shard_map/all_to_all | solution.py:39
  268.5 10.9 %slice_bitcast_fusion.1 = (f32[128,128,128]{2,1,0:T(8,128)}, f32[128,128,128]{2,1,0:T(8,128)}) fusion(f32[2,128,1,128,128]{4,3,0,2,1:T(8,128)} %all-to-all-done), kind=kLoop, calls=%fused_computation.18 | loop fusion | bytes 33554432 | tf_op jit(solution)/shard_map/squeeze | solution.py:47
  279.4 6.0 gather_fusion.2
  285.4 4.1 broadcast_select_fusion.1
  289.5 4.9 collective-permute-start
  294.4 6.0 gather_fusion.4
  300.4 2.4 broadcast_select_fusion
  302.8 1.8 copy-done
  304.6 3.0 collective-permute-start.1
  307.6 65.6 %collective-permute-done = f32[56,128,128]{2,1,0:T(8,128)} collective-permute-done((f32[56,128,128]{2,1,0:T(8,128)}, f32[56,128,128]{2,1,0:T(8,128)}, u32[]{:S(2)}, u32[]{:S(2)}) %collective-permute-start) | collective-permute-done | bytes 3670048 | tf_op jit(solution)/shard_map/ppermute | solution.py:11
  373.2 4.6 collective-permute-start.2
  377.8 106.0 %collective-permute-done.1 = f32[56,128,128]{2,1,0:T(8,128)S(1)} collective-permute-done((f32[56,128,128]{2,1,0:T(8,128)S(1)}, f32[56,128,128]{2,1,0:T(8,128)S(1)}, u32[]{:S(2)}, u32[]{:S(2)}) %collective-permute-start.1) | collective-permute-done | bytes 3670048 | tf_op jit(solution)/shard_map/ppermute | solution.py:11
  483.8 1.9 copy-done.1
  485.7 5.5 collective-permute-start.3
  491.2 0.0 collective-permute-done.2
  491.2 0.1 collective-permute-start.4
  491.4 118.9 %collective-permute-done.3 = f32[56,128,128]{2,1,0:T(8,128)} collective-permute-done((f32[56,128,128]{2,1,0:T(8,128)S(1)}, f32[56,128,128]{2,1,0:T(8,128)}, u32[]{:S(2)}, u32[]{:S(2)}) %collective-permute-start.3) | collective-permute-done | bytes 3670048 | tf_op jit(solution)/shard_map/ppermute | solution.py:11
  610.3 5.6 collective-permute-start.5
  616.1 4.8 gather_fusion.3
  620.9 4.9 gather_fusion.5
  625.7 10.1 %fusion.9 = f32[64,128,128]{2,1,0:T(8,128)} fusion(f32[64,128,128]{2,1,0:T(8,128)} %gather_fusion.5, f32[64,128,128]{2,1,0:T(8,128)} %gather_fusion.3, pred[64]{0:T(512)(128)(4,1)S(1)} %get-tuple-element.34, pred[64]{0:T(512)(128)(4,1)S(1)} %get-tuple-element.46), kind=kOutput, calls=%fused_computation.30 | convolution fusion | flops 1612709888 | bytes 12583040 | tf_op jit(solution)/shard_map/pij,pjk->pik/dot_general | solution.py:17
  635.8 2.5 broadcast.12.clone
  638.4 13.5 %scatter_fusion = f32[64,128,128]{2,1,0:T(8,128)} fusion(f32[64,128,128]{2,1,0:T(8,128)} %broadcast.12.clone, s32[64]{0:T(128)S(1)} %get-tuple-element.40, f32[64,128,128]{2,1,0:T(8,128)} %fusion.9), kind=kCustom, calls=%fused_computation.12 | custom fusion | flops 1048576 | bytes 12583168 | tf_op jit(solution)/shard_map/scatter-add | solution.py:24
  651.9 4.8 gather_fusion.6
  656.7 4.8 gather_fusion.7
  661.5 10.1 %fusion.6 = f32[64,128,128]{2,1,0:T(8,128)} fusion(f32[64,128,128]{2,1,0:T(8,128)} %gather_fusion.7, f32[64,128,128]{2,1,0:T(8,128)} %gather_fusion.6, pred[64]{0:T(512)(128)(4,1)S(1)} %get-tuple-element.32, pred[64]{0:T(512)(128)(4,1)S(1)} %get-tuple-element.48), kind=kOutput, calls=%fused_computation.27 | convolution fusion | flops 1612709888 | bytes 12583040 | tf_op jit(solution)/shard_map/pij,pjk->pik/dot_general | solution.py:17
  671.6 2.5 broadcast.12.clone.1
  674.0 14.4 %scatter_fusion.1 = f32[64,128,128]{2,1,0:T(8,128)} fusion(f32[64,128,128]{2,1,0:T(8,128)} %broadcast.12.clone.1, s32[64]{0:T(128)S(1)} %get-tuple-element.39, f32[64,128,128]{2,1,0:T(8,128)} %fusion.6), kind=kCustom, calls=%fused_computation.13 | custom fusion | flops 1048576 | bytes 12583168 | tf_op jit(solution)/shard_map/scatter-add | solution.py:24
  688.5 6.6 add.34
  695.0 4.8 gather_fusion.8
  699.9 4.8 gather_fusion.9
  704.7 10.1 %fusion.3 = f32[64,128,128]{2,1,0:T(8,128)} fusion(f32[64,128,128]{2,1,0:T(8,128)} %gather_fusion.9, f32[64,128,128]{2,1,0:T(8,128)} %gather_fusion.8, pred[64]{0:T(512)(128)(4,1)S(1)} %get-tuple-element.36, pred[64]{0:T(512)(128)(4,1)S(1)} %get-tuple-element.44), kind=kOutput, calls=%fused_computation.24 | convolution fusion | flops 1612709888 | bytes 12583040 | tf_op jit(solution)/shard_map/pij,pjk->pik/dot_general | solution.py:17
  714.7 13.1 %scatter_fusion.2 = f32[64,128,128]{2,1,0:T(8,128)} fusion(f32[64,128,128]{2,1,0:T(8,128)} %add.34, s32[64]{0:T(128)S(1)} %get-tuple-element.41, f32[64,128,128]{2,1,0:T(8,128)} %fusion.3), kind=kCustom, calls=%fused_computation.14 | custom fusion | flops 1048576 | bytes 12583168 | tf_op jit(solution)/shard_map/scatter-add | solution.py:24
  727.9 4.8 gather_fusion.10
  732.7 4.8 gather_fusion.11
  737.5 10.1 %fusion = f32[64,128,128]{2,1,0:T(8,128)} fusion(f32[64,128,128]{2,1,0:T(8,128)} %gather_fusion.11, f32[64,128,128]{2,1,0:T(8,128)} %gather_fusion.10, pred[64]{0:T(512)(128)(4,1)S(1)} %get-tuple-element.10, pred[64]{0:T(512)(128)(4,1)S(1)} %get-tuple-element.50), kind=kOutput, calls=%fused_computation.21 | convolution fusion | flops 1612709888 | bytes 12583040 | tf_op jit(solution)/shard_map/pij,pjk->pik/dot_general | solution.py:17
  747.6 2.5 broadcast.12.clone.2
  750.0 13.2 %scatter_fusion.3 = f32[64,128,128]{2,1,0:T(8,128)} fusion(f32[64,128,128]{2,1,0:T(8,128)} %broadcast.12.clone.2, s32[64]{0:T(128)S(1)} %get-tuple-element.38, f32[64,128,128]{2,1,0:T(8,128)} %fusion), kind=kCustom, calls=%fused_computation.15 | custom fusion | flops 1048576 | bytes 12583168 | tf_op jit(solution)/shard_map/scatter-add | solution.py:24
  763.2 6.6 add.35
  (32 shorter events, 0.1 us)
Async XLA Ops:
  28.0 11.7 %copy-start.5 = (s32[56]{0:T(128)S(1)}, s32[56]{0:T(128)}, u32[]{:S(2)}) copy-start(s32[56]{0:T(128)} %param.17) | copy-start | bytes 676
  28.0 11.7 %copy-start.6 = (s32[56]{0:T(128)S(1)}, s32[56]{0:T(128)}, u32[]{:S(2)}) copy-start(s32[56]{0:T(128)} %param.20) | copy-start | bytes 676
  28.0 240.5 %all-to-all-start = ((f32[2,128,1,128,128]{4,3,0,2,1:T(8,128)}), f32[2,128,1,128,128]{4,3,0,2,1:T(8,128)}, u32[]{:S(2)}, u32[]{:S(2)}) async-start(f32[2,128,1,128,128]{4,3,0,2,1:T(8,128)} %maximum_bitcast_fusion), calls=%async_computation | async-start | bytes 33554432 | tf_op jit(solution)/shard_map/all_to_all | solution.py:39
  289.5 83.7 %collective-permute-start = (f32[56,128,128]{2,1,0:T(8,128)}, f32[56,128,128]{2,1,0:T(8,128)}, u32[]{:S(2)}, u32[]{:S(2)}) collective-permute-start(f32[56,128,128]{2,1,0:T(8,128)} %broadcast_select_fusion.1), channel_id=1, source_target_pairs={{0,7},{1,0},{2,1},{3,2},{4,3},{5,4},{6,5},{7,6},{8,15},{9,8},{10,9... | collective-permute-start | bytes 11010056 | tf_op jit(solution)/shard_map/ppermute | solution.py:11
  300.4 315.5 %copy-start.3 = (s32[4,64]{1,0:T(4,128)S(1)}, s32[4,64]{1,0:T(4,128)}, u32[]{:S(2)}) copy-start(s32[4,64]{1,0:T(4,128)} %param.22) | copy-start | bytes 3076
  300.4 315.5 %copy-start.4 = (s32[4,64]{1,0:T(4,128)S(1)}, s32[4,64]{1,0:T(4,128)}, u32[]{:S(2)}) copy-start(s32[4,64]{1,0:T(4,128)} %param.21) | copy-start | bytes 3076
  300.4 315.6 %copy-start.2 = (s32[4,64]{1,0:T(4,128)S(1)}, s32[4,64]{1,0:T(4,128)}, u32[]{:S(2)}) copy-start(s32[4,64]{1,0:T(4,128)} %param.23) | copy-start | bytes 3076
  302.8 1.8 copy-start
  304.6 179.2 %collective-permute-start.1 = (f32[56,128,128]{2,1,0:T(8,128)S(1)}, f32[56,128,128]{2,1,0:T(8,128)S(1)}, u32[]{:S(2)}, u32[]{:S(2)}) collective-permute-start(f32[56,128,128]{2,1,0:T(8,128)S(1)} %broadcast_select_fusion), channel_id=1, source_target_pairs={{0,120},{8,0},{16,8},{24,16},{32,24},{40,32},{48,40},{56,48},{64,5... | collective-permute-start | bytes 11010056 | tf_op jit(solution)/shard_map/ppermute | solution.py:11
  373.2 118.1 %collective-permute-start.2 = (f32[56,128,128]{2,1,0:T(8,128)}, f32[56,128,128]{2,1,0:T(8,128)}, u32[]{:S(2)}, u32[]{:S(2)}) collective-permute-start(f32[56,128,128]{2,1,0:T(8,128)} %collective-permute-done), channel_id=1, source_target_pairs={{0,7},{1,0},{2,1},{3,2},{4,3},{5,4},{6,5},{7,6},{8,15},{9,8},{10,9... | collective-permute-start | bytes 11010056 | tf_op jit(solution)/shard_map/ppermute | solution.py:11
  483.8 1.9 copy-start.1
  485.7 124.6 %collective-permute-start.3 = (f32[56,128,128]{2,1,0:T(8,128)S(1)}, f32[56,128,128]{2,1,0:T(8,128)}, u32[]{:S(2)}, u32[]{:S(2)}) collective-permute-start(f32[56,128,128]{2,1,0:T(8,128)S(1)} %collective-permute-done.1), channel_id=1, source_target_pairs={{0,120},{8,0},{16,8},{24,16},{32,24},{40,32},{48,40},{56,48},{64,5... | collective-permute-start | bytes 11010056 | tf_op jit(solution)/shard_map/ppermute | solution.py:11
  491.2 236.6 %collective-permute-start.4 = (f32[56,128,128]{2,1,0:T(8,128)}, f32[56,128,128]{2,1,0:T(8,128)}, u32[]{:S(2)}, u32[]{:S(2)}) collective-permute-start(f32[56,128,128]{2,1,0:T(8,128)} %collective-permute-done.2), channel_id=1, source_target_pairs={{0,7},{1,0},{2,1},{3,2},{4,3},{5,4},{6,5},{7,6},{8,15},{9,8},{10,9... | collective-permute-start | bytes 11010056 | tf_op jit(solution)/shard_map/ppermute | solution.py:11
  610.3 122.4 %collective-permute-start.5 = (f32[56,128,128]{2,1,0:T(8,128)}, f32[56,128,128]{2,1,0:T(8,128)}, u32[]{:S(2)}, u32[]{:S(2)}) collective-permute-start(f32[56,128,128]{2,1,0:T(8,128)} %collective-permute-done.3), channel_id=1, source_target_pairs={{0,120},{8,0},{16,8},{24,16},{32,24},{40,32},{48,40},{56,48},{64,5... | collective-permute-start | bytes 11010056 | tf_op jit(solution)/shard_map/ppermute | solution.py:11
where the time goes:
time: 771 us; the launch traced here: 770 us
  waiting for transfers between devices  519 us (67%)
  other arithmetic  89.3 us (12%)
  local copies, waits for them, and re-layouts  85.2 us (11%)
  matrix products  40.3 us (5%)
  starting transfers between devices  35.5 us (5%)
    ppermute x6, waiting for transfers between devices, from_behind(): lax.ppermute(array, axis, [(i, (i + by) % peers) for i in range(peers)])  290 us
    all_to_all x1, waiting for transfers between devices, local(): lax.all_to_all(outgoing.reshape(2, devices, capacity, width, width), ('ro...  229 us
    scatter-add x4, other arithmetic, stack_product(): return jax.ops.segment_sum(products, index_c, num_segments=CBLK)  54.3 us
    dot_general x4, matrix products, stack_product(): jnp.einsum('pij,pjk->pik', left, right, precision=lax.Precision.HIGHEST,...  40.3 us
    ppermute x6, starting transfers between devices, from_behind(): lax.ppermute(array, axis, [(i, (i + by) % peers) for i in range(peers)])  23.9 us
    gather x4, local copies, waits for them, and re-layouts, stack_product(): right = jnp.take(panel_b, index_b, axis=0)  19.3 us
    gather x4, local copies, waits for them, and re-layouts, stack_product(): left = jnp.take(panel_a, index_a, axis=0)  19.2 us
  transfers between devices with their start and end apart: 7, of which 4 were waited for; matrix products, arithmetic and copies ran while one was open for 16% of the time, Pallas kernels for 0%

commit v1 on v0

v1 whole, which is shorter than its diff:
```python
import functools

import jax
import jax.numpy as jnp
from jax import lax
from jax.experimental import pallas as pl
from jax.experimental.pallas import tpu as pltpu
from jax.sharding import PartitionSpec as P

CBLK = 64
CHUNKS = 4
VMEM_LIMIT = 28 * 1024 * 1024

ANY = pl.BlockSpec(memory_space=pl.ANY)
SMEM = pl.BlockSpec(memory_space=pltpu.SMEM)


def permute(array, mapping):
    rows, cols = lax.axis_size("row"), lax.axis_size("col")
    pairs = []
    for r in range(rows):
        for c in range(cols):
            source = mapping(r, c)
            if source is not None:
                pairs.append(((source[0] % rows) * cols + source[1] % cols, r * cols + c))
    return lax.ppermute(array, ("row", "col"), pairs)


def fill_kernel(a_pick, b_pick, a_blocks, b_blocks, out, sem):
    panel = a_blocks.shape[0]
    slots = a_pick.shape[0]

    def body(q, carry):
        pa = a_pick[q]
        pb = b_pick[q]

        @pl.when(pa < panel)
        def _():
            pltpu.make_async_copy(a_blocks.at[pa], out.at[q, 0], sem.at[0]).start()

        @pl.when(pb < panel)
        def _():
            pltpu.make_async_copy(b_blocks.at[pb], out.at[q, 1], sem.at[1]).start()

        return carry

    lax.fori_loop(0, slots, body, 0)
    pltpu.make_async_copy(a_blocks, a_blocks, sem.at[0]).wait()
    pltpu.make_async_copy(b_blocks, b_blocks, sem.at[1]).wait()


def fill(a_pick, b_pick, a_blocks, b_blocks):
    slots = a_pick.shape[0]
    width = a_blocks.shape[1]
    nbytes = 4 * a_blocks.size * 4
    return pl.pallas_call(
        fill_kernel,
        out_shape=jax.ShapeDtypeStruct((slots, 2, width, width), jnp.float32),
        in_specs=[SMEM, SMEM, ANY, ANY],
        out_specs=ANY,
        scratch_shapes=[pltpu.SemaphoreType.DMA((2,))],
        cost_estimate=pl.CostEstimate(flops=0, bytes_accessed=nbytes, transcendentals=0),
        name="fill",
    )(a_pick, b_pick, a_blocks, b_blocks)


def compact_kernel(chunks, a_place, b_place, arrived, *refs):
    a_out = refs[:chunks]
    b_out = refs[chunks]
    sem = refs[chunks + 1]
    part = a_out[0].shape[0]
    for i in range(chunks):

        def body(j, carry, i=i):
            pltpu.make_async_copy(arrived.at[a_place[i * part + j], 0], a_out[i].at[j], sem.at[i]).start()
            return carry

        lax.fori_loop(0, part, body, 0)

    def body_b(j, carry):
        pltpu.make_async_copy(arrived.at[b_place[j], 1], b_out.at[j], sem.at[chunks]).start()
        return carry

    lax.fori_loop(0, b_out.shape[0], body_b, 0)
    for i in range(chunks):
        pltpu.make_async_copy(a_out[i], a_out[i], sem.at[i]).wait()
    pltpu.make_async_copy(b_out, b_out, sem.at[chunks]).wait()


def compact(a_place, b_place, arrived):
    panel = a_place.shape[0]
    width = arrived.shape[-1]
    shapes = [jax.ShapeDtypeStruct((panel // CHUNKS, width, width), jnp.float32)] * CHUNKS
    shapes.append(jax.ShapeDtypeStruct((panel, width, width), jnp.float32))
    outs = pl.pallas_call(
        functools.partial(compact_kernel, CHUNKS),
        out_shape=shapes,
        in_specs=[SMEM, SMEM, ANY],
        out_specs=[ANY] * (CHUNKS + 1),
        scratch_shapes=[pltpu.SemaphoreType.DMA((CHUNKS + 1,))],
        cost_estimate=pl.CostEstimate(flops=0, bytes_accessed=4 * panel * width * width * 4, transcendentals=0),
        name="compact",
    )(a_place, b_place, arrived)
    return list(outs[:CHUNKS]), outs[CHUNKS]


def split(value):
    high = value.astype(jnp.bfloat16)
    low = (value - high.astype(jnp.float32)).astype(jnp.bfloat16)
    return high, low


def block_product(left, right):
    lh, ll = split(left)
    rh, rl = split(right)
    both = jnp.dot(
        jnp.concatenate([lh, ll], axis=1),
        jnp.concatenate([rh, rh], axis=0),
        preferred_element_type=jnp.float32,
    )
    return both + jnp.dot(lh, rl, preferred_element_type=jnp.float32)


def step_kernel(chunks, has_c, n_b, core, index_a, index_b, index_c, *refs):
    a_parts = refs[:chunks]
    b_options = refs[chunks : chunks + n_b]
    refs = refs[chunks + n_b :]
    if has_c:
        c_in, refs = refs[0], refs[1:]
    c_out, a_ref, b_ref, c_ref, sem = refs
    part = a_parts[0].shape[0]
    blocks = c_out.shape[0]

    a_copies = [
        pltpu.make_async_copy(a_parts[i], a_ref.at[pl.ds(i * part, part)], sem.at[i]) for i in range(chunks)
    ]
    for copy in a_copies:
        copy.start()
    if n_b == 1:
        pltpu.make_async_copy(b_options[0], b_ref, sem.at[chunks]).start()
    else:
        for k in range(n_b):

            @pl.when(core[0] == k)
            def _(k=k):
                pltpu.make_async_copy(b_options[k], b_ref, sem.at[chunks]).start()

    if has_c:
        pltpu.make_async_copy(c_in, c_ref.at[pl.ds(0, blocks)], sem.at[chunks + 1]).start()
    else:
        c_ref[...] = jnp.zeros_like(c_ref)
    for copy in a_copies:
        copy.wait()
    pltpu.make_async_copy(b_options[0], b_ref, sem.at[chunks]).wait()
    if has_c:
        pltpu.make_async_copy(c_in, c_ref.at[pl.ds(0, blocks)], sem.at[chunks + 1]).wait()

    def body(e, carry):
        m = index_c[e]

        @pl.when(m < blocks)
        def _():
            c_ref[m] += block_product(a_ref[index_a[e]], b_ref[index_b[e]])

        return carry

    lax.fori_loop(0, index_a.shape[0], body, 0)
    out = pltpu.make_async_copy(c_ref.at[pl.ds(0, blocks)], c_out, sem.at[chunks + 1])
    out.start()
    out.wait()


def step_product(core, index_a, index_b, index_c, a_parts, b_options, total):
    chunks, n_b = len(a_parts), len(b_options)
    part, width, _ = a_parts[0].shape
    panel = b_options[0].shape[0]
    has_c = total is not None
    operands = [core, index_a, index_b, index_c, *a_parts, *b_options]
    in_specs = [SMEM] * 4 + [ANY] * (chunks + n_b)
    aliases = {}
    if has_c:
        aliases = {len(operands): 0}
        operands.append(total)
        in_specs.append(ANY)
    entries = index_a.shape[0]
    return pl.pallas_call(
        functools.partial(step_kernel, chunks, has_c, n_b),
        out_shape=jax.ShapeDtypeStruct((CBLK, width, width), jnp.float32),
        in_specs=in_specs,
        out_specs=ANY,
        scratch_shapes=[
            pltpu.VMEM((panel, width, width), jnp.float32),
            pltpu.VMEM((panel, width, width), jnp.float32),
            pltpu.VMEM((CBLK, width, width), jnp.float32),
            pltpu.SemaphoreType.DMA((chunks + 2,)),
        ],
        input_output_aliases=aliases,
        compiler_params=pltpu.CompilerParams(vmem_limit_bytes=VMEM_LIMIT),
        cost_estimate=pl.CostEstimate(
            flops=6 * entries * width**3, bytes_accessed=4 * 4 * panel * width * width, transcendentals=0
        ),
        name="step",
    )(*operands)


def local(a_blocks, a_pick, a_place, b_blocks, b_pick, b_place, prod_a, prod_b, prod_c):
    core = (lax.axis_index("row") % 2).astype(jnp.int32).reshape(1)
    odd = lax.axis_index("col") % 2 == 1

    outgoing = fill(a_pick, b_pick, a_blocks, b_blocks)
    arrived = lax.all_to_all(outgoing, ("row", "col"), split_axis=0, concat_axis=0, tiled=True)
    a0, b0 = compact(a_place, b_place, arrived)

    a2 = [permute(part, lambda r, c: (r, c + 2)) for part in a0]
    b1 = permute(b0, lambda r, c: (r + 1, c))
    b2_far = permute(b0, lambda r, c: (r + 2, c) if r % 2 else None)
    b3_far = permute(b0, lambda r, c: (r + 3, c) if r % 2 else None)
    a1 = [
        permute(jnp.where(odd, own, far), lambda r, c: (r, c ^ 1)) for own, far in zip(a0, a2)
    ]
    a3 = [permute(part, lambda r, c: (r, c + 2)) for part in a1]
    b2_near = permute(b1, lambda r, c: None if r % 2 else (r + 1, c))
    b3_near = permute(b2_far, lambda r, c: None if r % 2 else (r + 1, c))

    total = step_product(core, prod_a[0], prod_b[0], prod_c[0], a0, [b0], None)
    total = step_product(core, prod_a[2], prod_b[2], prod_c[2], a2, [b2_near, b2_far], total)
    total = step_product(core, prod_a[1], prod_b[1], prod_c[1], a1, [b1], total)
    total = step_product(core, prod_a[3], prod_b[3], prod_c[3], a3, [b3_near, b3_far], total)
    return total


def solution(mesh):
    placed = (
        P(("row", "col"), None, None),
        P(("row", "col")),
        P(("row", "col")),
        P(("row", "col"), None, None),
        P(("row", "col")),
        P(("row", "col")),
        P(None, ("row", "col")),
        P(None, ("row", "col")),
        P(None, ("row", "col")),
    )
    return jax.shard_map(
        local, mesh=mesh, in_specs=placed, out_specs=P(("row", "col"), None, None), check_vma=False
    )
```

time: 771 us -> 912 us (1.18)
  Pallas kernels: 0 us -> 505 us
  waiting for transfers between devices: 519 us -> 157 us
  blocking collectives: 0 us -> 199 us
  other arithmetic: 89.3 us -> 2.79 us
  local copies, waits for them, and re-layouts: 85.2 us -> 6.1 us
  matrix products: 40.3 us -> 0 us
    pallas_call x0 -> x6, Pallas kernels: none -> 505 us  [the longest x1 224 us: compact(): pl.pallas_call(functools.partial(compact_kernel, CHUNKS), out_shape=shape...]
    all_to_all x1 -> x0, waiting for transfers between devices: 229 us -> none  [local(): lax.all_to_all(outgoing.reshape(2, devices, capacity, width, width), ('ro...]
    all_to_all x0 -> x1, blocking collectives: none -> 199 us  [local(): lax.all_to_all(outgoing, ('row', 'col'), split_axis=0, concat_axis=0, til...]
    ppermute x6 -> x17, waiting for transfers between devices: 290 us -> 157 us  [permute(): return lax.ppermute(array, ('row', 'col'), pairs)]
    gather x12 -> x0, local copies, waits for them, and re-layouts: 63.2 us -> none  [the longest x4 19.3 us: stack_product(): right = jnp.take(panel_b, index_b, axis=0)]
    scatter-add x4 -> x0, other arithmetic: 54.3 us -> none  [stack_product(): return jax.ops.segment_sum(products, index_c, num_segments=CBLK)]
    dot_general x4 -> x0, matrix products: 40.3 us -> none  [stack_product(): jnp.einsum('pij,pjk->pik', left, right, precision=lax.Precision.HIGHEST,...]
    ppermute x6 -> x17, starting transfers between devices: 23.9 us -> 40.2 us  [permute(): return lax.ppermute(array, ('row', 'col'), pairs)]
  transfers between devices with their start and end apart: 7 -> 17, of which waited for: 4 -> 8; matrix products, arithmetic and copies ran while one was open for 16% -> 0% of each run, Pallas kernels for 0% -> 4%
where the time goes in v1:
time: 912 us; the launch traced here: 910 us
  Pallas kernels  505 us (55%)
  blocking collectives  199 us (22%)
  waiting for transfers between devices  157 us (17%)
  starting transfers between devices  40.2 us (4%)
    pallas_call x1, Pallas kernels, compact(): pl.pallas_call(functools.partial(compact_kernel, CHUNKS), out_shape=shape...  224 us
    pallas_call x1, Pallas kernels, fill(): pl.pallas_call(fill_kernel, out_shape=jax.ShapeDtypeStruct((slots, 2, wid...  224 us
    all_to_all x1, blocking collectives, local(): lax.all_to_all(outgoing, ('row', 'col'), split_axis=0, concat_axis=0, til...  199 us
    ppermute x17, waiting for transfers between devices, permute(): return lax.ppermute(array, ('row', 'col'), pairs)  157 us
    pallas_call x4, Pallas kernels, step_product(): pl.pallas_call(functools.partial(step_kernel, chunks, has_c, n_b), out_sh...  56.9 us
    ppermute x17, starting transfers between devices, permute(): return lax.ppermute(array, ('row', 'col'), pairs)  40.2 us
  transfers between devices with their start and end apart: 17, of which 8 were waited for; matrix products, arithmetic and copies ran while one was open for 0% of the time, Pallas kernels for 4%

profile of v1, /device:TPU:0, one launch (start us, length us, event | category | flops | bytes accessed | tf_op | source)
XLA Modules:
  0.0 910.5 jit_solution(9306601714366837175)
XLA Ops:
  0.0 224.1 %fill.1 = f32[128,2,128,128]{3,2,1,0:T(8,128)} custom-call(s32[128]{0:T(128)} %a_pick.1, s32[128]{0:T(128)} %b_pick.1, f32[56,128,128]{2,1,0:T(8,128)} %a_blocks.1, f32[56,128,128]{2,1,0:T(8,128)} %b_blocks.1), custom_call_target="tpu_custom_call" | custom-call | bytes 14680064 | tf_op jit(solution)/shard_map/fill/pallas_call | solution.py:56
  224.2 198.9 %all_to_all.5.arrived = f32[128,2,128,128]{3,2,1,0:T(8,128)} all-to-all(f32[128,2,128,128]{3,2,1,0:T(8,128)} %fill.1), channel_id=1, replica_groups=mesh['row'=16,'col'=8] {'row','col'}, dimensions={0} | all-to-all | bytes 33554432 | tf_op jit(solution)/shard_map/all_to_all | solution.py:211
  423.1 224.2 %compact.1 = (f32[14,128,128]{2,1,0:T(8,128)}, f32[14,128,128]{2,1,0:T(8,128)}, f32[14,128,128]{2,1,0:T(8,128)}, f32[14,128,128]{2,1,0:T(8,128)}, f32[56,128,128]{2,1,0:T(8,128)}) custom-call(s32[56]{0:T(128)} %a_place.1, s32[56]{0:T(128)} %b_place.1, f32[128,2,128,128]{3,2,1,0:T(8,128)} %all_to_all.5.arrived), custom_call_target="tpu_custom_call" | custom-call | bytes 14680064 | tf_op jit(solution)/shard_map/compact/pallas_call | solution.py:95
  647.3 0.5 collective-permute-start.15
  647.7 2.4 collective-permute-start.12
  650.2 1.6 collective-permute-start.9
  651.7 0.6 collective-permute-start.3
  652.3 73.8 %collective-permute-done.15.refs_4_ = f32[56,128,128]{2,1,0:T(8,128)} collective-permute-done((f32[56,128,128]{2,1,0:T(8,128)}, f32[56,128,128]{2,1,0:T(8,128)}, u32[]{:S(2)}, u32[]{:S(2)}) %collective-permute-start.15) | collective-permute-done | bytes 3670048 | tf_op jit(solution)/shard_map/ppermute | solution.py:26
  726.1 1.3 collective-permute-start.16
  727.4 1.2 collective-permute-start.6
  728.6 0.0 collective-permute-done.9.refs_3_
  728.6 0.1 collective-permute-start
  728.8 0.1 broadcast_select_fusion
  728.9 0.9 copy-done.5
  729.8 0.0 collective-permute-done.3.refs_1_
  729.8 2.4 collective-permute-start.10
  732.3 15.9 %collective-permute-done.6.refs_2_ = f32[14,128,128]{2,1,0:T(8,128)} collective-permute-done((f32[14,128,128]{2,1,0:T(8,128)}, f32[14,128,128]{2,1,0:T(8,128)}, u32[]{:S(2)}, u32[]{:S(2)}) %collective-permute-start.6) | collective-permute-done | bytes 917536 | tf_op jit(solution)/shard_map/ppermute | solution.py:26
  748.1 10.9 %collective-permute-start.14 = (f32[56,128,128]{2,1,0:T(8,128)}, f32[56,128,128]{2,1,0:T(8,128)}, u32[]{:S(2)}, u32[]{:S(2)}) collective-permute-start(f32[56,128,128]{2,1,0:T(8,128)} %get-tuple-element.14.refs_4_), channel_id=1, source_target_pairs={{32,8},{33,9},{34,10},{35,11},{36,12},{37,13},{38,14},{39,15},{48,... | collective-permute-start | bytes 11010056 | tf_op jit(solution)/shard_map/ppermute | solution.py:26
  759.0 1.3 collective-permute-start.13
  760.3 1.3 broadcast_select_fusion.1
  761.6 1.3 broadcast_select_fusion.2
  762.9 4.8 collective-permute-done.refs_0_
  767.7 0.8 collective-permute-start.7
  768.5 0.0 collective-permute-done.10.refs_3_
  768.5 1.2 collective-permute-start.4
  769.7 0.1 broadcast_select_fusion.3
  769.8 1.0 copy-done.7
  770.8 17.3 %collective-permute-done.7.refs_2_ = f32[14,128,128]{2,1,0:T(8,128)} collective-permute-done((f32[14,128,128]{2,1,0:T(8,128)S(1)}, f32[14,128,128]{2,1,0:T(8,128)}, u32[]{:S(2)}, u32[]{:S(2)}) %collective-permute-start.7) | collective-permute-done | bytes 917536 | tf_op jit(solution)/shard_map/ppermute | solution.py:26
  788.1 1.3 collective-permute-start.1
  789.4 18.3 %collective-permute-done.4.refs_1_ = f32[14,128,128]{2,1,0:T(8,128)} collective-permute-done((f32[14,128,128]{2,1,0:T(8,128)S(1)}, f32[14,128,128]{2,1,0:T(8,128)}, u32[]{:S(2)}, u32[]{:S(2)}) %collective-permute-start.4) | collective-permute-done | bytes 917536 | tf_op jit(solution)/shard_map/ppermute | solution.py:26
  807.7 5.4 collective-permute-start.11
  813.2 14.2 %collective-permute-done.1.refs_0_ = f32[14,128,128]{2,1,0:T(8,128)} collective-permute-done((f32[14,128,128]{2,1,0:T(8,128)S(1)}, f32[14,128,128]{2,1,0:T(8,128)}, u32[]{:S(2)}, u32[]{:S(2)}) %collective-permute-start.1) | collective-permute-done | bytes 917536 | tf_op jit(solution)/shard_map/ppermute | solution.py:26
  827.4 5.4 collective-permute-start.8
  832.8 0.4 collective-permute-done.11.refs_3_
  833.2 0.9 copy-done.11
  834.2 3.7 collective-permute-start.5
  837.8 0.0 collective-permute-done.16.refs_4_
  837.9 0.0 collective-permute-start.2
  837.9 1.2 copy-done.3
  839.1 2.0 copy-done.4
  841.2 9.9 %step.4.refs_6_ = f32[64,128,128]{2,1,0:T(8,128)} custom-call(s32[1]{0:T(128)} %bitcast.core, s32[64]{0:T(128)S(1)} %get-tuple-element.23.index_a, s32[64]{0:T(128)S(1)} %get-tuple-element.30.index_b, s32[64]{0:T(128)S(1)} %get-tuple-element.15.index_c, f32[14,128,128]{2,1,0:T(8,128)S(1)} %copy-done, f32[14,128,128]{2,1,0:T(8,128)S(1)} %copy-done.1, ...), custom_call_target="tpu_custom_call" | custom-call | flops 805306368 | bytes 14680064 | tf_op jit(solution)/shard_map/step/pallas_call | solution.py:186
  851.1 16.9 %step.5.refs_5_ = f32[64,128,128]{2,1,0:T(8,128)} custom-call(s32[1]{0:T(128)} %bitcast.core, s32[64]{0:T(128)S(1)} %get-tuple-element.26.index_a, s32[64]{0:T(128)S(1)} %get-tuple-element.27.index_b, s32[64]{0:T(128)S(1)} %get-tuple-element.18.index_c, f32[14,128,128]{2,1,0:T(8,128)S(1)} %copy-done.8, ...), custom_call_target="tpu_custom_call", output_to_operand_aliasing={{}: (10, {})} | custom-call | flops 805306368 | bytes 14680064 | tf_op jit(solution)/shard_map/step/pallas_call | solution.py:186
  868.0 12.7 %step.6.refs_6_ = f32[64,128,128]{2,1,0:T(8,128)} custom-call(s32[1]{0:T(128)} %bitcast.core, s32[64]{0:T(128)S(1)} %get-tuple-element.24.index_a, s32[64]{0:T(128)S(1)} %get-tuple-element.29.index_b, s32[64]{0:T(128)S(1)} %get-tuple-element.16.index_c, f32[14,128,128]{2,1,0:T(8,128)} %collective-permute-done.1.refs_0_, ...), custom_call_target="tpu_custom_call", output_to_operand_aliasing={{}: (9, {})} | custom-call | flops 805306368 | bytes 14680064 | tf_op jit(solution)/shard_map/step/pallas_call | solution.py:186
  880.7 0.0 collective-permute-done.8.refs_2_
  880.7 0.0 collective-permute-done.5.refs_1_
  880.7 12.3 %collective-permute-done.2.refs_0_ = f32[14,128,128]{2,1,0:T(8,128)} collective-permute-done((f32[14,128,128]{2,1,0:T(8,128)}, f32[14,128,128]{2,1,0:T(8,128)}, u32[]{:S(2)}, u32[]{:S(2)}) %collective-permute-start.2) | collective-permute-done | bytes 917536 | tf_op jit(solution)/shard_map/ppermute | solution.py:26
  893.1 0.0 collective-permute-done.13.refs_4_
  893.1 17.4 %step.7 = f32[64,128,128]{2,1,0:T(8,128)} custom-call(s32[1]{0:T(128)} %bitcast.core, s32[64]{0:T(128)S(1)} %get-tuple-element.25.index_a, s32[64]{0:T(128)S(1)} %get-tuple-element.28.index_b, s32[64]{0:T(128)S(1)} %get-tuple-element.17.index_c, f32[14,128,128]{2,1,0:T(8,128)} %collective-permute-done.2.refs_0_, ...), custom_call_target="tpu_custom_call", output_to_operand_aliasing={{}: (10, {})} | custom-call | flops 805306368 | bytes 14680064 | tf_op jit(solution)/shard_map/step/pallas_call | solution.py:186
  (31 shorter events, 0.1 us)
Async XLA Ops:
  647.2 114.4 %copy-start.1 = (f32[14,128,128]{2,1,0:T(8,128)S(1)}, f32[14,128,128]{2,1,0:T(8,128)}, u32[]{:S(2)}) copy-start(f32[14,128,128]{2,1,0:T(8,128)} %get-tuple-element.11.refs_1_) | copy-start | bytes 2752516
  647.3 78.9 %collective-permute-start.15 = (f32[56,128,128]{2,1,0:T(8,128)}, f32[56,128,128]{2,1,0:T(8,128)}, u32[]{:S(2)}, u32[]{:S(2)}) collective-permute-start(f32[56,128,128]{2,1,0:T(8,128)} %get-tuple-element.14.refs_4_), channel_id=1, source_target_pairs={{8,0},{9,1},{10,2},{11,3},{12,4},{13,5},{14,6},{15,7},{16,8},{17,9... | collective-permute-start | bytes 11010056 | tf_op jit(solution)/shard_map/ppermute | solution.py:26
  647.7 111.3 %collective-permute-start.12 = (f32[56,128,128]{2,1,0:T(8,128)}, f32[56,128,128]{2,1,0:T(8,128)}, u32[]{:S(2)}, u32[]{:S(2)}) collective-permute-start(f32[56,128,128]{2,1,0:T(8,128)} %get-tuple-element.14.refs_4_), channel_id=1, source_target_pairs={{24,8},{25,9},{26,10},{27,11},{28,12},{29,13},{30,14},{31,15},{40,... | collective-permute-start | bytes 11010056 | tf_op jit(solution)/shard_map/ppermute | solution.py:26
  650.2 78.5 %collective-permute-start.9 = (f32[14,128,128]{2,1,0:T(8,128)}, f32[14,128,128]{2,1,0:T(8,128)S(1)}, u32[]{:S(2)}, u32[]{:S(2)}) collective-permute-start(f32[14,128,128]{2,1,0:T(8,128)} %get-tuple-element.13.refs_3_), channel_id=1, source_target_pairs={{2,0},{3,1},{4,2},{5,3},{6,4},{7,5},{0,6},{1,7},{10,8},{11,9},{12,... | collective-permute-start | bytes 2752520 | tf_op jit(solution)/shard_map/ppermute | solution.py:26
  651.7 78.1 %collective-permute-start.3 = (f32[14,128,128]{2,1,0:T(8,128)}, f32[14,128,128]{2,1,0:T(8,128)}, u32[]{:S(2)}, u32[]{:S(2)}) collective-permute-start(f32[14,128,128]{2,1,0:T(8,128)} %get-tuple-element.11.refs_1_), channel_id=1, source_target_pairs={{2,0},{3,1},{4,2},{5,3},{6,4},{7,5},{0,6},{1,7},{10,8},{11,9},{12,... | collective-permute-start | bytes 2752520 | tf_op jit(solution)/shard_map/ppermute | solution.py:26
  726.1 111.7 %collective-permute-start.16 = (f32[56,128,128]{2,1,0:T(8,128)}, f32[56,128,128]{2,1,0:T(8,128)}, u32[]{:S(2)}, u32[]{:S(2)}) collective-permute-start(f32[56,128,128]{2,1,0:T(8,128)} %collective-permute-done.15.refs_4_), channel_id=1, source_target_pairs={{8,0},{9,1},{10,2},{11,3},{12,4},{13,5},{14,6},{15,7},{24,16},{25,... | collective-permute-start | bytes 11010056 | tf_op jit(solution)/shard_map/ppermute | solution.py:26
  727.4 20.7 %collective-permute-start.6 = (f32[14,128,128]{2,1,0:T(8,128)}, f32[14,128,128]{2,1,0:T(8,128)}, u32[]{:S(2)}, u32[]{:S(2)}) collective-permute-start(f32[14,128,128]{2,1,0:T(8,128)} %get-tuple-element.12.refs_2_), channel_id=1, source_target_pairs={{2,0},{3,1},{4,2},{5,3},{6,4},{7,5},{0,6},{1,7},{10,8},{11,9},{12,... | collective-permute-start | bytes 2752520 | tf_op jit(solution)/shard_map/ppermute | solution.py:26
  728.6 41.1 %copy-start = (f32[14,128,128]{2,1,0:T(8,128)S(1)}, f32[14,128,128]{2,1,0:T(8,128)}, u32[]{:S(2)}) copy-start(f32[14,128,128]{2,1,0:T(8,128)} %get-tuple-element.10.refs_0_) | copy-start | bytes 2752516
  728.6 39.0 %collective-permute-start = (f32[14,128,128]{2,1,0:T(8,128)}, f32[14,128,128]{2,1,0:T(8,128)S(1)}, u32[]{:S(2)}, u32[]{:S(2)}) collective-permute-start(f32[14,128,128]{2,1,0:T(8,128)} %get-tuple-element.10.refs_0_), channel_id=1, source_target_pairs={{2,0},{3,1},{4,2},{5,3},{6,4},{7,5},{0,6},{1,7},{10,8},{11,9},{12,... | collective-permute-start | bytes 2752520 | tf_op jit(solution)/shard_map/ppermute | solution.py:26
  728.9 1.0 copy-start.5
  729.8 108.1 %copy-start.13 = (s32[4,64]{1,0:T(4,128)S(1)}, s32[4,64]{1,0:T(4,128)}, u32[]{:S(2)}) copy-start(s32[4,64]{1,0:T(4,128)} %param.15) | copy-start | bytes 3076
  729.8 108.1 %copy-start.14 = (s32[4,64]{1,0:T(4,128)S(1)}, s32[4,64]{1,0:T(4,128)}, u32[]{:S(2)}) copy-start(s32[4,64]{1,0:T(4,128)} %param.17) | copy-start | bytes 3076
  729.8 108.1 %copy-start.15 = (s32[4,64]{1,0:T(4,128)S(1)}, s32[4,64]{1,0:T(4,128)}, u32[]{:S(2)}) copy-start(s32[4,64]{1,0:T(4,128)} %param.16) | copy-start | bytes 3076
  729.8 108.1 %copy-start.2 = (f32[14,128,128]{2,1,0:T(8,128)S(1)}, f32[14,128,128]{2,1,0:T(8,128)}, u32[]{:S(2)}) copy-start(f32[14,128,128]{2,1,0:T(8,128)} %get-tuple-element.12.refs_2_) | copy-start | bytes 2752516
  729.8 38.7 %collective-permute-start.10 = (f32[14,128,128]{2,1,0:T(8,128)S(1)}, f32[14,128,128]{2,1,0:T(8,128)S(1)}, u32[]{:S(2)}, u32[]{:S(2)}) collective-permute-start(f32[14,128,128]{2,1,0:T(8,128)S(1)} %broadcast_select_fusion), channel_id=1, source_target_pairs={{1,0},{0,1},{3,2},{2,3},{5,4},{4,5},{7,6},{6,7},{9,8},{8,9},{11,10... | collective-permute-start | bytes 2752520 | tf_op jit(solution)/shard_map/ppermute | solution.py:26
  748.1 144.9 %collective-permute-start.14 = (f32[56,128,128]{2,1,0:T(8,128)}, f32[56,128,128]{2,1,0:T(8,128)}, u32[]{:S(2)}, u32[]{:S(2)}) collective-permute-start(f32[56,128,128]{2,1,0:T(8,128)} %get-tuple-element.14.refs_4_), channel_id=1, source_target_pairs={{32,8},{33,9},{34,10},{35,11},{36,12},{37,13},{38,14},{39,15},{48,... | collective-permute-start | bytes 11010056 | tf_op jit(solution)/shard_map/ppermute | solution.py:26
  759.0 134.0 %collective-permute-start.13 = (f32[56,128,128]{2,1,0:T(8,128)}, f32[56,128,128]{2,1,0:T(8,128)}, u32[]{:S(2)}, u32[]{:S(2)}) collective-permute-start(f32[56,128,128]{2,1,0:T(8,128)} %collective-permute-done.12.refs_5_), channel_id=1, source_target_pairs={{8,0},{9,1},{10,2},{11,3},{12,4},{13,5},{14,6},{15,7},{24,16},{25,... | collective-permute-start | bytes 11010056 | tf_op jit(solution)/shard_map/ppermute | solution.py:26
  767.7 20.4 %collective-permute-start.7 = (f32[14,128,128]{2,1,0:T(8,128)S(1)}, f32[14,128,128]{2,1,0:T(8,128)}, u32[]{:S(2)}, u32[]{:S(2)}) collective-permute-start(f32[14,128,128]{2,1,0:T(8,128)S(1)} %broadcast_select_fusion.1), channel_id=1, source_target_pairs={{1,0},{0,1},{3,2},{2,3},{5,4},{4,5},{7,6},{6,7},{9,8},{8,9},{11,10... | collective-permute-start | bytes 2752520 | tf_op jit(solution)/shard_map/ppermute | solution.py:26
  768.5 39.3 %copy-start.9 = (f32[14,128,128]{2,1,0:T(8,128)}, f32[14,128,128]{2,1,0:T(8,128)S(1)}, u32[]{:S(2)}) copy-start(f32[14,128,128]{2,1,0:T(8,128)S(1)} %collective-permute-done.10.refs_3_) | copy-start | bytes 2752516
  768.5 39.3 %collective-permute-start.4 = (f32[14,128,128]{2,1,0:T(8,128)S(1)}, f32[14,128,128]{2,1,0:T(8,128)}, u32[]{:S(2)}, u32[]{:S(2)}) collective-permute-start(f32[14,128,128]{2,1,0:T(8,128)S(1)} %broadcast_select_fusion.2), channel_id=1, source_target_pairs={{1,0},{0,1},{3,2},{2,3},{5,4},{4,5},{7,6},{6,7},{9,8},{8,9},{11,10... | collective-permute-start | bytes 2752520 | tf_op jit(solution)/shard_map/ppermute | solution.py:26
  769.8 1.0 copy-start.7
  788.1 39.3 %collective-permute-start.1 = (f32[14,128,128]{2,1,0:T(8,128)S(1)}, f32[14,128,128]{2,1,0:T(8,128)}, u32[]{:S(2)}, u32[]{:S(2)}) collective-permute-start(f32[14,128,128]{2,1,0:T(8,128)S(1)} %broadcast_select_fusion.3), channel_id=1, source_target_pairs={{1,0},{0,1},{3,2},{2,3},{5,4},{4,5},{7,6},{6,7},{9,8},{8,9},{11,10... | collective-permute-start | bytes 2752520 | tf_op jit(solution)/shard_map/ppermute | solution.py:26
  807.7 25.5 %collective-permute-start.11 = (f32[14,128,128]{2,1,0:T(8,128)S(1)}, f32[14,128,128]{2,1,0:T(8,128)S(1)}, u32[]{:S(2)}, u32[]{:S(2)}) collective-permute-start(f32[14,128,128]{2,1,0:T(8,128)S(1)} %collective-permute-done.10.refs_3_), channel_id=1, source_target_pairs={{2,0},{3,1},{4,2},{5,3},{6,4},{7,5},{0,6},{1,7},{10,8},{11,9},{12,... | collective-permute-start | bytes 2752520 | tf_op jit(solution)/shard_map/ppermute | solution.py:26
  827.4 53.3 %collective-permute-start.8 = (f32[14,128,128]{2,1,0:T(8,128)}, f32[14,128,128]{2,1,0:T(8,128)}, u32[]{:S(2)}, u32[]{:S(2)}) collective-permute-start(f32[14,128,128]{2,1,0:T(8,128)} %collective-permute-done.7.refs_2_), channel_id=1, source_target_pairs={{2,0},{3,1},{4,2},{5,3},{6,4},{7,5},{0,6},{1,7},{10,8},{11,9},{12,... | collective-permute-start | bytes 2752520 | tf_op jit(solution)/shard_map/ppermute | solution.py:26
  833.2 0.9 copy-start.11
  834.2 46.6 %collective-permute-start.5 = (f32[14,128,128]{2,1,0:T(8,128)}, f32[14,128,128]{2,1,0:T(8,128)}, u32[]{:S(2)}, u32[]{:S(2)}) collective-permute-start(f32[14,128,128]{2,1,0:T(8,128)} %collective-permute-done.4.refs_1_), channel_id=1, source_target_pairs={{2,0},{3,1},{4,2},{5,3},{6,4},{7,5},{0,6},{1,7},{10,8},{11,9},{12,... | collective-permute-start | bytes 2752520 | tf_op jit(solution)/shard_map/ppermute | solution.py:26
  837.9 55.2 %collective-permute-start.2 = (f32[14,128,128]{2,1,0:T(8,128)}, f32[14,128,128]{2,1,0:T(8,128)}, u32[]{:S(2)}, u32[]{:S(2)}) collective-permute-start(f32[14,128,128]{2,1,0:T(8,128)} %collective-permute-done.1.refs_0_), channel_id=1, source_target_pairs={{2,0},{3,1},{4,2},{5,3},{6,4},{7,5},{0,6},{1,7},{10,8},{11,9},{12,... | collective-permute-start | bytes 2752520 | tf_op jit(solution)/shard_map/ppermute | solution.py:26
  837.9 1.2 copy-start.3
  839.1 2.0 copy-start.4
  841.1 9.9 %copy-start.6 = (f32[14,128,128]{2,1,0:T(8,128)S(1)}, f32[14,128,128]{2,1,0:T(8,128)}, u32[]{:S(2)}) copy-start(f32[14,128,128]{2,1,0:T(8,128)} %copy-done.5) | copy-start | bytes 2752516
  841.2 9.9 %copy-start.8 = (f32[14,128,128]{2,1,0:T(8,128)S(1)}, f32[14,128,128]{2,1,0:T(8,128)}, u32[]{:S(2)}) copy-start(f32[14,128,128]{2,1,0:T(8,128)} %copy-done.7) | copy-start | bytes 2752516
  851.1 16.9 %copy-start.10 = (f32[14,128,128]{2,1,0:T(8,128)S(1)}, f32[14,128,128]{2,1,0:T(8,128)}, u32[]{:S(2)}) copy-start(f32[14,128,128]{2,1,0:T(8,128)} %copy-done.9) | copy-start | bytes 2752516
  868.0 25.0 %copy-start.12 = (f32[14,128,128]{2,1,0:T(8,128)S(1)}, f32[14,128,128]{2,1,0:T(8,128)}, u32[]{:S(2)}) copy-start(f32[14,128,128]{2,1,0:T(8,128)} %copy-done.11) | copy-start | bytes 2752516

commit v2 on v1

v2 whole, which is shorter than its diff:
```python
import functools

import jax
import jax.numpy as jnp
from jax import lax
from jax.experimental import pallas as pl
from jax.experimental.pallas import tpu as pltpu
from jax.sharding import PartitionSpec as P

CBLK = 64
SIZES = (20, 20, 16)
GROUP = 4
VMEM_LIMIT = 60 * 1024 * 1024

ANY = pl.BlockSpec(memory_space=pl.ANY)
HBM = pl.BlockSpec(memory_space=pltpu.HBM)
SMEM = pl.BlockSpec(memory_space=pltpu.SMEM)


def permute(array, mapping):
    rows, cols = lax.axis_size("row"), lax.axis_size("col")
    pairs = []
    for r in range(rows):
        for c in range(cols):
            source = mapping(r, c)
            if source is not None:
                pairs.append(((source[0] % rows) * cols + source[1] % cols, r * cols + c))
    return lax.ppermute(array, ("row", "col"), pairs)


def fill_kernel(a_pick, b_pick, near_a, near_b, near_c, flags, a_blocks, b_blocks, out, a_ref, b_ref, sem):
    panel = a_blocks.shape[0]
    load_a = pltpu.make_async_copy(a_blocks, a_ref, sem.at[0])
    load_b = pltpu.make_async_copy(b_blocks, b_ref, sem.at[1])
    load_a.start()
    load_b.start()
    for side, (load, pick, held) in enumerate([(load_a, a_pick, a_ref), (load_b, b_pick, b_ref)]):
        load.wait()

        def body(q, carry, side=side, pick=pick, held=held):
            p = pick[q]

            @pl.when(p < panel)
            def _():
                pltpu.make_async_copy(held.at[p], out.at[q, side], sem.at[2 + side]).start()

            return carry

        lax.fori_loop(0, pick.shape[0], body, 0)
    pltpu.make_async_copy(a_blocks, a_ref, sem.at[2]).wait()
    pltpu.make_async_copy(b_blocks, b_ref, sem.at[3]).wait()


def fill(a_pick, b_pick, small, a_blocks, b_blocks):
    slots = a_pick.shape[0]
    panel, width, _ = a_blocks.shape
    return pl.pallas_call(
        fill_kernel,
        out_shape=jax.ShapeDtypeStruct((slots, 2, width, width), jnp.float32),
        in_specs=[SMEM] * 6 + [HBM, HBM],
        out_specs=HBM,
        scratch_shapes=[
            pltpu.VMEM((panel, width, width), jnp.float32),
            pltpu.VMEM((panel, width, width), jnp.float32),
            pltpu.SemaphoreType.DMA((4,)),
        ],
        compiler_params=pltpu.CompilerParams(vmem_limit_bytes=VMEM_LIMIT),
        cost_estimate=pl.CostEstimate(flops=0, bytes_accessed=16 * a_blocks.size, transcendentals=0),
        name="fill",
    )(a_pick, b_pick, *small, a_blocks, b_blocks)


def compact_kernel(a_place, b_place, arrived, a_out, b_out, a_ref, b_ref, in_sem, out_sem):
    sides = [(a_place, a_ref, a_out), (b_place, b_ref, b_out)]
    for side, (place, held, out) in enumerate(sides):

        def body(j, carry, side=side, place=place, held=held):
            pltpu.make_async_copy(arrived.at[place[j], side], held.at[j], in_sem.at[side]).start()
            return carry

        lax.fori_loop(0, place.shape[0], body, 0)
    for side, (place, held, out) in enumerate(sides):
        pltpu.make_async_copy(held, held, in_sem.at[side]).wait()
        pltpu.make_async_copy(held, out, out_sem.at[side]).start()
    for side, (place, held, out) in enumerate(sides):
        pltpu.make_async_copy(held, out, out_sem.at[side]).wait()


def compact(a_place, b_place, arrived):
    panel = a_place.shape[0]
    width = arrived.shape[-1]
    return pl.pallas_call(
        compact_kernel,
        out_shape=[jax.ShapeDtypeStruct((panel, width, width), jnp.float32)] * 2,
        in_specs=[SMEM, SMEM, HBM],
        out_specs=[HBM] * 2,
        scratch_shapes=[
            pltpu.VMEM((panel, width, width), jnp.float32),
            pltpu.VMEM((panel, width, width), jnp.float32),
            pltpu.SemaphoreType.DMA((2,)),
            pltpu.SemaphoreType.DMA((2,)),
        ],
        compiler_params=pltpu.CompilerParams(vmem_limit_bytes=VMEM_LIMIT),
        cost_estimate=pl.CostEstimate(flops=0, bytes_accessed=16 * panel * width * width, transcendentals=0),
        name="compact",
    )(a_place, b_place, arrived)


def split(value):
    high = value.astype(jnp.bfloat16)
    low = (value - high.astype(jnp.float32)).astype(jnp.bfloat16)
    return high, low


def block_product(left, right):
    lh, ll = split(left)
    rh, rl = split(right)
    both = jnp.dot(
        jnp.concatenate([lh, ll], axis=1),
        jnp.concatenate([rh, rh], axis=0),
        preferred_element_type=jnp.float32,
    )
    return both + jnp.dot(lh, rl, preferred_element_type=jnp.float32)


def step_kernel(t, first, parts, options, has_c, flags, index_a, index_b, index_c, *refs):
    a_parts, b_in = refs[:parts], refs[parts : parts + options]
    refs = refs[parts + options :]
    if has_c:
        c_in, refs = refs[0], refs[1:]
    c_out, a_ref, b_ref, c_ref, live, sem = refs
    sizes = [part.shape[0] for part in a_parts]
    last = first + sum(sizes)
    blocks = c_out.shape[0]
    entries = index_a.shape[1]

    copies = [
        pltpu.make_async_copy(a_parts[i], a_ref.at[pl.ds(sum(sizes[:i]), sizes[i])], sem.at[i])
        for i in range(parts)
    ]
    if has_c:
        copies.append(pltpu.make_async_copy(c_in, c_ref, sem.at[parts + 1]))
    for copy in copies:
        copy.start()
    b_copies = [pltpu.make_async_copy(ref, b_ref, sem.at[parts]) for ref in b_in]
    for k, copy in enumerate(b_copies):
        if options == 1:
            copy.start()
        else:
            pl.when(flags[0] == k)(copy.start)

    def listing(e, count):
        live[count] = e
        slot = index_a[t, e]
        used = (index_c[t, e] < blocks) & (slot >= first) & (slot < last)
        return count + jnp.where(used, 1, 0)

    count = lax.fori_loop(0, entries, listing, 0, unroll=4)
    if not has_c:
        c_ref[...] = jnp.zeros_like(c_ref)
    for copy in copies + b_copies[:1]:
        copy.wait()

    def add(at):
        e = live[at]
        c_ref[index_c[t, e]] += block_product(a_ref[index_a[t, e] - first], b_ref[index_b[t, e]])

    def several(g, carry):
        for u in range(GROUP):
            add(g * GROUP + u)
        return carry

    def single(at, carry):
        add(at)
        return carry

    groups = count // GROUP
    lax.fori_loop(0, groups, several, 0)
    lax.fori_loop(groups * GROUP, count, single, 0)
    out = pltpu.make_async_copy(c_ref, c_out, sem.at[parts + 1])
    out.start()
    out.wait()


def step_product(t, flags, prods, first, a_parts, b_in, total):
    parts, options = len(a_parts), len(b_in)
    held = sum(part.shape[0] for part in a_parts)
    width = a_parts[0].shape[1]
    panel = b_in[0].shape[0]
    has_c = total is not None
    operands = [flags, *prods, *a_parts, *b_in]
    in_specs = [SMEM] * 4 + [ANY] * (parts + options)
    aliases = {}
    if has_c:
        aliases = {len(operands): 0}
        operands.append(total)
        in_specs.append(ANY)
    entries = prods[0].shape[1]
    return pl.pallas_call(
        functools.partial(step_kernel, t, first, parts, options, has_c),
        out_shape=jax.ShapeDtypeStruct((CBLK, width, width), jnp.float32),
        in_specs=in_specs,
        out_specs=ANY,
        scratch_shapes=[
            pltpu.VMEM((held, width, width), jnp.float32),
            pltpu.VMEM((panel, width, width), jnp.float32),
            pltpu.VMEM((CBLK, width, width), jnp.float32),
            pltpu.SMEM((entries + 1,), jnp.int32),
            pltpu.SemaphoreType.DMA((parts + 2,)),
        ],
        input_output_aliases=aliases,
        compiler_params=pltpu.CompilerParams(vmem_limit_bytes=VMEM_LIMIT),
        cost_estimate=pl.CostEstimate(
            flops=6000 * entries * width**3, bytes_accessed=16 * panel * width * width, transcendentals=0
        ),
        name="step",
    )(*operands)


def together(*values):
    return lax.optimization_barrier(values)


def local(a_blocks, a_pick, a_place, b_blocks, b_pick, b_place, prod_a, prod_b, prod_c):
    flags = jnp.stack([lax.axis_index("row") % 2, lax.axis_index("col") % 2]).astype(jnp.int32)
    prods = (prod_a, prod_b, prod_c)
    outgoing = fill(a_pick, b_pick, (*prods, flags), a_blocks, b_blocks)
    arrived = lax.all_to_all(outgoing, ("row", "col"), split_axis=0, concat_axis=0, tiled=True)
    a0, b0 = compact(a_place, b_place, arrived)
    a0, b0, flags = together(a0, b0, flags)
    upper, odd = flags[0] == 1, flags[1] == 1

    step = functools.partial(step_product, flags=flags, prods=prods)
    a2 = permute(a0, lambda r, c: (r, c + 2))
    b1 = permute(b0, lambda r, c: (r + 1, c))
    b3_even = permute(b0, lambda r, c: None if r % 2 else (r + 3, c))
    total = step(0, first=0, a_parts=[a0], b_in=[b0], total=None)
    a0, a2, b0, b1, b3_even, total = together(a0, a2, b0, b1, b3_even, total)

    firsts = [sum(SIZES[:i]) for i in range(len(SIZES))]
    a1 = []
    for first, size in zip(firsts, SIZES):
        rows = slice(first, first + size)
        a1.append(permute(jnp.where(odd, a0[rows], a2[rows]), lambda r, c: (r, c ^ 1)))
    b2 = permute(jnp.where(upper, b1, b3_even), lambda r, c: (r ^ 1, c))
    b3_odd = permute(b0, lambda r, c: (r + 3, c) if r % 2 else None)
    total = step(2, first=0, a_parts=[a2], b_in=[b2], total=total)
    a1[-1], total = together(a1[-1], total)
    a3 = [permute(part, lambda r, c: (r, c + 2)) for part in a1]
    total = step(1, first=0, a_parts=a1, b_in=[b1], total=total)
    for first, part in zip(firsts, a3):
        total = step(3, first=first, a_parts=[part], b_in=[b3_even, b3_odd], total=total)
    return total


def solution(mesh):
    placed = (
        P(("row", "col"), None, None),
        P(("row", "col")),
        P(("row", "col")),
        P(("row", "col"), None, None),
        P(("row", "col")),
        P(("row", "col")),
        P(None, ("row", "col")),
        P(None, ("row", "col")),
        P(None, ("row", "col")),
    )
    return jax.shard_map(
        local, mesh=mesh, in_specs=placed, out_specs=P(("row", "col"), None, None), check_vma=False
    )
```

time: 912 us -> 426 us (0.47)
  Pallas kernels: 505 us -> 66.2 us
  waiting for transfers between devices: 157 us -> 131 us
  starting transfers between devices: 40.2 us -> 17.2 us
    pallas_call x5 -> x7, Pallas kernels: 281 us -> 60 us  [the longest x6 53.9 us: step_product(): pl.pallas_call(functools.partial(step_kernel, t, first, parts, options, h...]
    pallas_call x1, Pallas kernels: 224 us -> 6.13 us  [fill(): pl.pallas_call(fill_kernel, out_shape=jax.ShapeDtypeStruct((slots, 2, wid...]
    ppermute x17 -> x11, waiting for transfers between devices: 157 us -> 131 us  [permute(): return lax.ppermute(array, ('row', 'col'), pairs)]
    ppermute x17 -> x11, starting transfers between devices: 40.2 us -> 17.2 us  [permute(): return lax.ppermute(array, ('row', 'col'), pairs)]
  transfers between devices with their start and end apart: 17 -> 11, of which waited for: 8 -> 5; matrix products, arithmetic and copies ran while one was open for 0% -> 1% of each run, Pallas kernels for 4% -> 11%
where the time goes in v2:
time: 426 us
  blocking collectives  199 us (47%)
  waiting for transfers between devices  131 us (31%)
  Pallas kernels  66.2 us (16%)
  starting transfers between devices  17.2 us (4%)
  other arithmetic  8.06 us (2%)
    all_to_all x1, blocking collectives, local(): lax.all_to_all(outgoing, ('row', 'col'), split_axis=0, concat_axis=0, til...  199 us
    ppermute x11, waiting for transfers between devices, permute(): return lax.ppermute(array, ('row', 'col'), pairs)  131 us
    pallas_call x6, Pallas kernels, step_product(): pl.pallas_call(functools.partial(step_kernel, t, first, parts, options, h...  53.9 us
    ppermute x11, starting transfers between devices, permute(): return lax.ppermute(array, ('row', 'col'), pairs)  17.2 us
  transfers between devices with their start and end apart: 11, of which 5 were waited for; matrix products, arithmetic and copies ran while one was open for 1% of the time, Pallas kernels for 11%

profile of v2, /device:TPU:0, one launch (start us, length us, event | category | flops | bytes accessed | tf_op | source)
XLA Modules:
  0.0 425.6 jit_solution(5307908576076158460)
XLA Ops:
  0.0 0.7 pad_add_fusion.flags
  0.7 6.1 %fill.1 = f32[128,2,128,128]{3,2,1,0:T(8,128)} custom-call(s32[128]{0:T(128)} %a_pick.1, s32[128]{0:T(128)} %b_pick.1, s32[4,64]{1,0:T(4,128)} %index_a.11, s32[4,64]{1,0:T(4,128)} %index_b.11, s32[4,64]{1,0:T(4,128)} %index_c.11, s32[2]{0:T(128)} %pad_add_fusion.flags, f32[56,128,128]{2,1,0:T(8,128)} %a_blocks.1, f32[56,128,128]{2,1,0:T(8,128)} %b_blocks.1), custom_call_target="tpu_custom_call" | custom-call | bytes 14680064 | tf_op jit(solution)/shard_map/fill/pallas_call | solution.py:57
  6.8 198.9 %all_to_all.5.arrived = f32[128,2,128,128]{3,2,1,0:T(8,128)} all-to-all(f32[128,2,128,128]{3,2,1,0:T(8,128)} %fill.1), channel_id=1, replica_groups=mesh['row'=16,'col'=8] {'row','col'}, dimensions={0} | all-to-all | bytes 33554432 | tf_op jit(solution)/shard_map/all_to_all | solution.py:228
  205.7 6.1 %compact.1 = (f32[56,128,128]{2,1,0:T(8,128)}, f32[56,128,128]{2,1,0:T(8,128)}) custom-call(s32[56]{0:T(128)} %a_place.1, s32[56]{0:T(128)} %b_place.1, f32[128,2,128,128]{3,2,1,0:T(8,128)} %all_to_all.5.arrived), custom_call_target="tpu_custom_call" | custom-call | bytes 14680064 | tf_op jit(solution)/shard_map/compact/pallas_call | solution.py:92
  211.8 1.3 collective-permute-start.2
  213.1 5.8 %collective-permute-start.1 = (f32[56,128,128]{2,1,0:T(8,128)}, f32[56,128,128]{2,1,0:T(8,128)}, u32[]{:S(2)}, u32[]{:S(2)}) collective-permute-start(f32[56,128,128]{2,1,0:T(8,128)} %get-tuple-element.29.refs_1_), channel_id=1, source_target_pairs={{8,0},{9,1},{10,2},{11,3},{12,4},{13,5},{14,6},{15,7},{16,8},{17,9... | collective-permute-start | bytes 11010056 | tf_op jit(solution)/shard_map/ppermute | solution.py:28
  218.9 0.5 collective-permute-start
  219.4 0.0 copy-start.1
  219.4 9.8 %step.6.refs_2_ = f32[64,128,128]{2,1,0:T(8,128)} custom-call(s32[2]{0:T(128)} %pad_add_fusion.flags, s32[4,64]{1,0:T(4,128)} %index_a.11, s32[4,64]{1,0:T(4,128)} %index_b.11, s32[4,64]{1,0:T(4,128)} %index_c.11, f32[56,128,128]{2,1,0:T(8,128)} %get-tuple-element.23.refs_0_, f32[56,128,128]{2,1,0:T(8,128)} %get-tuple-element.29.refs_1_), custom_call_target="tpu_custom_call" | custom-call | flops 805306368000 | bytes 14680064 | tf_op jit(solution)/shard_map/step/pallas_call | solution.py:199
  229.2 0.0 copy-done.1
  229.2 0.6 fusion
  230.4 69.2 %collective-permute-done.refs_0_ = f32[56,128,128]{2,1,0:T(8,128)} collective-permute-done((f32[56,128,128]{2,1,0:T(8,128)}, f32[56,128,128]{2,1,0:T(8,128)}, u32[]{:S(2)}, u32[]{:S(2)}) %collective-permute-start) | collective-permute-done | bytes 3670048 | tf_op jit(solution)/shard_map/ppermute | solution.py:28
  299.6 0.0 collective-permute-done.2.refs_1_
  299.6 0.0 collective-permute-done.1.refs_3_
  299.6 0.0 copy-start
  299.6 2.9 broadcast_select_fusion
  302.6 0.1 collective-permute-start.4
  303.3 0.0 copy-done
  303.3 2.1 slice_select_fusion
  305.4 0.2 collective-permute-start.9
  305.6 1.9 collective-permute-start.7
  307.5 2.4 slice_select_fusion.2
  309.9 0.2 collective-permute-start.3
  310.1 3.4 collective-permute-start.6
  313.4 23.7 %collective-permute-done.9.refs_0_ = f32[20,128,128]{2,1,0:T(8,128)} collective-permute-done((f32[20,128,128]{2,1,0:T(8,128)S(1)}, f32[20,128,128]{2,1,0:T(8,128)}, u32[]{:S(2)}, u32[]{:S(2)}) %collective-permute-start.9) | collective-permute-done | bytes 1310752 | tf_op jit(solution)/shard_map/ppermute | solution.py:28
  337.1 1.3 collective-permute-start.10
  338.4 26.8 %collective-permute-done.7.refs_1_ = f32[20,128,128]{2,1,0:T(8,128)} collective-permute-done((f32[20,128,128]{2,1,0:T(8,128)S(1)}, f32[20,128,128]{2,1,0:T(8,128)}, u32[]{:S(2)}, u32[]{:S(2)}) %collective-permute-start.7) | collective-permute-done | bytes 1310752 | tf_op jit(solution)/shard_map/ppermute | solution.py:28
  365.2 1.3 collective-permute-start.8
  366.5 0.0 collective-permute-done.4.refs_1_
  366.5 0.0 copy-start.2
  366.5 1.8 copy-done.2
  368.4 10.3 %step.7.refs_4_ = f32[64,128,128]{2,1,0:T(8,128)} custom-call(s32[2]{0:T(128)} %pad_add_fusion.flags, s32[4,64]{1,0:T(4,128)} %index_a.11, s32[4,64]{1,0:T(4,128)} %index_b.11, s32[4,64]{1,0:T(4,128)} %index_c.11, f32[56,128,128]{2,1,0:T(8,128)} %collective-permute-done.refs_0_, f32[56,128,128]{2,1,0:T(8,128)} %copy-done.2, ...), custom_call_target="tpu_custom_call", output_to_operand_aliasing={{}: (6, {})} | custom-call | flops 805306368000 | bytes 14680064 | tf_op jit(solution)/shard_map/step/pallas_call | solution.py:199
  378.7 8.6 %collective-permute-done.3.refs_2_ = f32[16,128,128]{2,1,0:T(8,128)} collective-permute-done((f32[16,128,128]{2,1,0:T(8,128)}, f32[16,128,128]{2,1,0:T(8,128)}, u32[]{:S(2)}, u32[]{:S(2)}) %collective-permute-start.3) | collective-permute-done | bytes 1048608 | tf_op jit(solution)/shard_map/ppermute | solution.py:28
  387.3 1.3 collective-permute-start.5
  388.6 11.0 %step.8.refs_3_ = f32[64,128,128]{2,1,0:T(8,128)} custom-call(s32[2]{0:T(128)} %pad_add_fusion.flags, s32[4,64]{1,0:T(4,128)} %index_a.11, s32[4,64]{1,0:T(4,128)} %index_b.11, s32[4,64]{1,0:T(4,128)} %index_c.11, f32[20,128,128]{2,1,0:T(8,128)} %collective-permute-done.9.refs_0_, ...), custom_call_target="tpu_custom_call", output_to_operand_aliasing={{}: (8, {})} | custom-call | flops 805306368000 | bytes 14680064 | tf_op jit(solution)/shard_map/step/pallas_call | solution.py:199
  399.7 0.0 collective-permute-done.10.refs_0_
  399.7 0.0 collective-permute-done.6.refs_2_
  399.7 7.5 %step.9.refs_3_ = f32[64,128,128]{2,1,0:T(8,128)} custom-call(s32[2]{0:T(128)} %pad_add_fusion.flags, s32[4,64]{1,0:T(4,128)} %index_a.11, s32[4,64]{1,0:T(4,128)} %index_b.11, s32[4,64]{1,0:T(4,128)} %index_c.11, f32[20,128,128]{2,1,0:T(8,128)} %collective-permute-done.10.refs_0_, ...), custom_call_target="tpu_custom_call", output_to_operand_aliasing={{}: (7, {})} | custom-call | flops 805306368000 | bytes 14680064 | tf_op jit(solution)/shard_map/step/pallas_call | solution.py:199
  407.2 0.0 collective-permute-done.8.refs_0_
  407.2 7.8 %step.10.refs_3_ = f32[64,128,128]{2,1,0:T(8,128)} custom-call(s32[2]{0:T(128)} %pad_add_fusion.flags, s32[4,64]{1,0:T(4,128)} %index_a.11, s32[4,64]{1,0:T(4,128)} %index_b.11, s32[4,64]{1,0:T(4,128)} %index_c.11, f32[20,128,128]{2,1,0:T(8,128)} %collective-permute-done.8.refs_0_, ...), custom_call_target="tpu_custom_call", output_to_operand_aliasing={{}: (7, {})} | custom-call | flops 805306368000 | bytes 14680064 | tf_op jit(solution)/shard_map/step/pallas_call | solution.py:199
  415.0 3.1 collective-permute-done.5.refs_0_
  418.1 7.5 %step.11 = f32[64,128,128]{2,1,0:T(8,128)} custom-call(s32[2]{0:T(128)} %pad_add_fusion.flags, s32[4,64]{1,0:T(4,128)} %index_a.11, s32[4,64]{1,0:T(4,128)} %index_b.11, s32[4,64]{1,0:T(4,128)} %index_c.11, f32[16,128,128]{2,1,0:T(8,128)} %collective-permute-done.5.refs_0_, ...), custom_call_target="tpu_custom_call", output_to_operand_aliasing={{}: (7, {})} | custom-call | flops 805306368000 | bytes 14680064 | tf_op jit(solution)/shard_map/step/pallas_call | solution.py:199
Async XLA Ops:
  211.8 87.8 %collective-permute-start.2 = (f32[56,128,128]{2,1,0:T(8,128)}, f32[56,128,128]{2,1,0:T(8,128)}, u32[]{:S(2)}, u32[]{:S(2)}) collective-permute-start(f32[56,128,128]{2,1,0:T(8,128)} %get-tuple-element.29.refs_1_), channel_id=1, source_target_pairs={{24,0},{25,1},{26,2},{27,3},{28,4},{29,5},{30,6},{31,7},{40,16},{4... | collective-permute-start | bytes 11010056 | tf_op jit(solution)/shard_map/ppermute | solution.py:28
  213.1 86.5 %collective-permute-start.1 = (f32[56,128,128]{2,1,0:T(8,128)}, f32[56,128,128]{2,1,0:T(8,128)}, u32[]{:S(2)}, u32[]{:S(2)}) collective-permute-start(f32[56,128,128]{2,1,0:T(8,128)} %get-tuple-element.29.refs_1_), channel_id=1, source_target_pairs={{8,0},{9,1},{10,2},{11,3},{12,4},{13,5},{14,6},{15,7},{16,8},{17,9... | collective-permute-start | bytes 11010056 | tf_op jit(solution)/shard_map/ppermute | solution.py:28
  218.9 80.7 %collective-permute-start = (f32[56,128,128]{2,1,0:T(8,128)}, f32[56,128,128]{2,1,0:T(8,128)}, u32[]{:S(2)}, u32[]{:S(2)}) collective-permute-start(f32[56,128,128]{2,1,0:T(8,128)} %get-tuple-element.23.refs_0_), channel_id=1, source_target_pairs={{2,0},{3,1},{4,2},{5,3},{6,4},{7,5},{0,6},{1,7},{10,8},{11,9},{12,... | collective-permute-start | bytes 11010056 | tf_op jit(solution)/shard_map/ppermute | solution.py:28
  219.4 9.8 %copy-start.1 = (s32[2]{0:T(128)S(1)}, s32[2]{0:T(128)}, u32[]{:S(2)}) copy-start(s32[2]{0:T(128)} %pad_add_fusion.flags) | copy-start | bytes 28
  299.6 3.6 copy-start
  302.6 64.0 %collective-permute-start.4 = (f32[56,128,128]{2,1,0:T(8,128)S(1)}, f32[56,128,128]{2,1,0:T(8,128)S(1)}, u32[]{:S(2)}, u32[]{:S(2)}) collective-permute-start(f32[56,128,128]{2,1,0:T(8,128)S(1)} %broadcast_select_fusion), channel_id=1, source_target_pairs={{8,0},{9,1},{10,2},{11,3},{12,4},{13,5},{14,6},{15,7},{0,8},{1,9},... | collective-permute-start | bytes 11010056 | tf_op jit(solution)/shard_map/ppermute | solution.py:28
  305.4 31.8 %collective-permute-start.9 = (f32[20,128,128]{2,1,0:T(8,128)S(1)}, f32[20,128,128]{2,1,0:T(8,128)}, u32[]{:S(2)}, u32[]{:S(2)}) collective-permute-start(f32[20,128,128]{2,1,0:T(8,128)S(1)} %get-tuple-element.31), channel_id=1, source_target_pairs={{1,0},{0,1},{3,2},{2,3},{5,4},{4,5},{7,6},{6,7},{9,8},{8,9},{11,10... | collective-permute-start | bytes 3932168 | tf_op jit(solution)/shard_map/ppermute | solution.py:28
  305.6 59.6 %collective-permute-start.7 = (f32[20,128,128]{2,1,0:T(8,128)S(1)}, f32[20,128,128]{2,1,0:T(8,128)}, u32[]{:S(2)}, u32[]{:S(2)}) collective-permute-start(f32[20,128,128]{2,1,0:T(8,128)S(1)} %get-tuple-element.32), channel_id=1, source_target_pairs={{1,0},{0,1},{3,2},{2,3},{5,4},{4,5},{7,6},{6,7},{9,8},{8,9},{11,10... | collective-permute-start | bytes 3932168 | tf_op jit(solution)/shard_map/ppermute | solution.py:28
  309.9 77.4 %collective-permute-start.3 = (f32[16,128,128]{2,1,0:T(8,128)}, f32[16,128,128]{2,1,0:T(8,128)}, u32[]{:S(2)}, u32[]{:S(2)}) collective-permute-start(f32[16,128,128]{2,1,0:T(8,128)} %slice_select_fusion.2), channel_id=1, source_target_pairs={{1,0},{0,1},{3,2},{2,3},{5,4},{4,5},{7,6},{6,7},{9,8},{8,9},{11,10... | collective-permute-start | bytes 3145736 | tf_op jit(solution)/shard_map/ppermute | solution.py:28
  310.1 89.6 %collective-permute-start.6 = (f32[56,128,128]{2,1,0:T(8,128)}, f32[56,128,128]{2,1,0:T(8,128)}, u32[]{:S(2)}, u32[]{:S(2)}) collective-permute-start(f32[56,128,128]{2,1,0:T(8,128)} %get-tuple-element.29.refs_1_), channel_id=1, source_target_pairs={{32,8},{33,9},{34,10},{35,11},{36,12},{37,13},{38,14},{39,15},{48,... | collective-permute-start | bytes 11010056 | tf_op jit(solution)/shard_map/ppermute | solution.py:28
  337.1 62.5 %collective-permute-start.10 = (f32[20,128,128]{2,1,0:T(8,128)}, f32[20,128,128]{2,1,0:T(8,128)}, u32[]{:S(2)}, u32[]{:S(2)}) collective-permute-start(f32[20,128,128]{2,1,0:T(8,128)} %collective-permute-done.9.refs_0_), channel_id=1, source_target_pairs={{2,0},{3,1},{4,2},{5,3},{6,4},{7,5},{0,6},{1,7},{10,8},{11,9},{12,... | collective-permute-start | bytes 3932168 | tf_op jit(solution)/shard_map/ppermute | solution.py:28
  365.2 41.9 %collective-permute-start.8 = (f32[20,128,128]{2,1,0:T(8,128)}, f32[20,128,128]{2,1,0:T(8,128)}, u32[]{:S(2)}, u32[]{:S(2)}) collective-permute-start(f32[20,128,128]{2,1,0:T(8,128)} %collective-permute-done.7.refs_1_), channel_id=1, source_target_pairs={{2,0},{3,1},{4,2},{5,3},{6,4},{7,5},{0,6},{1,7},{10,8},{11,9},{12,... | collective-permute-start | bytes 3932168 | tf_op jit(solution)/shard_map/ppermute | solution.py:28
  366.5 1.8 copy-start.2
  387.3 30.8 %collective-permute-start.5 = (f32[16,128,128]{2,1,0:T(8,128)}, f32[16,128,128]{2,1,0:T(8,128)}, u32[]{:S(2)}, u32[]{:S(2)}) collective-permute-start(f32[16,128,128]{2,1,0:T(8,128)} %collective-permute-done.3.refs_2_), channel_id=1, source_target_pairs={{2,0},{3,1},{4,2},{5,3},{6,4},{7,5},{0,6},{1,7},{10,8},{11,9},{12,... | collective-permute-start | bytes 3145736 | tf_op jit(solution)/shard_map/ppermute | solution.py:28

commit v3 on v2

--- a/solution.py
+++ b/solution.py
@@ -8,7 +8,7 @@
 from jax.sharding import PartitionSpec as P
 
 CBLK = 64
-SIZES = (20, 20, 16)
+SIZES = (14, 14, 14, 14)
 GROUP = 4
 VMEM_LIMIT = 60 * 1024 * 1024
 
@@ -123,97 +123,216 @@
     return both + jnp.dot(lh, rl, preferred_element_type=jnp.float32)
 
 
-def step_kernel(t, first, parts, options, has_c, flags, index_a, index_b, index_c, *refs):
-    a_parts, b_in = refs[:parts], refs[parts : parts + options]
-    refs = refs[parts + options :]
-    if has_c:
-        c_in, refs = refs[0], refs[1:]
-    c_out, a_ref, b_ref, c_ref, live, sem = refs
-    sizes = [part.shape[0] for part in a_parts]
-    last = first + sum(sizes)
+def products_kernel(jobs, has_c, flags, index_a, index_b, index_c, *refs):
+    refs = list(refs)
+    sources = []
+    for _, _, sizes, options in jobs:
+        sources.append((refs[: len(sizes)], refs[len(sizes) : len(sizes) + options]))
+        del refs[: len(sizes) + options]
+    c_in = refs.pop(0) if has_c else None
+    c_out = refs.pop(0)
+    held = [(refs[2 * n], refs[2 * n + 1]) for n in range(len(jobs))]
+    c_ref, live, sem = refs[2 * len(jobs) :]
     blocks = c_out.shape[0]
     entries = index_a.shape[1]
 
-    copies = [
-        pltpu.make_async_copy(a_parts[i], a_ref.at[pl.ds(sum(sizes[:i]), sizes[i])], sem.at[i])
-        for i in range(parts)
-    ]
     if has_c:
-        copies.append(pltpu.make_async_copy(c_in, c_ref, sem.at[parts + 1]))
-    for copy in copies:
-        copy.start()
-    b_copies = [pltpu.make_async_copy(ref, b_ref, sem.at[parts]) for ref in b_in]
-    for k, copy in enumerate(b_copies):
-        if options == 1:
+        load_c = pltpu.make_async_copy(c_in, c_ref, sem.at[len(jobs), 0])
+        load_c.start()
+    waits = []
+    for n, (_, _, sizes, options) in enumerate(jobs):
+        a_ref, b_ref = held[n]
+        a_parts, b_in = sources[n]
+        copies = [
+            pltpu.make_async_copy(part, a_ref.at[pl.ds(sum(sizes[:i]), sizes[i])], sem.at[n, i])
+            for i, part in enumerate(a_parts)
+        ]
+        for copy in copies:
             copy.start()
-        else:
-            pl.when(flags[0] == k)(copy.start)
-
-    def listing(e, count):
-        live[count] = e
-        slot = index_a[t, e]
-        used = (index_c[t, e] < blocks) & (slot >= first) & (slot < last)
-        return count + jnp.where(used, 1, 0)
-
-    count = lax.fori_loop(0, entries, listing, 0, unroll=4)
-    if not has_c:
+        b_copies = [pltpu.make_async_copy(ref, b_ref, sem.at[n, len(sizes)]) for ref in b_in]
+        for k, copy in enumerate(b_copies):
+            if options == 1:
+                copy.start()
+            else:
+                pl.when(flags[0] == k)(copy.start)
+        waits.append(copies + b_copies[:1])
+
+    counts = []
+    for n, (t, first, sizes, _) in enumerate(jobs):
+
+        def listing(e, count, n=n, t=t, first=first, last=first + sum(sizes)):
+            live[n, count] = e
+            slot = index_a[t, e]
+            used = (index_c[t, e] < blocks) & (slot >= first) & (slot < last)
+            return count + jnp.where(used, 1, 0)
+
+        counts.append(lax.fori_loop(0, entries, listing, 0, unroll=4))
+    if has_c:
+        load_c.wait()
+    else:
         c_ref[...] = jnp.zeros_like(c_ref)
-    for copy in copies + b_copies[:1]:
-        copy.wait()
-
-    def add(at):
-        e = live[at]
-        c_ref[index_c[t, e]] += block_product(a_ref[index_a[t, e] - first], b_ref[index_b[t, e]])
-
-    def several(g, carry):
-        for u in range(GROUP):
-            add(g * GROUP + u)
-        return carry
-
-    def single(at, carry):
-        add(at)
-        return carry
-
-    groups = count // GROUP
-    lax.fori_loop(0, groups, several, 0)
-    lax.fori_loop(groups * GROUP, count, single, 0)
-    out = pltpu.make_async_copy(c_ref, c_out, sem.at[parts + 1])
+
+    for n, (t, first, _, _) in enumerate(jobs):
+        a_ref, b_ref = held[n]
+        for copy in waits[n]:
+            copy.wait()
+
+        def add(at, n=n, t=t, first=first, a_ref=a_ref, b_ref=b_ref):
+            e = live[n, at]
+            c_ref[index_c[t, e]] += block_product(a_ref[index_a[t, e] - first], b_ref[index_b[t, e]])
+
+        def several(g, carry, add=add):
+            for u in range(GROUP):
+                add(g * GROUP + u)
+            return carry
+
+        def single(at, carry, add=add):
+            add(at)
+            return carry
+
+        groups = counts[n] // GROUP
+        lax.fori_loop(0, groups, several, 0)
+        lax.fori_loop(groups * GROUP, counts[n], single, 0)
+    out = pltpu.make_async_copy(c_ref, c_out, sem.at[len(jobs), 0])
     out.start()
     out.wait()
 
 
-def step_product(t, flags, prods, first, a_parts, b_in, total):
-    parts, options = len(a_parts), len(b_in)
-    held = sum(part.shape[0] for part in a_parts)
-    width = a_parts[0].shape[1]
-    panel = b_in[0].shape[0]
+def products(flags, prods, jobs, total):
+    entries = prods[0].shape[1]
+    width = jobs[0][2][0].shape[1]
     has_c = total is not None
-    operands = [flags, *prods, *a_parts, *b_in]
-    in_specs = [SMEM] * 4 + [ANY] * (parts + options)
+    operands = [flags, *prods]
+    scratch = []
+    static = []
+    for t, first, parts, b_in in jobs:
+        operands += [*parts, *b_in]
+        sizes = tuple(part.shape[0] for part in parts)
+        static.append((t, first, sizes, len(b_in)))
+        scratch.append(pltpu.VMEM((sum(sizes), width, width), jnp.float32))
+        scratch.append(pltpu.VMEM(b_in[0].shape, jnp.float32))
     aliases = {}
     if has_c:
         aliases = {len(operands): 0}
         operands.append(total)
-        in_specs.append(ANY)
-    entries = prods[0].shape[1]
+    slots = max(len(sizes) for _, _, sizes, _ in static) + 1
     return pl.pallas_call(
-        functools.partial(step_kernel, t, first, parts, options, has_c),
+        functools.partial(products_kernel, tuple(static), has_c),
         out_shape=jax.ShapeDtypeStruct((CBLK, width, width), jnp.float32),
-        in_specs=in_specs,
+        in_specs=[SMEM] * 4 + [ANY] * (len(operands) - 4),
         out_specs=ANY,
-        scratch_shapes=[
-            pltpu.VMEM((held, width, width), jnp.float32),
-            pltpu.VMEM((panel, width, width), jnp.float32),
+        scratch_shapes=scratch
+        + [
             pltpu.VMEM((CBLK, width, width), jnp.float32),
-            pltpu.SMEM((entries + 1,), jnp.int32),
-            pltpu.SemaphoreType.DMA((parts + 2,)),
+            pltpu.SMEM((len(jobs), entries + 1), jnp.int32),
+            pltpu.SemaphoreType.DMA((len(jobs) + 1, slots)),
         ],
         input_output_aliases=aliases,
         compiler_params=pltpu.CompilerParams(vmem_limit_bytes=VMEM_LIMIT),
         cost_estimate=pl.CostEstimate(
-            flops=6000 * entries * width**3, bytes_accessed=16 * panel * width * width, transcendentals=0
+            flops=6000 * entries * width**3, bytes_accessed=8 * CBLK * width * width, transcendentals=0
         ),
-        name="step",
+        name="products",
+    )(*operands)
+
+
+def last_kernel(t, first, options, flags, index_a, index_b, index_c, *refs):
+    a_in, b_in = refs[0], refs[1 : 1 + options]
+    c_in, c_out, a_ref, b_ref, c_ref, live, place, sem = refs[1 + options :]
+    blocks = c_out.shape[0]
+    entries = index_a.shape[1]
+    size = a_in.shape[0]
+
+    def clear(m, carry):
+        place[m] = -1
+        return carry
+
+    lax.fori_loop(0, blocks, clear, 0, unroll=8)
+
+    def fetch(e, counts):
+        slot, m = index_a[t, e] - first, index_c[t, e]
+        used = (m < blocks) & (slot >= 0) & (slot < size)
+        count, kept = counts
+        new = used & (place[jnp.minimum(m, blocks - 1)] < 0)
+
+        @pl.when(used)
+        def _():
+            live[count] = e
+            pltpu.make_async_copy(a_in.at[slot], a_ref.at[count], sem.at[0]).start()
+            for k, ref in enumerate(b_in):
+
+                @pl.when(flags[0] == k)
+                def _(ref=ref):
+                    pltpu.make_async_copy(ref.at[index_b[t, e]], b_ref.at[count], sem.at[0]).start()
+
+        @pl.when(new)
+        def _():
+            place[m] = kept
+            live[entries + kept] = m
+            pltpu.make_async_copy(c_in.at[m], c_ref.at[kept], sem.at[0]).start()
+
+        return count + jnp.where(used, 1, 0), kept + jnp.where(new, 1, 0)
+
+    count, kept = lax.fori_loop(0, entries, fetch, (0, 0))
+
+    def arrive(_, carry):
+        pltpu.make_async_copy(c_in.at[0], c_ref.at[0], sem.at[0]).wait()
+        return carry
+
+    lax.fori_loop(0, 2 * count + kept, arrive, 0)
+
+    def add(at):
+        c_ref[place[index_c[t, live[at]]]] += block_product(a_ref[at], b_ref[at])
+
+    def several(g, carry):
+        for u in range(GROUP):
+            add(g * GROUP + u)
+        return carry
+
+    def single(at, carry):
+        add(at)
+        return carry
+
+    groups = count // GROUP
+    lax.fori_loop(0, groups, several, 0)
+    lax.fori_loop(groups * GROUP, count, single, 0)
+
+    def store(k, carry):
+        pltpu.make_async_copy(c_ref.at[k], c_out.at[live[entries + k]], sem.at[1]).start()
+        return carry
+
+    lax.fori_loop(0, kept, store, 0)
+
+    def leave(_, carry):
+        pltpu.make_async_copy(c_ref.at[0], c_out.at[0], sem.at[1]).wait()
+        return carry
+
+    lax.fori_loop(0, kept, leave, 0)
+
+
+def last_products(flags, prods, t, first, a_in, b_in, total):
+    entries = prods[0].shape[1]
+    block = a_in.shape[1:]
+    operands = [flags, *prods, a_in, *b_in, total]
+    return pl.pallas_call(
+        functools.partial(last_kernel, t, first, len(b_in)),
+        out_shape=jax.ShapeDtypeStruct(total.shape, jnp.float32),
+        in_specs=[SMEM] * 4 + [ANY] * (len(operands) - 4),
+        out_specs=ANY,
+        scratch_shapes=[
+            pltpu.VMEM((entries, *block), jnp.float32),
+            pltpu.VMEM((entries, *block), jnp.float32),
+            pltpu.VMEM((total.shape[0], *block), jnp.float32),
+            pltpu.SMEM((entries + total.shape[0],), jnp.int32),
+            pltpu.SMEM((total.shape[0],), jnp.int32),
+            pltpu.SemaphoreType.DMA((2,)),
+        ],
+        input_output_aliases={len(operands) - 1: 0},
+        compiler_params=pltpu.CompilerParams(vmem_limit_bytes=VMEM_LIMIT),
+        cost_estimate=pl.CostEstimate(
+            flops=6000 * entries * block[0] ** 3, bytes_accessed=8 * total.size, transcendentals=0
+        ),
+        name="last_products",
     )(*operands)
 
 
@@ -230,27 +349,43 @@
     a0, b0, flags = together(a0, b0, flags)
     upper, odd = flags[0] == 1, flags[1] == 1
 
-    step = functools.partial(step_product, flags=flags, prods=prods)
+    add = functools.partial(products, flags, prods)
     a2 = permute(a0, lambda r, c: (r, c + 2))
     b1 = permute(b0, lambda r, c: (r + 1, c))
     b3_even = permute(b0, lambda r, c: None if r % 2 else (r + 3, c))
-    total = step(0, first=0, a_parts=[a0], b_in=[b0], total=None)
+    total = add([(0, 0, [a0], [b0])], None)
     a0, a2, b0, b1, b3_even, total = together(a0, a2, b0, b1, b3_even, total)
 
     firsts = [sum(SIZES[:i]) for i in range(len(SIZES))]
-    a1 = []
+    cross = []
     for first, size in zip(firsts, SIZES):
         rows = slice(first, first + size)
-        a1.append(permute(jnp.where(odd, a0[rows], a2[rows]), lambda r, c: (r, c ^ 1)))
+        cross.append(jnp.where(odd, a0[rows], a2[rows]))
+        if first == 0:
+            a0, a2, cross[0] = together(a0, a2, cross[0])
+    b1, b3_even, cross[0] = together(b1, b3_even, cross[0])
+    a1 = [permute(part, lambda r, c: (r, c ^ 1)) for part in cross]
     b2 = permute(jnp.where(upper, b1, b3_even), lambda r, c: (r ^ 1, c))
+    b0, a1[0] = together(b0, a1[0])
     b3_odd = permute(b0, lambda r, c: (r + 3, c) if r % 2 else None)
-    total = step(2, first=0, a_parts=[a2], b_in=[b2], total=total)
-    a1[-1], total = together(a1[-1], total)
-    a3 = [permute(part, lambda r, c: (r, c + 2)) for part in a1]
-    total = step(1, first=0, a_parts=a1, b_in=[b1], total=total)
-    for first, part in zip(firsts, a3):
-        total = step(3, first=first, a_parts=[part], b_in=[b3_even, b3_odd], total=total)
-    return total
+    b3 = [b3_even, b3_odd]
+    a3 = []
+
+    def onward():
+        a3.append(permute(a1[len(a3)], lambda r, c: (r, c + 2)))
+
+    onward()
+    total = add([(2, 0, [a2], [b2])], total)
+    a1[1], total = together(a1[1], total)
+    onward()
+    total = add([(1, 0, a1[:2], [b1])], total)
+    a1[2], total = together(a1[2], total)
+    onward()
+    total = add([(3, 0, a3[:1], b3)], total)
+    a1[3], total = together(a1[3], total)
+    onward()
+    total = add([(1, firsts[2], a1[2:], [b1]), (3, firsts[1], a3[1:3], b3)], total)
+    return last_products(flags, prods, 3, firsts[3], a3[3], b3, total)
 
 
 def solution(mesh):

time: 426 us -> 413 us (0.969)
  waiting for transfers between devices: 131 us -> 119 us
    ppermute x11 -> x13, waiting for transfers between devices: 131 us -> 119 us  [permute(): return lax.ppermute(array, ('row', 'col'), pairs)]
    ppermute x11 -> x13, starting transfers between devices: 17.2 us -> 20.2 us  [permute(): return lax.ppermute(array, ('row', 'col'), pairs)]
  transfers between devices with their start and end apart: 11 -> 13, of which waited for: 5 -> 8; matrix products, arithmetic and copies ran while one was open for 1% -> 1% of each run, Pallas kernels for 11% -> 11%
where the time goes in v3:
time: 413 us
  blocking collectives  199 us (48%)
  waiting for transfers between devices  119 us (29%)
  Pallas kernels  63 us (15%)
  starting transfers between devices  20.2 us (5%)
  other arithmetic  8.06 us (2%)
    all_to_all x1, blocking collectives, local(): lax.all_to_all(outgoing, ('row', 'col'), split_axis=0, concat_axis=0, til...  199 us
    ppermute x13, waiting for transfers between devices, permute(): return lax.ppermute(array, ('row', 'col'), pairs)  119 us
    pallas_call x5, Pallas kernels, products(): pl.pallas_call(functools.partial(products_kernel, tuple(static), has_c),...  45.9 us
    ppermute x13, starting transfers between devices, permute(): return lax.ppermute(array, ('row', 'col'), pairs)  20.2 us
  transfers between devices with their start and end apart: 13, of which 8 were waited for; matrix products, arithmetic and copies ran while one was open for 1% of the time, Pallas kernels for 11%

profile of v3, /device:TPU:0, one launch (start us, length us, event | category | flops | bytes accessed | tf_op | source)
XLA Modules:
  0.0 412.8 jit_solution(11239609321280822846)
XLA Ops:
  0.0 0.7 pad_add_fusion.flags
  0.7 6.1 %fill.1 = f32[128,2,128,128]{3,2,1,0:T(8,128)} custom-call(s32[128]{0:T(128)} %a_pick.1, s32[128]{0:T(128)} %b_pick.1, s32[4,64]{1,0:T(4,128)} %index_a.11, s32[4,64]{1,0:T(4,128)} %index_b.11, s32[4,64]{1,0:T(4,128)} %index_c.11, s32[2]{0:T(128)} %pad_add_fusion.flags, f32[56,128,128]{2,1,0:T(8,128)} %a_blocks.1, f32[56,128,128]{2,1,0:T(8,128)} %b_blocks.1), custom_call_target="tpu_custom_call" | custom-call | bytes 14680064 | tf_op jit(solution)/shard_map/fill/pallas_call | solution.py:57
  6.7 199.0 %all_to_all.5.arrived = f32[128,2,128,128]{3,2,1,0:T(8,128)} all-to-all(f32[128,2,128,128]{3,2,1,0:T(8,128)} %fill.1), channel_id=1, replica_groups=mesh['row'=16,'col'=8] {'row','col'}, dimensions={0} | all-to-all | bytes 33554432 | tf_op jit(solution)/shard_map/all_to_all | solution.py:347
  205.7 6.1 %compact.1 = (f32[56,128,128]{2,1,0:T(8,128)}, f32[56,128,128]{2,1,0:T(8,128)}) custom-call(s32[56]{0:T(128)} %a_place.1, s32[56]{0:T(128)} %b_place.1, f32[128,2,128,128]{3,2,1,0:T(8,128)} %all_to_all.5.arrived), custom_call_target="tpu_custom_call" | custom-call | bytes 14680064 | tf_op jit(solution)/shard_map/compact/pallas_call | solution.py:92
  211.8 1.3 collective-permute-start.2
  213.1 5.8 %collective-permute-start.1 = (f32[56,128,128]{2,1,0:T(8,128)}, f32[56,128,128]{2,1,0:T(8,128)}, u32[]{:S(2)}, u32[]{:S(2)}) collective-permute-start(f32[56,128,128]{2,1,0:T(8,128)} %get-tuple-element.46.refs_1_), channel_id=1, source_target_pairs={{8,0},{9,1},{10,2},{11,3},{12,4},{13,5},{14,6},{15,7},{16,8},{17,9... | collective-permute-start | bytes 11010056 | tf_op jit(solution)/shard_map/ppermute | solution.py:28
  218.9 0.5 collective-permute-start
  219.4 0.0 copy-start.1
  219.4 0.0 copy-start
  219.4 10.0 %products.5.refs_2_ = f32[64,128,128]{2,1,0:T(8,128)} custom-call(s32[2]{0:T(128)} %pad_add_fusion.flags, s32[4,64]{1,0:T(4,128)} %index_a.11, s32[4,64]{1,0:T(4,128)} %index_b.11, s32[4,64]{1,0:T(4,128)} %index_c.11, f32[56,128,128]{2,1,0:T(8,128)} %get-tuple-element.37.refs_0_, f32[56,128,128]{2,1,0:T(8,128)} %get-tuple-element.46.refs_1_), custom_call_target="tpu_custom_call" | custom-call | flops 805306368000 | bytes 8388608 | tf_op jit(solution)/shard_map/products/pallas_call | solution.py:219
  229.4 0.0 copy-done.1
  229.4 0.6 fusion
  231.2 68.4 %collective-permute-done.refs_0_ = f32[56,128,128]{2,1,0:T(8,128)} collective-permute-done((f32[56,128,128]{2,1,0:T(8,128)}, f32[56,128,128]{2,1,0:T(8,128)}, u32[]{:S(2)}, u32[]{:S(2)}) %collective-permute-start) | collective-permute-done | bytes 3670048 | tf_op jit(solution)/shard_map/ppermute | solution.py:28
  299.6 0.0 collective-permute-done.2.refs_1_.refs_5_
  299.6 0.0 collective-permute-done.1.refs_2_
  299.6 0.0 copy-done
  299.6 1.3 slice_select_fusion.3
  300.9 2.7 broadcast_select_fusion
  303.6 0.1 collective-permute-start.9
  303.7 0.2 collective-permute-start.4
  304.0 3.4 slice_select_fusion
  307.3 1.9 collective-permute-start.8
  309.2 0.2 collective-permute-start.7
  309.4 1.9 collective-permute-start.3
  311.2 15.8 %collective-permute-done.4.refs_0_ = f32[14,128,128]{2,1,0:T(8,128)} collective-permute-done((f32[14,128,128]{2,1,0:T(8,128)S(1)}, f32[14,128,128]{2,1,0:T(8,128)}, u32[]{:S(2)}, u32[]{:S(2)}) %collective-permute-start.4) | collective-permute-done | bytes 917536 | tf_op jit(solution)/shard_map/ppermute | solution.py:28
  327.1 1.3 collective-permute-start.5
  328.4 0.0 collective-permute-done.9.refs_1_
  328.4 0.0 copy-start.2
  328.4 1.8 copy-done.2
  330.2 3.2 collective-permute-start.6
  333.4 10.9 %products.6.refs_3_ = f32[64,128,128]{2,1,0:T(8,128)} custom-call(s32[2]{0:T(128)} %pad_add_fusion.flags, s32[4,64]{1,0:T(4,128)} %index_a.11, s32[4,64]{1,0:T(4,128)} %index_b.11, s32[4,64]{1,0:T(4,128)} %index_c.11, f32[56,128,128]{2,1,0:T(8,128)} %collective-permute-done.refs_0_, f32[56,128,128]{2,1,0:T(8,128)} %copy-done.2, ...), custom_call_target="tpu_custom_call", output_to_operand_aliasing={{}: (6, {})} | custom-call | flops 805306368000 | bytes 8388608 | tf_op jit(solution)/shard_map/products/pallas_call | solution.py:219
  344.3 2.5 collective-permute-done.8.refs_1_
  346.7 1.3 collective-permute-start.11
  348.0 7.6 %products.7.refs_3_ = f32[64,128,128]{2,1,0:T(8,128)} custom-call(s32[2]{0:T(128)} %pad_add_fusion.flags, s32[4,64]{1,0:T(4,128)} %index_a.11, s32[4,64]{1,0:T(4,128)} %index_b.11, s32[4,64]{1,0:T(4,128)} %index_c.11, f32[14,128,128]{2,1,0:T(8,128)} %collective-permute-done.4.refs_0_, ...), custom_call_target="tpu_custom_call", output_to_operand_aliasing={{}: (7, {})} | custom-call | flops 805306368000 | bytes 8388608 | tf_op jit(solution)/shard_map/products/pallas_call | solution.py:219
  355.6 10.8 %collective-permute-done.7.refs_0_ = f32[14,128,128]{2,1,0:T(8,128)} collective-permute-done((f32[14,128,128]{2,1,0:T(8,128)}, f32[14,128,128]{2,1,0:T(8,128)}, u32[]{:S(2)}, u32[]{:S(2)}) %collective-permute-start.7) | collective-permute-done | bytes 917536 | tf_op jit(solution)/shard_map/ppermute | solution.py:28
  366.4 1.3 collective-permute-start.12
  367.7 0.0 collective-permute-done.5.refs_0_
  367.7 4.5 %collective-permute-done.6.refs_2_.refs_6_ = f32[56,128,128]{2,1,0:T(8,128)} collective-permute-done((f32[56,128,128]{2,1,0:T(8,128)}, f32[56,128,128]{2,1,0:T(8,128)}, u32[]{:S(2)}, u32[]{:S(2)}) %collective-permute-start.6) | collective-permute-done | bytes 3670048 | tf_op jit(solution)/shard_map/ppermute | solution.py:28
  372.2 7.5 %products.8.refs_7_ = f32[64,128,128]{2,1,0:T(8,128)} custom-call(s32[2]{0:T(128)} %pad_add_fusion.flags, s32[4,64]{1,0:T(4,128)} %index_a.11, s32[4,64]{1,0:T(4,128)} %index_b.11, s32[4,64]{1,0:T(4,128)} %index_c.11, f32[14,128,128]{2,1,0:T(8,128)} %collective-permute-done.5.refs_0_, ...), custom_call_target="tpu_custom_call", output_to_operand_aliasing={{}: (7, {})} | custom-call | flops 805306368000 | bytes 8388608 | tf_op jit(solution)/shard_map/products/pallas_call | solution.py:219
  379.7 5.9 %collective-permute-done.3.refs_1_ = f32[14,128,128]{2,1,0:T(8,128)} collective-permute-done((f32[14,128,128]{2,1,0:T(8,128)}, f32[14,128,128]{2,1,0:T(8,128)}, u32[]{:S(2)}, u32[]{:S(2)}) %collective-permute-start.3) | collective-permute-done | bytes 917536 | tf_op jit(solution)/shard_map/ppermute | solution.py:28
  385.6 1.3 collective-permute-start.10
  386.9 1.2 collective-permute-done.12.refs_4_
  388.1 0.0 collective-permute-done.11.refs_3_
  388.1 10.0 %products.9.refs_3_ = f32[64,128,128]{2,1,0:T(8,128)} custom-call(s32[2]{0:T(128)} %pad_add_fusion.flags, s32[4,64]{1,0:T(4,128)} %index_a.11, s32[4,64]{1,0:T(4,128)} %index_b.11, s32[4,64]{1,0:T(4,128)} %index_c.11, f32[14,128,128]{2,1,0:T(8,128)} %collective-permute-done.7.refs_0_, ...), custom_call_target="tpu_custom_call", output_to_operand_aliasing={{}: (11, {})} | custom-call | flops 805306368000 | bytes 8388608 | tf_op jit(solution)/shard_map/products/pallas_call | solution.py:219
  398.1 9.7 %collective-permute-done.10.refs_0_ = f32[14,128,128]{2,1,0:T(8,128)} collective-permute-done((f32[14,128,128]{2,1,0:T(8,128)}, f32[14,128,128]{2,1,0:T(8,128)}, u32[]{:S(2)}, u32[]{:S(2)}) %collective-permute-start.10) | collective-permute-done | bytes 917536 | tf_op jit(solution)/shard_map/ppermute | solution.py:28
  407.8 5.0 %last_products.1 = f32[64,128,128]{2,1,0:T(8,128)} custom-call(s32[2]{0:T(128)} %pad_add_fusion.flags, s32[4,64]{1,0:T(4,128)} %index_a.11, s32[4,64]{1,0:T(4,128)} %index_b.11, s32[4,64]{1,0:T(4,128)} %index_c.11, f32[14,128,128]{2,1,0:T(8,128)} %collective-permute-done.10.refs_0_, ...), custom_call_target="tpu_custom_call", output_to_operand_aliasing={{}: (7, {})} | custom-call | flops 805306368000 | bytes 8388608 | tf_op jit(solution)/shard_map/last_products/pallas_call | solution.py:317
Async XLA Ops:
  211.8 87.8 %collective-permute-start.2 = (f32[56,128,128]{2,1,0:T(8,128)}, f32[56,128,128]{2,1,0:T(8,128)}, u32[]{:S(2)}, u32[]{:S(2)}) collective-permute-start(f32[56,128,128]{2,1,0:T(8,128)} %get-tuple-element.46.refs_1_), channel_id=1, source_target_pairs={{24,0},{25,1},{26,2},{27,3},{28,4},{29,5},{30,6},{31,7},{40,16},{4... | collective-permute-start | bytes 11010056 | tf_op jit(solution)/shard_map/ppermute | solution.py:28
  213.1 86.5 %collective-permute-start.1 = (f32[56,128,128]{2,1,0:T(8,128)}, f32[56,128,128]{2,1,0:T(8,128)}, u32[]{:S(2)}, u32[]{:S(2)}) collective-permute-start(f32[56,128,128]{2,1,0:T(8,128)} %get-tuple-element.46.refs_1_), channel_id=1, source_target_pairs={{8,0},{9,1},{10,2},{11,3},{12,4},{13,5},{14,6},{15,7},{16,8},{17,9... | collective-permute-start | bytes 11010056 | tf_op jit(solution)/shard_map/ppermute | solution.py:28
  218.9 80.7 %collective-permute-start = (f32[56,128,128]{2,1,0:T(8,128)}, f32[56,128,128]{2,1,0:T(8,128)}, u32[]{:S(2)}, u32[]{:S(2)}) collective-permute-start(f32[56,128,128]{2,1,0:T(8,128)} %get-tuple-element.37.refs_0_), channel_id=1, source_target_pairs={{2,0},{3,1},{4,2},{5,3},{6,4},{7,5},{0,6},{1,7},{10,8},{11,9},{12,... | collective-permute-start | bytes 11010056 | tf_op jit(solution)/shard_map/ppermute | solution.py:28
  219.4 10.0 %copy-start.1 = (s32[2]{0:T(128)S(1)}, s32[2]{0:T(128)}, u32[]{:S(2)}) copy-start(s32[2]{0:T(128)} %pad_add_fusion.flags) | copy-start | bytes 28
  219.4 80.2 %copy-start = (f32[56,128,128]{2,1,0:T(8,128)S(1)}, f32[56,128,128]{2,1,0:T(8,128)}, u32[]{:S(2)}) copy-start(f32[56,128,128]{2,1,0:T(8,128)} %get-tuple-element.37.refs_0_) | copy-start | bytes 11010052
  303.6 24.7 %collective-permute-start.9 = (f32[56,128,128]{2,1,0:T(8,128)S(1)}, f32[56,128,128]{2,1,0:T(8,128)S(1)}, u32[]{:S(2)}, u32[]{:S(2)}) collective-permute-start(f32[56,128,128]{2,1,0:T(8,128)S(1)} %broadcast_select_fusion), channel_id=1, source_target_pairs={{8,0},{9,1},{10,2},{11,3},{12,4},{13,5},{14,6},{15,7},{0,8},{1,9},... | collective-permute-start | bytes 11010056 | tf_op jit(solution)/shard_map/ppermute | solution.py:28
  303.7 23.3 %collective-permute-start.4 = (f32[14,128,128]{2,1,0:T(8,128)S(1)}, f32[14,128,128]{2,1,0:T(8,128)}, u32[]{:S(2)}, u32[]{:S(2)}) collective-permute-start(f32[14,128,128]{2,1,0:T(8,128)S(1)} %slice_select_fusion.3), channel_id=1, source_target_pairs={{1,0},{0,1},{3,2},{2,3},{5,4},{4,5},{7,6},{6,7},{9,8},{8,9},{11,10... | collective-permute-start | bytes 2752520 | tf_op jit(solution)/shard_map/ppermute | solution.py:28
  307.3 39.4 %collective-permute-start.8 = (f32[14,128,128]{2,1,0:T(8,128)}, f32[14,128,128]{2,1,0:T(8,128)}, u32[]{:S(2)}, u32[]{:S(2)}) collective-permute-start(f32[14,128,128]{2,1,0:T(8,128)} %get-tuple-element.55), channel_id=1, source_target_pairs={{1,0},{0,1},{3,2},{2,3},{5,4},{4,5},{7,6},{6,7},{9,8},{8,9},{11,10... | collective-permute-start | bytes 2752520 | tf_op jit(solution)/shard_map/ppermute | solution.py:28
  309.2 57.2 %collective-permute-start.7 = (f32[14,128,128]{2,1,0:T(8,128)}, f32[14,128,128]{2,1,0:T(8,128)}, u32[]{:S(2)}, u32[]{:S(2)}) collective-permute-start(f32[14,128,128]{2,1,0:T(8,128)} %get-tuple-element.56), channel_id=1, source_target_pairs={{1,0},{0,1},{3,2},{2,3},{5,4},{4,5},{7,6},{6,7},{9,8},{8,9},{11,10... | collective-permute-start | bytes 2752520 | tf_op jit(solution)/shard_map/ppermute | solution.py:28
  309.4 76.2 %collective-permute-start.3 = (f32[14,128,128]{2,1,0:T(8,128)}, f32[14,128,128]{2,1,0:T(8,128)}, u32[]{:S(2)}, u32[]{:S(2)}) collective-permute-start(f32[14,128,128]{2,1,0:T(8,128)} %get-tuple-element.57), channel_id=1, source_target_pairs={{1,0},{0,1},{3,2},{2,3},{5,4},{4,5},{7,6},{6,7},{9,8},{8,9},{11,10... | collective-permute-start | bytes 2752520 | tf_op jit(solution)/shard_map/ppermute | solution.py:28
  327.1 40.6 %collective-permute-start.5 = (f32[14,128,128]{2,1,0:T(8,128)}, f32[14,128,128]{2,1,0:T(8,128)}, u32[]{:S(2)}, u32[]{:S(2)}) collective-permute-start(f32[14,128,128]{2,1,0:T(8,128)} %collective-permute-done.4.refs_0_), channel_id=1, source_target_pairs={{2,0},{3,1},{4,2},{5,3},{6,4},{7,5},{0,6},{1,7},{10,8},{11,9},{12,... | collective-permute-start | bytes 2752520 | tf_op jit(solution)/shard_map/ppermute | solution.py:28
  328.4 1.8 copy-start.2
  330.2 42.0 %collective-permute-start.6 = (f32[56,128,128]{2,1,0:T(8,128)}, f32[56,128,128]{2,1,0:T(8,128)}, u32[]{:S(2)}, u32[]{:S(2)}) collective-permute-start(f32[56,128,128]{2,1,0:T(8,128)} %get-tuple-element.46.refs_1_), channel_id=1, source_target_pairs={{32,8},{33,9},{34,10},{35,11},{36,12},{37,13},{38,14},{39,15},{48,... | collective-permute-start | bytes 11010056 | tf_op jit(solution)/shard_map/ppermute | solution.py:28
  346.7 41.4 %collective-permute-start.11 = (f32[14,128,128]{2,1,0:T(8,128)}, f32[14,128,128]{2,1,0:T(8,128)}, u32[]{:S(2)}, u32[]{:S(2)}) collective-permute-start(f32[14,128,128]{2,1,0:T(8,128)} %collective-permute-done.8.refs_1_), channel_id=1, source_target_pairs={{2,0},{3,1},{4,2},{5,3},{6,4},{7,5},{0,6},{1,7},{10,8},{11,9},{12,... | collective-permute-start | bytes 2752520 | tf_op jit(solution)/shard_map/ppermute | solution.py:28
  366.4 21.7 %collective-permute-start.12 = (f32[14,128,128]{2,1,0:T(8,128)}, f32[14,128,128]{2,1,0:T(8,128)}, u32[]{:S(2)}, u32[]{:S(2)}) collective-permute-start(f32[14,128,128]{2,1,0:T(8,128)} %collective-permute-done.7.refs_0_), channel_id=1, source_target_pairs={{2,0},{3,1},{4,2},{5,3},{6,4},{7,5},{0,6},{1,7},{10,8},{11,9},{12,... | collective-permute-start | bytes 2752520 | tf_op jit(solution)/shard_map/ppermute | solution.py:28
  385.6 22.2 %collective-permute-start.10 = (f32[14,128,128]{2,1,0:T(8,128)}, f32[14,128,128]{2,1,0:T(8,128)}, u32[]{:S(2)}, u32[]{:S(2)}) collective-permute-start(f32[14,128,128]{2,1,0:T(8,128)} %collective-permute-done.3.refs_1_), channel_id=1, source_target_pairs={{2,0},{3,1},{4,2},{5,3},{6,4},{7,5},{0,6},{1,7},{10,8},{11,9},{12,... | collective-permute-start | bytes 2752520 | tf_op jit(solution)/shard_map/ppermute | solution.py:28

commit v4 on v3

v4 whole, which is shorter than its diff:
```python
import functools

import jax
import jax.numpy as jnp
from jax import lax
from jax.experimental import pallas as pl
from jax.experimental.pallas import tpu as pltpu
from jax.sharding import PartitionSpec as P

CBLK = 64
AHEAD = 3
SIZES = (20, 20, 16)
GROUP = 4
VMEM_LIMIT = 60 * 1024 * 1024

ANY = pl.BlockSpec(memory_space=pl.ANY)
HBM = pl.BlockSpec(memory_space=pltpu.HBM)
SMEM = pl.BlockSpec(memory_space=pltpu.SMEM)


def permute(array, mapping):
    rows, cols = lax.axis_size("row"), lax.axis_size("col")
    pairs = []
    for r in range(rows):
        for c in range(cols):
            source = mapping(r, c)
            if source is not None:
                pairs.append(((source[0] % rows) * cols + source[1] % cols, r * cols + c))
    return lax.ppermute(array, ("row", "col"), pairs)


def fill_kernel(cols, a_pick, b_pick, near_a, near_b, near_c, flags, a_blocks, b_blocks, out, a_ref, b_ref, sem):
    panel = a_blocks.shape[0]
    half = a_blocks.shape[1] // 2
    load_a = pltpu.make_async_copy(a_blocks, a_ref, sem.at[0])
    load_b = pltpu.make_async_copy(b_blocks, b_ref, sem.at[1])
    load_a.start()
    load_b.start()
    upper, lower = pl.ds(0, half), pl.ds(half, half)

    def fill_a(q, carry):
        p = a_pick[q]
        col = lax.rem(q, cols)
        behind = q - col + lax.rem(col + cols - AHEAD, cols)

        @pl.when(p < panel)
        def _():
            pltpu.make_async_copy(a_ref.at[p, upper], out.at[q, 0, upper], sem.at[2]).start()
            pltpu.make_async_copy(a_ref.at[p, lower], out.at[behind, 0, lower], sem.at[2]).start()

        return carry

    def fill_b(q, carry):
        p = b_pick[q]

        @pl.when(p < panel)
        def _():
            pltpu.make_async_copy(b_ref.at[p], out.at[q, 1], sem.at[3]).start()

        return carry

    load_a.wait()
    lax.fori_loop(0, a_pick.shape[0], fill_a, 0)
    load_b.wait()
    lax.fori_loop(0, b_pick.shape[0], fill_b, 0)
    pltpu.make_async_copy(a_blocks, a_ref, sem.at[2]).wait()
    pltpu.make_async_copy(b_blocks, b_ref, sem.at[3]).wait()


def fill(cols, a_pick, b_pick, small, a_blocks, b_blocks):
    slots = a_pick.shape[0]
    panel, width, _ = a_blocks.shape
    return pl.pallas_call(
        functools.partial(fill_kernel, cols),
        out_shape=jax.ShapeDtypeStruct((slots, 2, width, width), jnp.float32),
        in_specs=[SMEM] * 6 + [HBM, HBM],
        out_specs=HBM,
        scratch_shapes=[
            pltpu.VMEM((panel, width, width), jnp.float32),
            pltpu.VMEM((panel, width, width), jnp.float32),
            pltpu.SemaphoreType.DMA((4,)),
        ],
        compiler_params=pltpu.CompilerParams(vmem_limit_bytes=VMEM_LIMIT),
        cost_estimate=pl.CostEstimate(flops=0, bytes_accessed=16 * a_blocks.size, transcendentals=0),
        name="fill",
    )(a_pick, b_pick, *small, a_blocks, b_blocks)


def compact_kernel(a_place, far_place, b_place, arrived, up_out, low_out, b_out, up_ref, low_ref, b_ref, in_sem, out_sem):
    half = up_out.shape[1]
    sides = [
        (a_place, 0, pl.ds(0, half), up_ref, up_out),
        (far_place, 0, pl.ds(half, half), low_ref, low_out),
        (b_place, 1, pl.ds(0, 2 * half), b_ref, b_out),
    ]
    for n, (place, side, rows, held, out) in enumerate(sides):

        def body(j, carry, n=n, place=place, side=side, rows=rows, held=held):
            pltpu.make_async_copy(arrived.at[place[j], side, rows], held.at[j], in_sem.at[n]).start()
            return carry

        lax.fori_loop(0, place.shape[0], body, 0, unroll=4)
    for n, (place, side, rows, held, out) in enumerate(sides):
        pltpu.make_async_copy(held, held, in_sem.at[n]).wait()
        pltpu.make_async_copy(held, out, out_sem.at[n]).start()
    for n, (place, side, rows, held, out) in enumerate(sides):
        pltpu.make_async_copy(held, out, out_sem.at[n]).wait()


def compact(a_place, far_place, b_place, arrived):
    panel = a_place.shape[0]
    width = arrived.shape[-1]
    shapes = [(panel, width // 2, width), (panel, width // 2, width), (panel, width, width)]
    return pl.pallas_call(
        compact_kernel,
        out_shape=[jax.ShapeDtypeStruct(shape, jnp.float32) for shape in shapes],
        in_specs=[SMEM, SMEM, SMEM, HBM],
        out_specs=[HBM] * 3,
        scratch_shapes=[pltpu.VMEM(shape, jnp.float32) for shape in shapes]
        + [pltpu.SemaphoreType.DMA((3,)), pltpu.SemaphoreType.DMA((3,))],
        compiler_params=pltpu.CompilerParams(vmem_limit_bytes=VMEM_LIMIT),
        cost_estimate=pl.CostEstimate(flops=0, bytes_accessed=16 * panel * width * width, transcendentals=0),
        name="compact",
    )(a_place, far_place, b_place, arrived)


def split(value):
    high = value.astype(jnp.bfloat16)
    low = (value - high.astype(jnp.float32)).astype(jnp.bfloat16)
    return high, low


def block_product(left, right):
    lh, ll = split(left)
    rh, rl = split(right)
    both = jnp.dot(
        jnp.concatenate([lh, ll], axis=1),
        jnp.concatenate([rh, rh], axis=0),
        preferred_element_type=jnp.float32,
    )
    return both + jnp.dot(lh, rl, preferred_element_type=jnp.float32)


def rows_of(ref, spec):
    if spec is None:
        return ref
    if len(spec) == 3:
        return ref.at[spec[0], pl.ds(spec[1], spec[2])]
    return ref.at[pl.ds(spec[0], spec[1])]


def products_kernel(jobs, has_c, flags, index_a, index_b, index_c, *refs):
    refs, scratch = refs[: len(refs) - len(jobs) * 2 - 3], refs[len(refs) - len(jobs) * 2 - 3 :]
    held = [(scratch[2 * n], scratch[2 * n + 1]) for n in range(len(jobs))]
    c_ref, live, sem = scratch[2 * len(jobs) :]
    c_out = refs[-1]
    blocks = c_out.shape[0]
    entries = index_a.shape[1]
    half = c_ref.shape[1] // 2

    if has_c:
        load_c = pltpu.make_async_copy(refs[-2], c_ref, sem.at[len(jobs), 0])
        load_c.start()
    waits = []
    for n, (_, _, _, upper, lower, b) in enumerate(jobs):
        a_ref, b_ref = held[n]
        copies = [
            pltpu.make_async_copy(rows_of(refs[upper[0]], upper[1]), a_ref.at[:, pl.ds(0, half)], sem.at[n, 0]),
            pltpu.make_async_copy(rows_of(refs[lower[0]], lower[1]), a_ref.at[:, pl.ds(half, half)], sem.at[n, 1]),
        ]
        for copy in copies:
            copy.start()
        for k, source in enumerate(b):
            copy = pltpu.make_async_copy(refs[source], b_ref, sem.at[n, 2])
            if len(b) == 1:
                copy.start()
            else:
                pl.when(flags[0] == k)(copy.start)
        waits.append([*copies, copy])

    counts = []
    for n, (t, first, size, _, _, _) in enumerate(jobs):

        def listing(e, count, n=n, t=t, first=first, size=size):
            live[n, count] = e
            slot = index_a[t, e]
            used = (index_c[t, e] < blocks) & (slot >= first) & (slot < first + size)
            return count + jnp.where(used, 1, 0)

        counts.append(lax.fori_loop(0, entries, listing, 0, unroll=4))
    if has_c:
        load_c.wait()
    else:
        c_ref[...] = jnp.zeros_like(c_ref)

    for n, (t, first, _, _, _, _) in enumerate(jobs):
        a_ref, b_ref = held[n]
        for copy in waits[n]:
            copy.wait()

        def add(at, n=n, t=t, first=first, a_ref=a_ref, b_ref=b_ref):
            e = live[n, at]
            c_ref[index_c[t, e]] += block_product(a_ref[index_a[t, e] - first], b_ref[index_b[t, e]])

        def several(g, carry, add=add):
            for u in range(GROUP):
                add(g * GROUP + u)
            return carry

        def single(at, carry, add=add):
            add(at)
            return carry

        groups = counts[n] // GROUP
        lax.fori_loop(0, groups, several, 0)
        lax.fori_loop(groups * GROUP, counts[n], single, 0)
    out = pltpu.make_async_copy(c_ref, c_out, sem.at[len(jobs), 0])
    out.start()
    out.wait()


def products(flags, prods, jobs, total):
    entries = prods[0].shape[1]
    width = jobs[0][5][0].shape[1]
    has_c = total is not None
    arrays = []

    def number(array):
        for n, known in enumerate(arrays):
            if known is array:
                return n
        arrays.append(array)
        return len(arrays) - 1

    static = []
    scratch = []
    for t, first, size, upper, lower, b in jobs:
        static.append((t, first, size, (number(upper[0]), upper[1]), (number(lower[0]), lower[1]), tuple(number(x) for x in b)))
        scratch.append(pltpu.VMEM((size, width, width), jnp.float32))
        scratch.append(pltpu.VMEM(b[0].shape, jnp.float32))
    operands = [flags, *prods, *arrays]
    aliases = {}
    if has_c:
        aliases = {len(operands): 0}
        operands.append(total)
    return pl.pallas_call(
        functools.partial(products_kernel, tuple(static), has_c),
        out_shape=jax.ShapeDtypeStruct((CBLK, width, width), jnp.float32),
        in_specs=[SMEM] * 4 + [ANY] * (len(operands) - 4),
        out_specs=ANY,
        scratch_shapes=scratch
        + [
            pltpu.VMEM((CBLK, width, width), jnp.float32),
            pltpu.SMEM((len(jobs), entries + 1), jnp.int32),
            pltpu.SemaphoreType.DMA((len(jobs) + 1, 3)),
        ],
        input_output_aliases=aliases,
        compiler_params=pltpu.CompilerParams(vmem_limit_bytes=VMEM_LIMIT),
        cost_estimate=pl.CostEstimate(
            flops=6000 * entries * width**3, bytes_accessed=8 * CBLK * width * width, transcendentals=0
        ),
        name="products",
    )(*operands)


def last_kernel(jobs, flags, index_a, index_b, index_c, *refs):
    c_in, c_out, a_ref, b_ref, c_ref, live, place, sem = refs[len(refs) - 8 :]
    blocks = c_out.shape[0]
    entries = index_a.shape[1]
    half = c_ref.shape[1] // 2
    room = len(jobs) * entries

    def clear(m, carry):
        place[m] = -1
        return carry

    lax.fori_loop(0, blocks, clear, 0, unroll=8)

    counts = (0, 0)
    for t, first, size, upper, lower, b in jobs:

        def fetch(e, counts, t=t, first=first, size=size, upper=upper, lower=lower, b=b):
            slot, m = index_a[t, e] - first, index_c[t, e]
            used = (m < blocks) & (slot >= 0) & (slot < size)
            count, kept = counts
            new = used & (place[jnp.minimum(m, blocks - 1)] < 0)

            @pl.when(used)
            def _():
                live[count] = m
                for part, (n, spec) in enumerate((upper, lower)):
                    source = rows_of(refs[n], spec).at[slot]
                    target = a_ref.at[count, pl.ds(part * half, half)]
                    pltpu.make_async_copy(source, target, sem.at[0]).start()
                for k, n in enumerate(b):
                    copy = pltpu.make_async_copy(refs[n].at[index_b[t, e]], b_ref.at[count], sem.at[0])
                    if len(b) == 1:
                        copy.start()
                    else:
                        pl.when(flags[0] == k)(copy.start)

            @pl.when(new)
            def _():
                place[m] = kept
                live[room + kept] = m
                pltpu.make_async_copy(c_in.at[m], c_ref.at[kept], sem.at[0]).start()

            return count + jnp.where(used, 1, 0), kept + jnp.where(new, 1, 0)

        counts = lax.fori_loop(0, entries, fetch, counts)
    count, kept = counts

    def arrive(_, carry):
        pltpu.make_async_copy(c_in.at[0], c_ref.at[0], sem.at[0]).wait()
        return carry

    lax.fori_loop(0, 2 * count + kept, arrive, 0)

    def add(at):
        c_ref[place[live[at]]] += block_product(a_ref[at], b_ref[at])

    def several(g, carry):
        for u in range(GROUP):
            add(g * GROUP + u)
        return carry

    def single(at, carry):
        add(at)
        return carry

    groups = count // GROUP
    lax.fori_loop(0, groups, several, 0)
    lax.fori_loop(groups * GROUP, count, single, 0)

    def store(k, carry):
        pltpu.make_async_copy(c_ref.at[k], c_out.at[live[room + k]], sem.at[1]).start()
        return carry

    lax.fori_loop(0, kept, store, 0)

    def leave(_, carry):
        pltpu.make_async_copy(c_ref.at[0], c_out.at[0], sem.at[1]).wait()
        return carry

    lax.fori_loop(0, kept, leave, 0)


def last_products(flags, prods, jobs, total):
    entries = prods[0].shape[1]
    block = total.shape[1:]
    arrays = []
    static = []
    for t, first, size, upper, lower, b in jobs:
        n = len(arrays)
        arrays += [upper[0], lower[0], *b]
        static.append((t, first, size, (n, upper[1]), (n + 1, lower[1]), tuple(range(n + 2, len(arrays)))))
    operands = [flags, *prods, *arrays, total]
    room = len(jobs) * entries
    return pl.pallas_call(
        functools.partial(last_kernel, tuple(static)),
        out_shape=jax.ShapeDtypeStruct(total.shape, jnp.float32),
        in_specs=[SMEM] * 4 + [ANY] * (len(operands) - 4),
        out_specs=ANY,
        scratch_shapes=[
            pltpu.VMEM((room, *block), jnp.float32),
            pltpu.VMEM((room, *block), jnp.float32),
            pltpu.VMEM((total.shape[0], *block), jnp.float32),
            pltpu.SMEM((room + total.shape[0],), jnp.int32),
            pltpu.SMEM((total.shape[0],), jnp.int32),
            pltpu.SemaphoreType.DMA((2,)),
        ],
        input_output_aliases={len(operands) - 1: 0},
        compiler_params=pltpu.CompilerParams(vmem_limit_bytes=VMEM_LIMIT),
        cost_estimate=pl.CostEstimate(
            flops=6000 * entries * block[0] ** 3, bytes_accessed=8 * total.size, transcendentals=0
        ),
        name="last_products",
    )(*operands)


def together(*values):
    return lax.optimization_barrier(values)


def local(a_blocks, a_pick, a_place, b_blocks, b_pick, b_place, prod_a, prod_b, prod_c):
    flags = jnp.stack([lax.axis_index("row") % 2, lax.axis_index("col") % 2]).astype(jnp.int32)
    prods = (prod_a, prod_b, prod_c)
    far_place = permute(a_place, lambda r, c: (r, c + AHEAD))
    outgoing = fill(lax.axis_size("col"), a_pick, b_pick, (*prods, flags), a_blocks, b_blocks)
    outgoing, far_place, flags = together(outgoing, far_place, flags)
    arrived = lax.all_to_all(outgoing, ("row", "col"), split_axis=0, concat_axis=0, tiled=True)
    up0, low3, b0 = compact(a_place, far_place, b_place, arrived)
    up0, low3, b0, flags = together(up0, low3, b0, flags)
    core1, odd = flags[0] == 1, flags[1] == 1

    up2 = permute(up0, lambda r, c: (r, c + 2))
    low1 = permute(low3, lambda r, c: (r, c - 2))
    b2 = permute(b0, lambda r, c: (r + 2, c))
    near0 = permute(b0, lambda r, c: (r ^ 1, c))
    firsts = [sum(SIZES[:i]) for i in range(len(SIZES))]
    last = len(SIZES) - 1
    cross = []
    for first, size in zip(firsts, SIZES):
        rows = slice(first, first + size)
        cross.append((jnp.where(odd, up0[rows], up2[rows]), jnp.where(odd, low1[rows], low3[rows])))
    cross = [jnp.stack(pair) for pair in cross[:last]] + [*cross[last]]
    *cross, b0, b2, near0 = together(*cross, b0, b2, near0)

    def over(part):
        return permute(part, lambda r, c: (r, c ^ 1))

    mid = [over(part) for part in cross[:last]]
    cross[last], cross[last + 1], mid[0] = together(cross[last], cross[last + 1], mid[0])
    mid += [over(cross[last]), over(cross[last + 1])]
    near2 = permute(b2, lambda r, c: (r ^ 1, c))
    far3 = permute(b0, lambda r, c: (r + 3, c) if r % 2 else None)
    b1, b3 = [near0, near2], [near2, far3]
    ends = []

    def onward(up1, low2):
        up3 = permute(up1, lambda r, c: (r, c + 2))
        low0 = permute(low2, lambda r, c: (r, c - 2))
        ends.append((up3, low0))

    def middle(i, up1, low2):
        first, size = firsts[i], SIZES[i]
        part = (first, size)
        return [(1, first, size, up1, (low1, part), b1), (2, first, size, (up2, part), low2, [b2])]

    def outer(i):
        first, size = firsts[i], SIZES[i]
        part = (first, size)
        return [
            (0, first, size, (up0, part), (ends[i][1], None), [b0]),
            (3, first, size, (ends[i][0], None), (low3, part), b3),
        ]

    total = None
    jobs = []
    for i in range(last):
        if i > 0:
            mid[i], total = together(mid[i], total)
        onward(mid[i][0], mid[i][1])
        size = SIZES[i]
        jobs = middle(i, (mid[i], (0, 0, size)), (mid[i], (1, 0, size))) + jobs
        total = products(flags, prods, jobs, total)
        jobs = outer(i)
    mid[last], mid[last + 1], total = together(mid[last], mid[last + 1], total)
    onward(mid[last], mid[last + 1])
    jobs = middle(last, (mid[last], None), (mid[last + 1], None)) + jobs
    total = products(flags, prods, jobs, total)
    return last_products(flags, prods, outer(last), total)


def solution(mesh):
    placed = (
        P(("row", "col"), None, None),
        P(("row", "col")),
        P(("row", "col")),
        P(("row", "col"), None, None),
        P(("row", "col")),
        P(("row", "col")),
        P(None, ("row", "col")),
        P(None, ("row", "col")),
        P(None, ("row", "col")),
    )
    return jax.shard_map(
        local, mesh=mesh, in_specs=placed, out_specs=P(("row", "col"), None, None), check_vma=False
    )
```

time: 413 us -> 404 us (0.978)
  Pallas kernels: 63 us -> 53.3 us
  waiting for transfers between devices: 119 us -> 111 us
  starting transfers between devices: 20.2 us -> 27.9 us
  local copies, waits for them, and re-layouts: 2.46 us -> 6.6 us
    pallas_call x5 -> x3, Pallas kernels: 45.9 us -> 32.2 us  [products(): pl.pallas_call(functools.partial(products_kernel, tuple(static), has_c),...]
    ppermute x13 -> x17, waiting for transfers between devices: 119 us -> 111 us  [permute(): return lax.ppermute(array, ('row', 'col'), pairs)]
    ppermute x13 -> x17, starting transfers between devices: 20.2 us -> 27.9 us  [permute(): return lax.ppermute(array, ('row', 'col'), pairs)]
    select_n x3 -> x2, other arithmetic: 7.4 us -> 2.78 us  [the longest x1 1.9 us: local(): jnp.where(odd, low1[rows], low3[rows])]
  transfers between devices with their start and end apart: 13 -> 17, of which waited for: 8 -> 6; matrix products, arithmetic and copies ran while one was open for 1% -> 3% of each run, Pallas kernels for 11% -> 9%
where the time goes in v4:
time: 404 us; the launch traced here: 403 us
  blocking collectives  197 us (49%)
  waiting for transfers between devices  111 us (27%)
  Pallas kernels  53.3 us (13%)
  starting transfers between devices  27.9 us (7%)
  other arithmetic  7.27 us (2%)
  local copies, waits for them, and re-layouts  6.6 us (2%)
    all_to_all x1, blocking collectives, local(): lax.all_to_all(outgoing, ('row', 'col'), split_axis=0, concat_axis=0, til...  197 us
    ppermute x17, waiting for transfers between devices, permute(): return lax.ppermute(array, ('row', 'col'), pairs)  111 us
    pallas_call x3, Pallas kernels, products(): pl.pallas_call(functools.partial(products_kernel, tuple(static), has_c),...  32.2 us
    ppermute x17, starting transfers between devices, permute(): return lax.ppermute(array, ('row', 'col'), pairs)  27.9 us
  transfers between devices with their start and end apart: 17, of which 6 were waited for; matrix products, arithmetic and copies ran while one was open for 3% of the time, Pallas kernels for 9%

profile of v4, /device:TPU:0, one launch (start us, length us, event | category | flops | bytes accessed | tf_op | source)
XLA Modules:
  0.0 403.4 jit_solution(13177964947149248761)
XLA Ops:
  0.0 4.1 %collective-permute-start = (s32[56]{0:T(128)}, s32[56]{0:T(128)S(1)}, u32[]{:S(2)}, u32[]{:S(2)}) collective-permute-start(s32[56]{0:T(128)} %a_place.1), channel_id=1, source_target_pairs={{3,0},{4,1},{5,2},{6,3},{7,4},{0,5},{1,6},{2,7},{11,8},{12,9},{13,... | collective-permute-start | bytes 680 | tf_op jit(solution)/shard_map/ppermute | solution.py:29
  4.1 0.7 pad_add_fusion.flags
  4.8 6.0 %fill.1 = f32[128,2,128,128]{3,2,1,0:T(8,128)} custom-call(s32[128]{0:T(128)} %a_pick.1, s32[128]{0:T(128)} %b_pick.1, s32[4,64]{1,0:T(4,128)} %index_a.7, s32[4,64]{1,0:T(4,128)} %index_b.7, s32[4,64]{1,0:T(4,128)} %index_c.7, s32[2]{0:T(128)} %pad_add_fusion.flags, f32[56,128,128]{2,1,0:T(8,128)} %a_blocks.1, f32[56,128,128]{2,1,0:T(8,128)} %b_blocks.1), custom_call_target="tpu_custom_call" | custom-call | bytes 14680064 | tf_op jit(solution)/shard_map/fill/pallas_call | solution.py:73
  10.8 0.0 collective-permute-done.far_place
  10.8 0.0 copy-start.5
  10.8 196.6 %all_to_all.5.arrived = f32[128,2,128,128]{3,2,1,0:T(8,128)} all-to-all(f32[128,2,128,128]{3,2,1,0:T(8,128)} %fill.1), channel_id=1, replica_groups=mesh['row'=16,'col'=8] {'row','col'}, dimensions={0} | all-to-all | bytes 33554432 | tf_op jit(solution)/shard_map/all_to_all | solution.py:391
  207.5 7.1 %compact.1 = (f32[56,64,128]{2,1,0:T(8,128)}, f32[56,64,128]{2,1,0:T(8,128)}, f32[56,128,128]{2,1,0:T(8,128)}) custom-call(s32[56]{0:T(128)} %a_place.1, s32[56]{0:T(128)} %copy-done.5, s32[56]{0:T(128)} %b_place.1, f32[128,2,128,128]{3,2,1,0:T(8,128)} %all_to_all.5.arrived), custom_call_target="tpu_custom_call" | custom-call | bytes 14680064 | tf_op jit(solution)/shard_map/compact/pallas_call | solution.py:114
  214.6 0.5 collective-permute-start.3
  215.1 0.1 collective-permute-start.4
  215.2 3.6 collective-permute-start.2
  218.8 0.0 collective-permute-start.1
  218.8 0.6 slice.51
  220.1 39.0 %collective-permute-done.2.refs_1_ = f32[56,64,128]{2,1,0:T(8,128)S(1)} collective-permute-done((f32[56,64,128]{2,1,0:T(8,128)}, f32[56,64,128]{2,1,0:T(8,128)S(1)}, u32[]{:S(2)}, u32[]{:S(2)}) %collective-permute-start.2) | collective-permute-done | bytes 1835040 | tf_op jit(solution)/shard_map/ppermute | solution.py:29
  259.1 2.2 fusion
  261.3 0.0 collective-permute-done.1.refs_4_
  261.3 0.4 copy-done
  261.7 0.2 fusion.1
  261.8 1.5 pad_maximum_fusion
  263.3 0.9 slice_select_fusion.5
  264.2 1.9 slice_select_fusion.4
  266.1 30.4 %collective-permute-done.3.refs_5_.refs_6_ = f32[56,128,128]{2,1,0:T(8,128)S(1)} collective-permute-done((f32[56,128,128]{2,1,0:T(8,128)}, f32[56,128,128]{2,1,0:T(8,128)S(1)}, u32[]{:S(2)}, u32[]{:S(2)}) %collective-permute-start.3) | collective-permute-done | bytes 3670048 | tf_op jit(solution)/shard_map/ppermute | solution.py:29
  296.5 0.0 collective-permute-done.4.refs_2_
  296.5 0.1 collective-permute-start.9
  296.6 1.8 collective-permute-start.5
  298.3 0.3 collective-permute-start.8
  298.7 4.0 collective-permute-start.12
  302.7 25.5 %collective-permute-done.5.refs_0_ = f32[2,20,64,128]{3,2,1,0:T(8,128)S(1)} collective-permute-done((f32[2,20,64,128]{3,2,1,0:T(8,128)S(1)}, f32[2,20,64,128]{3,2,1,0:T(8,128)S(1)}, u32[]{:S(2)}, u32[]{:S(2)}) %collective-permute-start.5) | collective-permute-done | bytes 1310752 | tf_op jit(solution)/shard_map/ppermute | solution.py:29
  328.2 1.7 collective-permute-start.6
  329.9 1.2 slice_bitcast_fusion.2
  331.2 2.0 collective-permute-start.10
  333.2 0.0 collective-permute-done.9.refs_3_.refs_5_
  333.2 1.8 copy-done.8
  335.0 1.2 collective-permute-start.11
  336.2 8.3 %products.3.refs_12_ = f32[64,128,128]{2,1,0:T(8,128)} custom-call(s32[2]{0:T(128)} %pad_add_fusion.flags, s32[4,64]{1,0:T(4,128)} %index_a.7, s32[4,64]{1,0:T(4,128)} %index_b.7, s32[4,64]{1,0:T(4,128)} %index_c.7, f32[2,20,64,128]{3,2,1,0:T(8,128)} %copy-done.3, f32[56,64,128]{2,1,0:T(8,128)} %copy-done.1, f32[56,128,128]{2,1,0:T(8,128)} %copy-done.7, ...), custom_call_target="tpu_custom_call" | custom-call | flops 805306368000 | bytes 8388608 | tf_op jit(solution)/shard_map/products/pallas_call | solution.py:246
  344.5 11.9 %collective-permute-done.8.refs_0_ = f32[2,20,64,128]{3,2,1,0:T(8,128)} collective-permute-done((f32[2,20,64,128]{3,2,1,0:T(8,128)}, f32[2,20,64,128]{3,2,1,0:T(8,128)}, u32[]{:S(2)}, u32[]{:S(2)}) %collective-permute-start.8) | collective-permute-done | bytes 1310752 | tf_op jit(solution)/shard_map/ppermute | solution.py:29
  356.4 1.7 collective-permute-start.7
  358.1 2.6 slice_bitcast_fusion
  360.7 0.0 collective-permute-done.10.refs_7_
  360.7 1.9 collective-permute-start.15
  362.6 1.4 collective-permute-start.16
  363.9 12.0 %products.4.refs_13_ = f32[64,128,128]{2,1,0:T(8,128)} custom-call(s32[2]{0:T(128)} %pad_add_fusion.flags, s32[4,64]{1,0:T(4,128)} %index_a.7, s32[4,64]{1,0:T(4,128)} %index_b.7, s32[4,64]{1,0:T(4,128)} %index_c.7, f32[2,20,64,128]{3,2,1,0:T(8,128)} %collective-permute-done.8.refs_0_, f32[56,64,128]{2,1,0:T(8,128)} %copy-done.1, ...), custom_call_target="tpu_custom_call", output_to_operand_aliasing={{}: (16, {})} | custom-call | flops 805306368000 | bytes 8388608 | tf_op jit(solution)/shard_map/products/pallas_call | solution.py:246
  376.0 2.5 collective-permute-done.7.refs_5_
  378.4 3.5 collective-permute-start.13
  381.9 0.0 collective-permute-done.15.refs_8_
  381.9 0.0 collective-permute-done.16.refs_10_
  381.9 11.9 %products.5.refs_7_ = f32[64,128,128]{2,1,0:T(8,128)} custom-call(s32[2]{0:T(128)} %pad_add_fusion.flags, s32[4,64]{1,0:T(4,128)} %index_a.7, s32[4,64]{1,0:T(4,128)} %index_b.7, s32[4,64]{1,0:T(4,128)} %index_c.7, f32[16,64,128]{2,1,0:T(8,128)} %collective-permute-done.6.refs_0_, f32[56,64,128]{2,1,0:T(8,128)} %copy-done.1, ...), custom_call_target="tpu_custom_call", output_to_operand_aliasing={{}: (17, {})} | custom-call | flops 805306368000 | bytes 8388608 | tf_op jit(solution)/shard_map/products/pallas_call | solution.py:246
  393.8 1.6 collective-permute-done.14.refs_3_
  395.4 7.9 %last_products.1 = f32[64,128,128]{2,1,0:T(8,128)} custom-call(s32[2]{0:T(128)} %pad_add_fusion.flags, s32[4,64]{1,0:T(4,128)} %index_a.7, s32[4,64]{1,0:T(4,128)} %index_b.7, s32[4,64]{1,0:T(4,128)} %index_c.7, f32[56,64,128]{2,1,0:T(8,128)} %get-tuple-element.37.refs_6_.refs_7_.refs_0_, ...), custom_call_target="tpu_custom_call", output_to_operand_aliasing={{}: (11, {})} | custom-call | flops 805306368000 | bytes 8388608 | tf_op jit(solution)/shard_map/last_products/pallas_call | solution.py:359
  (20 shorter events, 0.0 us)
Async XLA Ops:
  0.0 10.8 %collective-permute-start = (s32[56]{0:T(128)}, s32[56]{0:T(128)S(1)}, u32[]{:S(2)}, u32[]{:S(2)}) collective-permute-start(s32[56]{0:T(128)} %a_place.1), channel_id=1, source_target_pairs={{3,0},{4,1},{5,2},{6,3},{7,4},{0,5},{1,6},{2,7},{11,8},{12,9},{13,... | collective-permute-start | bytes 680 | tf_op jit(solution)/shard_map/ppermute | solution.py:29
  10.8 196.6 %copy-start.5 = (s32[56]{0:T(128)}, s32[56]{0:T(128)S(1)}, u32[]{:S(2)}) copy-start(s32[56]{0:T(128)S(1)} %collective-permute-done.far_place) | copy-start | bytes 676
  207.5 11.4 %copy-start.4 = (s32[2]{0:T(128)S(1)}, s32[2]{0:T(128)}, u32[]{:S(2)}) copy-start(s32[2]{0:T(128)} %pad_add_fusion.flags) | copy-start | bytes 28
  214.6 81.9 %collective-permute-start.3 = (f32[56,128,128]{2,1,0:T(8,128)}, f32[56,128,128]{2,1,0:T(8,128)S(1)}, u32[]{:S(2)}, u32[]{:S(2)}) collective-permute-start(f32[56,128,128]{2,1,0:T(8,128)} %get-tuple-element.50.refs_8_.refs_9_.refs_2_), channel_id=1, source_target_pairs={{16,0},{17,1},{18,2},{19,3},{20,4},{21,5},{22,6},{23,7},{24,8},{25... | collective-permute-start | bytes 11010056 | tf_op jit(solution)/shard_map/ppermute | solution.py:29
  215.1 81.4 %collective-permute-start.4 = (f32[56,128,128]{2,1,0:T(8,128)}, f32[56,128,128]{2,1,0:T(8,128)S(1)}, u32[]{:S(2)}, u32[]{:S(2)}) collective-permute-start(f32[56,128,128]{2,1,0:T(8,128)} %get-tuple-element.50.refs_8_.refs_9_.refs_2_), channel_id=1, source_target_pairs={{8,0},{9,1},{10,2},{11,3},{12,4},{13,5},{14,6},{15,7},{0,8},{1,9},... | collective-permute-start | bytes 11010056 | tf_op jit(solution)/shard_map/ppermute | solution.py:29
  215.2 43.9 %collective-permute-start.2 = (f32[56,64,128]{2,1,0:T(8,128)}, f32[56,64,128]{2,1,0:T(8,128)S(1)}, u32[]{:S(2)}, u32[]{:S(2)}) collective-permute-start(f32[56,64,128]{2,1,0:T(8,128)} %get-tuple-element.38.refs_10_.refs_11_.refs_4_), channel_id=1, source_target_pairs={{6,0},{7,1},{0,2},{1,3},{2,4},{3,5},{4,6},{5,7},{14,8},{15,9},{8,1... | collective-permute-start | bytes 5505032 | tf_op jit(solution)/shard_map/ppermute | solution.py:29
  218.8 42.5 %collective-permute-start.1 = (f32[56,64,128]{2,1,0:T(8,128)}, f32[56,64,128]{2,1,0:T(8,128)S(1)}, u32[]{:S(2)}, u32[]{:S(2)}) collective-permute-start(f32[56,64,128]{2,1,0:T(8,128)} %get-tuple-element.37.refs_6_.refs_7_.refs_0_), channel_id=1, source_target_pairs={{2,0},{3,1},{4,2},{5,3},{6,4},{7,5},{0,6},{1,7},{10,8},{11,9},{12,... | collective-permute-start | bytes 5505032 | tf_op jit(solution)/shard_map/ppermute | solution.py:29
  259.1 5.1 %copy-start.1 = (f32[56,64,128]{2,1,0:T(8,128)}, f32[56,64,128]{2,1,0:T(8,128)S(1)}, u32[]{:S(2)}) copy-start(f32[56,64,128]{2,1,0:T(8,128)S(1)} %collective-permute-done.2.refs_1_) | copy-start | bytes 5505028
  259.1 2.6 copy-start
  261.7 1.7 copy-start.2
  296.5 31.8 %copy-start.6 = (f32[56,128,128]{2,1,0:T(8,128)}, f32[56,128,128]{2,1,0:T(8,128)S(1)}, u32[]{:S(2)}) copy-start(f32[56,128,128]{2,1,0:T(8,128)S(1)} %collective-permute-done.3.refs_5_.refs_6_) | copy-start | bytes 11010052
  296.5 36.7 %copy-start.7 = (f32[56,128,128]{2,1,0:T(8,128)}, f32[56,128,128]{2,1,0:T(8,128)S(1)}, u32[]{:S(2)}) copy-start(f32[56,128,128]{2,1,0:T(8,128)S(1)} %collective-permute-done.4.refs_2_) | copy-start | bytes 11010052
  296.5 36.7 %collective-permute-start.9 = (f32[56,128,128]{2,1,0:T(8,128)S(1)}, f32[56,128,128]{2,1,0:T(8,128)S(1)}, u32[]{:S(2)}, u32[]{:S(2)}) collective-permute-start(f32[56,128,128]{2,1,0:T(8,128)S(1)} %collective-permute-done.3.refs_5_.refs_6_), channel_id=1, source_target_pairs={{8,0},{9,1},{10,2},{11,3},{12,4},{13,5},{14,6},{15,7},{0,8},{1,9},... | collective-permute-start | bytes 11010056 | tf_op jit(solution)/shard_map/ppermute | solution.py:29
  296.6 31.7 %collective-permute-start.5 = (f32[2,20,64,128]{3,2,1,0:T(8,128)S(1)}, f32[2,20,64,128]{3,2,1,0:T(8,128)S(1)}, u32[]{:S(2)}, u32[]{:S(2)}) collective-permute-start(f32[2,20,64,128]{3,2,1,0:T(8,128)S(1)} %get-tuple-element.42), channel_id=1, source_target_pairs={{1,0},{0,1},{3,2},{2,3},{5,4},{4,5},{7,6},{6,7},{9,8},{8,9},{11,10... | collective-permute-start | bytes 3932168 | tf_op jit(solution)/shard_map/ppermute | solution.py:29
  298.3 58.1 %collective-permute-start.8 = (f32[2,20,64,128]{3,2,1,0:T(8,128)}, f32[2,20,64,128]{3,2,1,0:T(8,128)}, u32[]{:S(2)}, u32[]{:S(2)}) collective-permute-start(f32[2,20,64,128]{3,2,1,0:T(8,128)} %get-tuple-element.45), channel_id=1, source_target_pairs={{1,0},{0,1},{3,2},{2,3},{5,4},{4,5},{7,6},{6,7},{9,8},{8,9},{11,10... | collective-permute-start | bytes 3932168 | tf_op jit(solution)/shard_map/ppermute | solution.py:29
  298.7 65.3 %collective-permute-start.12 = (f32[56,128,128]{2,1,0:T(8,128)}, f32[56,128,128]{2,1,0:T(8,128)}, u32[]{:S(2)}, u32[]{:S(2)}) collective-permute-start(f32[56,128,128]{2,1,0:T(8,128)} %get-tuple-element.50.refs_8_.refs_9_.refs_2_), channel_id=1, source_target_pairs={{32,8},{33,9},{34,10},{35,11},{36,12},{37,13},{38,14},{39,15},{48,... | collective-permute-start | bytes 11010056 | tf_op jit(solution)/shard_map/ppermute | solution.py:29
  328.2 8.0 %copy-start.3 = (f32[2,20,64,128]{3,2,1,0:T(8,128)}, f32[2,20,64,128]{3,2,1,0:T(8,128)S(1)}, u32[]{:S(2)}) copy-start(f32[2,20,64,128]{3,2,1,0:T(8,128)S(1)} %collective-permute-done.5.refs_0_) | copy-start | bytes 3932164
  328.2 47.7 %collective-permute-start.6 = (f32[16,64,128]{2,1,0:T(8,128)}, f32[16,64,128]{2,1,0:T(8,128)}, u32[]{:S(2)}, u32[]{:S(2)}) collective-permute-start(f32[16,64,128]{2,1,0:T(8,128)} %slice_select_fusion.5), channel_id=1, source_target_pairs={{1,0},{0,1},{3,2},{2,3},{5,4},{4,5},{7,6},{6,7},{9,8},{8,9},{11,10... | collective-permute-start | bytes 1572872 | tf_op jit(solution)/shard_map/ppermute | solution.py:29
  331.2 29.5 %collective-permute-start.10 = (f32[20,64,128]{2,1,0:T(8,128)}, f32[20,64,128]{2,1,0:T(8,128)}, u32[]{:S(2)}, u32[]{:S(2)}) collective-permute-start(f32[20,64,128]{2,1,0:T(8,128)} %get-tuple-element.62), channel_id=1, source_target_pairs={{6,0},{7,1},{0,2},{1,3},{2,4},{3,5},{4,6},{5,7},{14,8},{15,9},{8,1... | collective-permute-start | bytes 1966088 | tf_op jit(solution)/shard_map/ppermute | solution.py:29
  333.2 1.8 copy-start.8
  335.0 27.5 %collective-permute-start.11 = (f32[20,64,128]{2,1,0:T(8,128)}, f32[20,64,128]{2,1,0:T(8,128)}, u32[]{:S(2)}, u32[]{:S(2)}) collective-permute-start(f32[20,64,128]{2,1,0:T(8,128)} %get-tuple-element.61), channel_id=1, source_target_pairs={{2,0},{3,1},{4,2},{5,3},{6,4},{7,5},{0,6},{1,7},{10,8},{11,9},{12,... | collective-permute-start | bytes 1966088 | tf_op jit(solution)/shard_map/ppermute | solution.py:29
  356.4 22.0 %collective-permute-start.7 = (f32[16,64,128]{2,1,0:T(8,128)}, f32[16,64,128]{2,1,0:T(8,128)}, u32[]{:S(2)}, u32[]{:S(2)}) collective-permute-start(f32[16,64,128]{2,1,0:T(8,128)} %slice_select_fusion.4), channel_id=1, source_target_pairs={{1,0},{0,1},{3,2},{2,3},{5,4},{4,5},{7,6},{6,7},{9,8},{8,9},{11,10... | collective-permute-start | bytes 1572872 | tf_op jit(solution)/shard_map/ppermute | solution.py:29
  360.7 21.2 %collective-permute-start.15 = (f32[20,64,128]{2,1,0:T(8,128)}, f32[20,64,128]{2,1,0:T(8,128)}, u32[]{:S(2)}, u32[]{:S(2)}) collective-permute-start(f32[20,64,128]{2,1,0:T(8,128)} %get-tuple-element.60), channel_id=1, source_target_pairs={{6,0},{7,1},{0,2},{1,3},{2,4},{3,5},{4,6},{5,7},{14,8},{15,9},{8,1... | collective-permute-start | bytes 1966088 | tf_op jit(solution)/shard_map/ppermute | solution.py:29
  362.6 19.4 %collective-permute-start.16 = (f32[20,64,128]{2,1,0:T(8,128)}, f32[20,64,128]{2,1,0:T(8,128)}, u32[]{:S(2)}, u32[]{:S(2)}) collective-permute-start(f32[20,64,128]{2,1,0:T(8,128)} %get-tuple-element.59), channel_id=1, source_target_pairs={{2,0},{3,1},{4,2},{5,3},{6,4},{7,5},{0,6},{1,7},{10,8},{11,9},{12,... | collective-permute-start | bytes 1966088 | tf_op jit(solution)/shard_map/ppermute | solution.py:29
  378.4 15.4 %collective-permute-start.13 = (f32[16,64,128]{2,1,0:T(8,128)}, f32[16,64,128]{2,1,0:T(8,128)}, u32[]{:S(2)}, u32[]{:S(2)}) collective-permute-start(f32[16,64,128]{2,1,0:T(8,128)} %collective-permute-done.7.refs_5_), channel_id=1, source_target_pairs={{6,0},{7,1},{0,2},{1,3},{2,4},{3,5},{4,6},{5,7},{14,8},{15,9},{8,1... | collective-permute-start | bytes 1572872 | tf_op jit(solution)/shard_map/ppermute | solution.py:29
  381.9 13.5 %collective-permute-start.14 = (f32[16,64,128]{2,1,0:T(8,128)}, f32[16,64,128]{2,1,0:T(8,128)}, u32[]{:S(2)}, u32[]{:S(2)}) collective-permute-start(f32[16,64,128]{2,1,0:T(8,128)} %collective-permute-done.6.refs_0_), channel_id=1, source_target_pairs={{2,0},{3,1},{4,2},{5,3},{6,4},{7,5},{0,6},{1,7},{10,8},{11,9},{12,... | collective-permute-start | bytes 1572872 | tf_op jit(solution)/shard_map/ppermute | solution.py:29

commit v5 on v4

--- a/solution.py
+++ b/solution.py
@@ -9,6 +9,7 @@
 
 CBLK = 64
 AHEAD = 3
+PIECES = 4
 SIZES = (20, 20, 16)
 GROUP = 4
 VMEM_LIMIT = 60 * 1024 * 1024
@@ -86,42 +87,46 @@
     )(a_pick, b_pick, *small, a_blocks, b_blocks)
 
 
-def compact_kernel(a_place, far_place, b_place, arrived, up_out, low_out, b_out, up_ref, low_ref, b_ref, in_sem, out_sem):
-    half = up_out.shape[1]
-    sides = [
-        (a_place, 0, pl.ds(0, half), up_ref, up_out),
-        (far_place, 0, pl.ds(half, half), low_ref, low_out),
-        (b_place, 1, pl.ds(0, 2 * half), b_ref, b_out),
-    ]
-    for n, (place, side, rows, held, out) in enumerate(sides):
-
-        def body(j, carry, n=n, place=place, side=side, rows=rows, held=held):
-            pltpu.make_async_copy(arrived.at[place[j], side, rows], held.at[j], in_sem.at[n]).start()
+def compact_kernel(parts, *refs):
+    number = len(parts)
+    places, arrived, outs, held = refs[:number], refs[number], refs[number + 1 : 2 * number + 1], refs[2 * number + 1 :]
+    in_sem, out_sem = held[number:]
+    pieces = [(n, k) for n in range(number) for k in range(PIECES)]
+    for n, k in pieces:
+        side, first, size = parts[n]
+        step = places[n].shape[0] // PIECES
+
+        def body(j, carry, n=n, k=k, side=side, rows=pl.ds(first, size)):
+            source = arrived.at[places[n][j], side, rows]
+            pltpu.make_async_copy(source, held[n].at[j], in_sem.at[n, k]).start()
             return carry
 
-        lax.fori_loop(0, place.shape[0], body, 0, unroll=4)
-    for n, (place, side, rows, held, out) in enumerate(sides):
-        pltpu.make_async_copy(held, held, in_sem.at[n]).wait()
-        pltpu.make_async_copy(held, out, out_sem.at[n]).start()
-    for n, (place, side, rows, held, out) in enumerate(sides):
-        pltpu.make_async_copy(held, out, out_sem.at[n]).wait()
-
-
-def compact(a_place, far_place, b_place, arrived):
-    panel = a_place.shape[0]
+        lax.fori_loop(k * step, (k + 1) * step, body, 0, unroll=2)
+    copies = []
+    for n, k in pieces:
+        step = places[n].shape[0] // PIECES
+        piece = held[n].at[pl.ds(k * step, step)]
+        copies.append(pltpu.make_async_copy(piece, outs[n].at[pl.ds(k * step, step)], out_sem.at[n, k]))
+        pltpu.make_async_copy(piece, piece, in_sem.at[n, k]).wait()
+        copies[-1].start()
+    for copy in copies:
+        copy.wait()
+
+
+def compact(places, parts, arrived):
     width = arrived.shape[-1]
-    shapes = [(panel, width // 2, width), (panel, width // 2, width), (panel, width, width)]
+    shapes = [(place.shape[0], size, width) for place, (_, _, size) in zip(places, parts)]
     return pl.pallas_call(
-        compact_kernel,
+        functools.partial(compact_kernel, tuple(parts)),
         out_shape=[jax.ShapeDtypeStruct(shape, jnp.float32) for shape in shapes],
-        in_specs=[SMEM, SMEM, SMEM, HBM],
-        out_specs=[HBM] * 3,
+        in_specs=[SMEM] * len(parts) + [HBM],
+        out_specs=[HBM] * len(parts),
         scratch_shapes=[pltpu.VMEM(shape, jnp.float32) for shape in shapes]
-        + [pltpu.SemaphoreType.DMA((3,)), pltpu.SemaphoreType.DMA((3,))],
+        + [pltpu.SemaphoreType.DMA((len(parts), PIECES)), pltpu.SemaphoreType.DMA((len(parts), PIECES))],
         compiler_params=pltpu.CompilerParams(vmem_limit_bytes=VMEM_LIMIT),
-        cost_estimate=pl.CostEstimate(flops=0, bytes_accessed=16 * panel * width * width, transcendentals=0),
+        cost_estimate=pl.CostEstimate(flops=10**11, bytes_accessed=16 * 2**20, transcendentals=0),
         name="compact",
-    )(a_place, far_place, b_place, arrived)
+    )(*places, arrived)
 
 
 def split(value):
@@ -133,12 +138,15 @@
 def block_product(left, right):
     lh, ll = split(left)
     rh, rl = split(right)
-    both = jnp.dot(
+    width = right.shape[1]
+    wide = jnp.dot(
         jnp.concatenate([lh, ll], axis=1),
-        jnp.concatenate([rh, rh], axis=0),
+        jnp.concatenate(
+            [jnp.concatenate([rh, rl], axis=1), jnp.concatenate([rh, jnp.zeros_like(rl)], axis=1)], axis=0
+        ),
         preferred_element_type=jnp.float32,
     )
-    return both + jnp.dot(lh, rl, preferred_element_type=jnp.float32)
+    return wide[:, :width] + wide[:, width:]
 
 
 def rows_of(ref, spec):
@@ -263,77 +271,121 @@
     )(*operands)
 
 
-def last_kernel(jobs, flags, index_a, index_b, index_c, *refs):
-    c_in, c_out, a_ref, b_ref, c_ref, live, place, sem = refs[len(refs) - 8 :]
-    blocks = c_out.shape[0]
+def plan_kernel(ranges, index_a, index_b, index_c, plan):
+    blocks = CBLK
     entries = index_a.shape[1]
-    half = c_ref.shape[1] // 2
-    room = len(jobs) * entries
 
     def clear(m, carry):
-        place[m] = -1
+        plan[4, m] = -1
         return carry
 
     lax.fori_loop(0, blocks, clear, 0, unroll=8)
-
     counts = (0, 0)
-    for t, first, size, upper, lower, b in jobs:
-
-        def fetch(e, counts, t=t, first=first, size=size, upper=upper, lower=lower, b=b):
+    for n, (t, first, size) in enumerate(ranges):
+
+        def note(e, counts, t=t, first=first, size=size):
             slot, m = index_a[t, e] - first, index_c[t, e]
             used = (m < blocks) & (slot >= 0) & (slot < size)
             count, kept = counts
-            new = used & (place[jnp.minimum(m, blocks - 1)] < 0)
+            new = used & (plan[4, jnp.minimum(m, blocks - 1)] < 0)
+
+            @pl.when(new)
+            def _():
+                plan[4, m] = kept
+                plan[3, kept] = m
 
             @pl.when(used)
             def _():
-                live[count] = m
-                for part, (n, spec) in enumerate((upper, lower)):
-                    source = rows_of(refs[n], spec).at[slot]
-                    target = a_ref.at[count, pl.ds(part * half, half)]
-                    pltpu.make_async_copy(source, target, sem.at[0]).start()
-                for k, n in enumerate(b):
-                    copy = pltpu.make_async_copy(refs[n].at[index_b[t, e]], b_ref.at[count], sem.at[0])
-                    if len(b) == 1:
-                        copy.start()
-                    else:
-                        pl.when(flags[0] == k)(copy.start)
-
-            @pl.when(new)
-            def _():
-                place[m] = kept
-                live[room + kept] = m
-                pltpu.make_async_copy(c_in.at[m], c_ref.at[kept], sem.at[0]).start()
+                plan[0, count] = slot
+                plan[1, count] = index_b[t, e]
+                plan[2, count] = plan[4, m]
 
             return count + jnp.where(used, 1, 0), kept + jnp.where(new, 1, 0)
 
-        counts = lax.fori_loop(0, entries, fetch, counts)
-    count, kept = counts
+        counts = lax.fori_loop(0, entries, note, counts)
+        plan[5, n] = counts[0]
+    plan[5, len(ranges)] = counts[1]
+
+
+def make_plan(prods, ranges):
+    entries = prods[0].shape[1]
+    return pl.pallas_call(
+        functools.partial(plan_kernel, tuple(ranges)),
+        out_shape=jax.ShapeDtypeStruct((6, max(len(ranges) * entries, CBLK)), jnp.int32),
+        in_specs=[SMEM] * 3,
+        out_specs=SMEM,
+        name="plan",
+    )(*prods)
+
+
+def last_kernel(jobs, flags, plan, *refs):
+    number = len(jobs)
+    c_in, c_out, b_ref, c_ref, sem = refs[len(refs) - number - 5 : len(refs) - number - 3] + refs[len(refs) - 3 :]
+    held = refs[len(refs) - number - 3 : len(refs) - 3]
+    half = c_ref.shape[1] // 2
+    kept = plan[5, number]
+
+    copies = []
+    for n, (upper, lower, _) in enumerate(jobs):
+        for part, (source, spec) in enumerate((upper, lower)):
+            rows = held[n].at[:, pl.ds(part * half, half)]
+            copies.append(pltpu.make_async_copy(rows_of(refs[source], spec), rows, sem.at[2 + 2 * n + part]))
+    for copy in copies:
+        copy.start()
+
+    begin = 0
+    for n, (_, _, b) in enumerate(jobs):
+        end = plan[5, n]
+
+        def fetch(at, carry, b=b):
+            for k, source in enumerate(b):
+                copy = pltpu.make_async_copy(refs[source].at[plan[1, at]], b_ref.at[at], sem.at[0])
+                if len(b) == 1:
+                    copy.start()
+                else:
+                    pl.when(flags[0] == k)(copy.start)
+            return carry
+
+        lax.fori_loop(begin, end, fetch, 0)
+        begin = end
+
+    def fetch_c(k, carry):
+        pltpu.make_async_copy(c_in.at[plan[3, k]], c_ref.at[k], sem.at[0]).start()
+        return carry
+
+    lax.fori_loop(0, kept, fetch_c, 0)
 
     def arrive(_, carry):
         pltpu.make_async_copy(c_in.at[0], c_ref.at[0], sem.at[0]).wait()
         return carry
 
-    lax.fori_loop(0, 2 * count + kept, arrive, 0)
-
-    def add(at):
-        c_ref[place[live[at]]] += block_product(a_ref[at], b_ref[at])
-
-    def several(g, carry):
-        for u in range(GROUP):
-            add(g * GROUP + u)
-        return carry
-
-    def single(at, carry):
-        add(at)
-        return carry
-
-    groups = count // GROUP
-    lax.fori_loop(0, groups, several, 0)
-    lax.fori_loop(groups * GROUP, count, single, 0)
+    lax.fori_loop(0, begin + kept, arrive, 0)
+    for copy in copies:
+        copy.wait()
+
+    begin = 0
+    for n in range(number):
+        end = plan[5, n]
+
+        def add(at, a_ref=held[n]):
+            c_ref[plan[2, at]] += block_product(a_ref[plan[0, at]], b_ref[at])
+
+        def several(g, carry, begin=begin, add=add):
+            for u in range(GROUP):
+                add(begin + g * GROUP + u)
+            return carry
+
+        def single(at, carry, add=add):
+            add(at)
+            return carry
+
+        groups = (end - begin) // GROUP
+        lax.fori_loop(0, groups, several, 0)
+        lax.fori_loop(begin + groups * GROUP, end, single, 0)
+        begin = end
 
     def store(k, carry):
-        pltpu.make_async_copy(c_ref.at[k], c_out.at[live[room + k]], sem.at[1]).start()
+        pltpu.make_async_copy(c_ref.at[k], c_out.at[plan[3, k]], sem.at[1]).start()
         return carry
 
     lax.fori_loop(0, kept, store, 0)
@@ -345,29 +397,25 @@
     lax.fori_loop(0, kept, leave, 0)
 
 
-def last_products(flags, prods, jobs, total):
-    entries = prods[0].shape[1]
+def last_products(flags, plan, entries, jobs, total):
     block = total.shape[1:]
     arrays = []
     static = []
-    for t, first, size, upper, lower, b in jobs:
+    for _, _, size, upper, lower, b in jobs:
         n = len(arrays)
         arrays += [upper[0], lower[0], *b]
-        static.append((t, first, size, (n, upper[1]), (n + 1, lower[1]), tuple(range(n + 2, len(arrays)))))
-    operands = [flags, *prods, *arrays, total]
-    room = len(jobs) * entries
+        static.append(((n, upper[1]), (n + 1, lower[1]), tuple(range(n + 2, len(arrays)))))
+    operands = [flags, plan, *arrays, total]
     return pl.pallas_call(
         functools.partial(last_kernel, tuple(static)),
         out_shape=jax.ShapeDtypeStruct(total.shape, jnp.float32),
-        in_specs=[SMEM] * 4 + [ANY] * (len(operands) - 4),
+        in_specs=[SMEM] * 2 + [ANY] * (len(operands) - 2),
         out_specs=ANY,
-        scratch_shapes=[
-            pltpu.VMEM((room, *block), jnp.float32),
-            pltpu.VMEM((room, *block), jnp.float32),
-            pltpu.VMEM((total.shape[0], *block), jnp.float32),
-            pltpu.SMEM((room + total.shape[0],), jnp.int32),
-            pltpu.SMEM((total.shape[0],), jnp.int32),
-            pltpu.SemaphoreType.DMA((2,)),
+        scratch_shapes=[pltpu.VMEM((size, *block), jnp.float32) for _, _, size, _, _, _ in jobs]
+        + [
+            pltpu.VMEM((len(jobs) * entries, *block), jnp.float32),
+            pltpu.VMEM(total.shape, jnp.float32),
+            pltpu.SemaphoreType.DMA((2 + 2 * len(jobs),)),
         ],
         input_output_aliases={len(operands) - 1: 0},
         compiler_params=pltpu.CompilerParams(vmem_limit_bytes=VMEM_LIMIT),
@@ -389,8 +437,12 @@
     outgoing = fill(lax.axis_size("col"), a_pick, b_pick, (*prods, flags), a_blocks, b_blocks)
     outgoing, far_place, flags = together(outgoing, far_place, flags)
     arrived = lax.all_to_all(outgoing, ("row", "col"), split_axis=0, concat_axis=0, tiled=True)
-    up0, low3, b0 = compact(a_place, far_place, b_place, arrived)
-    up0, low3, b0, flags = together(up0, low3, b0, flags)
+    width = arrived.shape[-1]
+    half = width // 2
+    (b0,) = compact([b_place], [(1, 0, width)], arrived)
+    arrived, b0 = together(arrived, b0)
+    up0, low3 = compact([a_place, far_place], [(0, 0, half), (0, half, half)], arrived)
+    up0, low3, flags = together(up0, low3, flags)
     core1, odd = flags[0] == 1, flags[1] == 1
 
     up2 = permute(up0, lambda r, c: (r, c + 2))
@@ -404,7 +456,8 @@
         rows = slice(first, first + size)
         cross.append((jnp.where(odd, up0[rows], up2[rows]), jnp.where(odd, low1[rows], low3[rows])))
     cross = [jnp.stack(pair) for pair in cross[:last]] + [*cross[last]]
-    *cross, b0, b2, near0 = together(*cross, b0, b2, near0)
+    plan = make_plan(prods, [(t, firsts[last], SIZES[last]) for t in (0, 3)])
+    *cross, b0, b2, near0, plan = together(*cross, b0, b2, near0, plan)
 
     def over(part):
         return permute(part, lambda r, c: (r, c ^ 1))
@@ -449,7 +502,7 @@
     onward(mid[last], mid[last + 1])
     jobs = middle(last, (mid[last], None), (mid[last + 1], None)) + jobs
     total = products(flags, prods, jobs, total)
-    return last_products(flags, prods, outer(last), total)
+    return last_products(flags, plan, prod_a.shape[1], outer(last), total)
 
 
 def solution(mesh):

time: 404 us -> 399 us (0.988)
  waiting for transfers between devices: 111 us -> 102 us
    ppermute x17, waiting for transfers between devices: 111 us -> 102 us  [permute(): return lax.ppermute(array, ('row', 'col'), pairs)]
    pallas_call x1 -> x3, Pallas kernels: 7.14 us -> 12 us  [the longest x2 7.74 us: compact(): pl.pallas_call(functools.partial(compact_kernel, tuple(parts)), out_shape...]
  transfers between devices with their start and end apart: 17 -> 17, of which waited for: 6 -> 6; matrix products, arithmetic and copies ran while one was open for 3% -> 3% of each run, Pallas kernels for 9% -> 12%
where the time goes in v5:
time: 399 us; the launch traced here: 398 us
  blocking collectives  197 us (49%)
  waiting for transfers between devices  102 us (26%)
  Pallas kernels  56.5 us (14%)
  starting transfers between devices  27.9 us (7%)
  other arithmetic  9.48 us (2%)
  local copies, waits for them, and re-layouts  4.69 us (1%)
    all_to_all x1, blocking collectives, local(): lax.all_to_all(outgoing, ('row', 'col'), split_axis=0, concat_axis=0, til...  197 us
    ppermute x17, waiting for transfers between devices, permute(): return lax.ppermute(array, ('row', 'col'), pairs)  102 us
    pallas_call x3, Pallas kernels, products(): pl.pallas_call(functools.partial(products_kernel, tuple(static), has_c),...  32.4 us
    ppermute x17, starting transfers between devices, permute(): return lax.ppermute(array, ('row', 'col'), pairs)  27.9 us
  transfers between devices with their start and end apart: 17, of which 6 were waited for; matrix products, arithmetic and copies ran while one was open for 3% of the time, Pallas kernels for 12%

profile of v5, /device:TPU:0, one launch (start us, length us, event | category | flops | bytes accessed | tf_op | source)
XLA Modules:
  0.0 398.3 jit_solution(13146081662999358724)
XLA Ops:
  0.0 4.1 %collective-permute-start = (s32[56]{0:T(128)}, s32[56]{0:T(128)S(1)}, u32[]{:S(2)}, u32[]{:S(2)}) collective-permute-start(s32[56]{0:T(128)} %refs_0_.3), channel_id=1, source_target_pairs={{3,0},{4,1},{5,2},{6,3},{7,4},{0,5},{1,6},{2,7},{11,8},{12,9},{13,... | collective-permute-start | bytes 680 | tf_op jit(solution)/shard_map/ppermute | solution.py:30
  4.1 0.6 pad_add_fusion.flags
  4.7 6.0 %fill.1 = f32[128,2,128,128]{3,2,1,0:T(8,128)} custom-call(s32[128]{0:T(128)} %a_pick.1, s32[128]{0:T(128)} %b_pick.1, s32[4,64]{1,0:T(4,128)} %index_a.7, s32[4,64]{1,0:T(4,128)} %index_b.7, s32[4,64]{1,0:T(4,128)} %index_c.7, s32[2]{0:T(128)} %pad_add_fusion.flags, f32[56,128,128]{2,1,0:T(8,128)} %a_blocks.1, f32[56,128,128]{2,1,0:T(8,128)} %b_blocks.1), custom_call_target="tpu_custom_call" | custom-call | bytes 14680064 | tf_op jit(solution)/shard_map/fill/pallas_call | solution.py:74
  10.7 0.0 collective-permute-done.refs_1_
  10.7 0.0 copy-start.4
  10.8 196.7 %all_to_all.5.refs_1_.refs_2_ = f32[128,2,128,128]{3,2,1,0:T(8,128)} all-to-all(f32[128,2,128,128]{3,2,1,0:T(8,128)} %fill.1), channel_id=1, replica_groups=mesh['row'=16,'col'=8] {'row','col'}, dimensions={0} | all-to-all | bytes 33554432 | tf_op jit(solution)/shard_map/all_to_all | solution.py:439
  207.4 3.7 compact.2.refs_8_.refs_9_.refs_2_
  211.2 0.5 collective-permute-start.3
  211.7 0.1 collective-permute-start.4
  211.7 4.0 %compact.3 = (f32[56,64,128]{2,1,0:T(8,128)}, f32[56,64,128]{2,1,0:T(8,128)}) custom-call(s32[56]{0:T(128)} %refs_0_.3, s32[56]{0:T(128)} %copy-done.4, f32[128,2,128,128]{3,2,1,0:T(8,128)} %all_to_all.5.refs_1_.refs_2_), custom_call_target="tpu_custom_call" | custom-call | flops 99999997952 | bytes 16777216 | tf_op jit(solution)/shard_map/compact/pallas_call | solution.py:119
  215.8 3.7 collective-permute-start.2
  219.5 0.0 collective-permute-start.1
  219.5 4.2 %plan.1 = s32[6,128]{1,0:T(8,128)} custom-call(s32[4,64]{1,0:T(4,128)} %index_a.7, s32[4,64]{1,0:T(4,128)} %index_b.7, s32[4,64]{1,0:T(4,128)} %index_c.7), custom_call_target="tpu_custom_call" | custom-call | tf_op jit(solution)/shard_map/plan/pallas_call | solution.py:312
  223.7 0.6 slice.51
  225.0 34.8 %collective-permute-done.2.refs_1_ = f32[56,64,128]{2,1,0:T(8,128)S(1)} collective-permute-done((f32[56,64,128]{2,1,0:T(8,128)}, f32[56,64,128]{2,1,0:T(8,128)S(1)}, u32[]{:S(2)}, u32[]{:S(2)}) %collective-permute-start.2) | collective-permute-done | bytes 1835040 | tf_op jit(solution)/shard_map/ppermute | solution.py:30
  259.8 2.2 fusion
  261.9 0.0 collective-permute-done.1.refs_4_
  262.0 0.4 copy-done
  262.3 1.5 fusion.1
  263.8 1.4 pad_maximum_fusion
  265.2 1.9 slice_select_fusion.5
  267.1 1.9 slice_select_fusion.4
  269.0 24.1 %collective-permute-done.3.refs_5_.refs_6_ = f32[56,128,128]{2,1,0:T(8,128)} collective-permute-done((f32[56,128,128]{2,1,0:T(8,128)}, f32[56,128,128]{2,1,0:T(8,128)}, u32[]{:S(2)}, u32[]{:S(2)}) %collective-permute-start.3) | collective-permute-done | bytes 3670048 | tf_op jit(solution)/shard_map/ppermute | solution.py:30
  293.1 0.0 collective-permute-done.4.refs_2_
  293.1 0.0 collective-permute-start.9
  293.1 1.7 collective-permute-start.5
  294.8 0.3 collective-permute-start.8
  295.2 4.2 %collective-permute-start.12 = (f32[56,128,128]{2,1,0:T(8,128)}, f32[56,128,128]{2,1,0:T(8,128)}, u32[]{:S(2)}, u32[]{:S(2)}) collective-permute-start(f32[56,128,128]{2,1,0:T(8,128)} %compact.2.refs_8_.refs_9_.refs_2_), channel_id=1, source_target_pairs={{32,8},{33,9},{34,10},{35,11},{36,12},{37,13},{38,14},{39,15},{48,... | collective-permute-start | bytes 11010056 | tf_op jit(solution)/shard_map/ppermute | solution.py:30
  299.3 25.4 %collective-permute-done.5.refs_0_ = f32[2,20,64,128]{3,2,1,0:T(8,128)S(1)} collective-permute-done((f32[2,20,64,128]{3,2,1,0:T(8,128)S(1)}, f32[2,20,64,128]{3,2,1,0:T(8,128)S(1)}, u32[]{:S(2)}, u32[]{:S(2)}) %collective-permute-start.5) | collective-permute-done | bytes 1310752 | tf_op jit(solution)/shard_map/ppermute | solution.py:30
  324.7 1.7 collective-permute-start.6
  326.4 1.2 slice_bitcast_fusion.2
  327.6 2.0 collective-permute-start.10
  329.7 0.0 collective-permute-done.9.refs_3_.refs_5_
  329.7 1.2 collective-permute-start.11
  330.9 8.1 %products.3.refs_12_ = f32[64,128,128]{2,1,0:T(8,128)} custom-call(s32[2]{0:T(128)} %pad_add_fusion.flags, s32[4,64]{1,0:T(4,128)} %index_a.7, s32[4,64]{1,0:T(4,128)} %index_b.7, s32[4,64]{1,0:T(4,128)} %index_c.7, f32[2,20,64,128]{3,2,1,0:T(8,128)} %copy-done.2, f32[56,64,128]{2,1,0:T(8,128)} %copy-done.1, f32[56,128,128]{2,1,0:T(8,128)} %collective-permute-done.4.refs_2_, ...), custom_call_target="tpu_custom_call" | custom-call | flops 805306368000 | bytes 8388608 | tf_op jit(solution)/shard_map/products/pallas_call | solution.py:254
  339.0 13.9 %collective-permute-done.8.refs_0_ = f32[2,20,64,128]{3,2,1,0:T(8,128)} collective-permute-done((f32[2,20,64,128]{3,2,1,0:T(8,128)}, f32[2,20,64,128]{3,2,1,0:T(8,128)}, u32[]{:S(2)}, u32[]{:S(2)}) %collective-permute-start.8) | collective-permute-done | bytes 1310752 | tf_op jit(solution)/shard_map/ppermute | solution.py:30
  352.9 1.7 collective-permute-start.7
  354.6 2.5 slice_bitcast_fusion
  357.1 0.0 collective-permute-done.10.refs_7_
  357.1 1.9 collective-permute-start.15
  359.0 1.4 collective-permute-start.16
  360.3 11.7 %products.4.refs_13_ = f32[64,128,128]{2,1,0:T(8,128)} custom-call(s32[2]{0:T(128)} %pad_add_fusion.flags, s32[4,64]{1,0:T(4,128)} %index_a.7, s32[4,64]{1,0:T(4,128)} %index_b.7, s32[4,64]{1,0:T(4,128)} %index_c.7, f32[2,20,64,128]{3,2,1,0:T(8,128)} %collective-permute-done.8.refs_0_, f32[56,64,128]{2,1,0:T(8,128)} %copy-done.1, ...), custom_call_target="tpu_custom_call", output_to_operand_aliasing={{}: (16, {})} | custom-call | flops 805306368000 | bytes 8388608 | tf_op jit(solution)/shard_map/products/pallas_call | solution.py:254
  372.1 2.9 collective-permute-done.7.refs_5_
  375.0 3.5 collective-permute-start.13
  378.5 12.5 %products.5.refs_7_ = f32[64,128,128]{2,1,0:T(8,128)} custom-call(s32[2]{0:T(128)} %pad_add_fusion.flags, s32[4,64]{1,0:T(4,128)} %index_a.7, s32[4,64]{1,0:T(4,128)} %index_b.7, s32[4,64]{1,0:T(4,128)} %index_c.7, f32[16,64,128]{2,1,0:T(8,128)} %collective-permute-done.6.refs_0_, f32[56,64,128]{2,1,0:T(8,128)} %copy-done.1, ...), custom_call_target="tpu_custom_call", output_to_operand_aliasing={{}: (17, {})} | custom-call | flops 805306368000 | bytes 8388608 | tf_op jit(solution)/shard_map/products/pallas_call | solution.py:254
  391.1 0.0 collective-permute-done.13.refs_1_
  391.1 1.0 collective-permute-done.14.refs_3_
  392.1 6.2 %last_products.1 = f32[64,128,128]{2,1,0:T(8,128)} custom-call(s32[2]{0:T(128)} %pad_add_fusion.flags, s32[6,128]{1,0:T(8,128)} %plan.1, f32[56,64,128]{2,1,0:T(8,128)} %get-tuple-element.38.refs_6_.refs_7_.refs_0_, f32[16,64,128]{2,1,0:T(8,128)} %collective-permute-done.13.refs_1_, ...), custom_call_target="tpu_custom_call", output_to_operand_aliasing={{}: (9, {})} | custom-call | flops 805306368000 | bytes 8388608 | tf_op jit(solution)/shard_map/last_products/pallas_call | solution.py:409
  (14 shorter events, 0.0 us)
Async XLA Ops:
  0.0 10.7 %collective-permute-start = (s32[56]{0:T(128)}, s32[56]{0:T(128)S(1)}, u32[]{:S(2)}, u32[]{:S(2)}) collective-permute-start(s32[56]{0:T(128)} %refs_0_.3), channel_id=1, source_target_pairs={{3,0},{4,1},{5,2},{6,3},{7,4},{0,5},{1,6},{2,7},{11,8},{12,9},{13,... | collective-permute-start | bytes 680 | tf_op jit(solution)/shard_map/ppermute | solution.py:30
  10.7 196.7 %copy-start.4 = (s32[56]{0:T(128)}, s32[56]{0:T(128)S(1)}, u32[]{:S(2)}) copy-start(s32[56]{0:T(128)S(1)} %collective-permute-done.refs_1_) | copy-start | bytes 676
  211.2 12.6 %copy-start.3 = (s32[2]{0:T(128)S(1)}, s32[2]{0:T(128)}, u32[]{:S(2)}) copy-start(s32[2]{0:T(128)} %pad_add_fusion.flags) | copy-start | bytes 28
  211.2 82.0 %collective-permute-start.3 = (f32[56,128,128]{2,1,0:T(8,128)}, f32[56,128,128]{2,1,0:T(8,128)}, u32[]{:S(2)}, u32[]{:S(2)}) collective-permute-start(f32[56,128,128]{2,1,0:T(8,128)} %compact.2.refs_8_.refs_9_.refs_2_), channel_id=1, source_target_pairs={{16,0},{17,1},{18,2},{19,3},{20,4},{21,5},{22,6},{23,7},{24,8},{25... | collective-permute-start | bytes 11010056 | tf_op jit(solution)/shard_map/ppermute | solution.py:30
  211.7 81.5 %collective-permute-start.4 = (f32[56,128,128]{2,1,0:T(8,128)}, f32[56,128,128]{2,1,0:T(8,128)}, u32[]{:S(2)}, u32[]{:S(2)}) collective-permute-start(f32[56,128,128]{2,1,0:T(8,128)} %compact.2.refs_8_.refs_9_.refs_2_), channel_id=1, source_target_pairs={{8,0},{9,1},{10,2},{11,3},{12,4},{13,5},{14,6},{15,7},{0,8},{1,9},... | collective-permute-start | bytes 11010056 | tf_op jit(solution)/shard_map/ppermute | solution.py:30
  215.8 44.0 %collective-permute-start.2 = (f32[56,64,128]{2,1,0:T(8,128)}, f32[56,64,128]{2,1,0:T(8,128)S(1)}, u32[]{:S(2)}, u32[]{:S(2)}) collective-permute-start(f32[56,64,128]{2,1,0:T(8,128)} %get-tuple-element.39.refs_10_.refs_11_.refs_4_), channel_id=1, source_target_pairs={{6,0},{7,1},{0,2},{1,3},{2,4},{3,5},{4,6},{5,7},{14,8},{15,9},{8,1... | collective-permute-start | bytes 5505032 | tf_op jit(solution)/shard_map/ppermute | solution.py:30
  219.5 42.5 %collective-permute-start.1 = (f32[56,64,128]{2,1,0:T(8,128)}, f32[56,64,128]{2,1,0:T(8,128)}, u32[]{:S(2)}, u32[]{:S(2)}) collective-permute-start(f32[56,64,128]{2,1,0:T(8,128)} %get-tuple-element.38.refs_6_.refs_7_.refs_0_), channel_id=1, source_target_pairs={{2,0},{3,1},{4,2},{5,3},{6,4},{7,5},{0,6},{1,7},{10,8},{11,9},{12,... | collective-permute-start | bytes 5505032 | tf_op jit(solution)/shard_map/ppermute | solution.py:30
  259.8 7.3 %copy-start.1 = (f32[56,64,128]{2,1,0:T(8,128)}, f32[56,64,128]{2,1,0:T(8,128)S(1)}, u32[]{:S(2)}) copy-start(f32[56,64,128]{2,1,0:T(8,128)S(1)} %collective-permute-done.2.refs_1_) | copy-start | bytes 5505028
  259.8 2.6 copy-start
  293.1 36.5 %collective-permute-start.9 = (f32[56,128,128]{2,1,0:T(8,128)}, f32[56,128,128]{2,1,0:T(8,128)}, u32[]{:S(2)}, u32[]{:S(2)}) collective-permute-start(f32[56,128,128]{2,1,0:T(8,128)} %collective-permute-done.3.refs_5_.refs_6_), channel_id=1, source_target_pairs={{8,0},{9,1},{10,2},{11,3},{12,4},{13,5},{14,6},{15,7},{0,8},{1,9},... | collective-permute-start | bytes 11010056 | tf_op jit(solution)/shard_map/ppermute | solution.py:30
  293.1 31.6 %collective-permute-start.5 = (f32[2,20,64,128]{3,2,1,0:T(8,128)S(1)}, f32[2,20,64,128]{3,2,1,0:T(8,128)S(1)}, u32[]{:S(2)}, u32[]{:S(2)}) collective-permute-start(f32[2,20,64,128]{3,2,1,0:T(8,128)S(1)} %get-tuple-element.44), channel_id=1, source_target_pairs={{1,0},{0,1},{3,2},{2,3},{5,4},{4,5},{7,6},{6,7},{9,8},{8,9},{11,10... | collective-permute-start | bytes 3932168 | tf_op jit(solution)/shard_map/ppermute | solution.py:30
  294.8 58.1 %collective-permute-start.8 = (f32[2,20,64,128]{3,2,1,0:T(8,128)}, f32[2,20,64,128]{3,2,1,0:T(8,128)}, u32[]{:S(2)}, u32[]{:S(2)}) collective-permute-start(f32[2,20,64,128]{3,2,1,0:T(8,128)} %get-tuple-element.47), channel_id=1, source_target_pairs={{1,0},{0,1},{3,2},{2,3},{5,4},{4,5},{7,6},{6,7},{9,8},{8,9},{11,10... | collective-permute-start | bytes 3932168 | tf_op jit(solution)/shard_map/ppermute | solution.py:30
  295.2 65.2 %collective-permute-start.12 = (f32[56,128,128]{2,1,0:T(8,128)}, f32[56,128,128]{2,1,0:T(8,128)}, u32[]{:S(2)}, u32[]{:S(2)}) collective-permute-start(f32[56,128,128]{2,1,0:T(8,128)} %compact.2.refs_8_.refs_9_.refs_2_), channel_id=1, source_target_pairs={{32,8},{33,9},{34,10},{35,11},{36,12},{37,13},{38,14},{39,15},{48,... | collective-permute-start | bytes 11010056 | tf_op jit(solution)/shard_map/ppermute | solution.py:30
  324.7 6.2 %copy-start.2 = (f32[2,20,64,128]{3,2,1,0:T(8,128)}, f32[2,20,64,128]{3,2,1,0:T(8,128)S(1)}, u32[]{:S(2)}) copy-start(f32[2,20,64,128]{3,2,1,0:T(8,128)S(1)} %collective-permute-done.5.refs_0_) | copy-start | bytes 3932164
  324.7 47.4 %collective-permute-start.6 = (f32[16,64,128]{2,1,0:T(8,128)}, f32[16,64,128]{2,1,0:T(8,128)}, u32[]{:S(2)}, u32[]{:S(2)}) collective-permute-start(f32[16,64,128]{2,1,0:T(8,128)} %slice_select_fusion.5), channel_id=1, source_target_pairs={{1,0},{0,1},{3,2},{2,3},{5,4},{4,5},{7,6},{6,7},{9,8},{8,9},{11,10... | collective-permute-start | bytes 1572872 | tf_op jit(solution)/shard_map/ppermute | solution.py:30
  327.6 29.5 %collective-permute-start.10 = (f32[20,64,128]{2,1,0:T(8,128)}, f32[20,64,128]{2,1,0:T(8,128)}, u32[]{:S(2)}, u32[]{:S(2)}) collective-permute-start(f32[20,64,128]{2,1,0:T(8,128)} %get-tuple-element.64), channel_id=1, source_target_pairs={{6,0},{7,1},{0,2},{1,3},{2,4},{3,5},{4,6},{5,7},{14,8},{15,9},{8,1... | collective-permute-start | bytes 1966088 | tf_op jit(solution)/shard_map/ppermute | solution.py:30
  329.7 29.3 %collective-permute-start.11 = (f32[20,64,128]{2,1,0:T(8,128)}, f32[20,64,128]{2,1,0:T(8,128)}, u32[]{:S(2)}, u32[]{:S(2)}) collective-permute-start(f32[20,64,128]{2,1,0:T(8,128)} %get-tuple-element.63), channel_id=1, source_target_pairs={{2,0},{3,1},{4,2},{5,3},{6,4},{7,5},{0,6},{1,7},{10,8},{11,9},{12,... | collective-permute-start | bytes 1966088 | tf_op jit(solution)/shard_map/ppermute | solution.py:30
  352.9 22.1 %collective-permute-start.7 = (f32[16,64,128]{2,1,0:T(8,128)}, f32[16,64,128]{2,1,0:T(8,128)}, u32[]{:S(2)}, u32[]{:S(2)}) collective-permute-start(f32[16,64,128]{2,1,0:T(8,128)} %slice_select_fusion.4), channel_id=1, source_target_pairs={{1,0},{0,1},{3,2},{2,3},{5,4},{4,5},{7,6},{6,7},{9,8},{8,9},{11,10... | collective-permute-start | bytes 1572872 | tf_op jit(solution)/shard_map/ppermute | solution.py:30
  357.1 21.4 %collective-permute-start.15 = (f32[20,64,128]{2,1,0:T(8,128)}, f32[20,64,128]{2,1,0:T(8,128)}, u32[]{:S(2)}, u32[]{:S(2)}) collective-permute-start(f32[20,64,128]{2,1,0:T(8,128)} %get-tuple-element.62), channel_id=1, source_target_pairs={{6,0},{7,1},{0,2},{1,3},{2,4},{3,5},{4,6},{5,7},{14,8},{15,9},{8,1... | collective-permute-start | bytes 1966088 | tf_op jit(solution)/shard_map/ppermute | solution.py:30
  359.0 19.5 %collective-permute-start.16 = (f32[20,64,128]{2,1,0:T(8,128)}, f32[20,64,128]{2,1,0:T(8,128)}, u32[]{:S(2)}, u32[]{:S(2)}) collective-permute-start(f32[20,64,128]{2,1,0:T(8,128)} %get-tuple-element.61), channel_id=1, source_target_pairs={{2,0},{3,1},{4,2},{5,3},{6,4},{7,5},{0,6},{1,7},{10,8},{11,9},{12,... | collective-permute-start | bytes 1966088 | tf_op jit(solution)/shard_map/ppermute | solution.py:30
  375.0 16.1 %collective-permute-start.13 = (f32[16,64,128]{2,1,0:T(8,128)}, f32[16,64,128]{2,1,0:T(8,128)}, u32[]{:S(2)}, u32[]{:S(2)}) collective-permute-start(f32[16,64,128]{2,1,0:T(8,128)} %collective-permute-done.7.refs_5_), channel_id=1, source_target_pairs={{6,0},{7,1},{0,2},{1,3},{2,4},{3,5},{4,6},{5,7},{14,8},{15,9},{8,1... | collective-permute-start | bytes 1572872 | tf_op jit(solution)/shard_map/ppermute | solution.py:30
  378.5 13.6 %collective-permute-start.14 = (f32[16,64,128]{2,1,0:T(8,128)}, f32[16,64,128]{2,1,0:T(8,128)}, u32[]{:S(2)}, u32[]{:S(2)}) collective-permute-start(f32[16,64,128]{2,1,0:T(8,128)} %collective-permute-done.6.refs_0_), channel_id=1, source_target_pairs={{2,0},{3,1},{4,2},{5,3},{6,4},{7,5},{0,6},{1,7},{10,8},{11,9},{12,... | collective-permute-start | bytes 1572872 | tf_op jit(solution)/shard_map/ppermute | solution.py:30

commit v6 on v5

--- a/solution.py
+++ b/solution.py
@@ -210,9 +210,13 @@
             e = live[n, at]
             c_ref[index_c[t, e]] += block_product(a_ref[index_a[t, e] - first], b_ref[index_b[t, e]])
 
-        def several(g, carry, add=add):
-            for u in range(GROUP):
-                add(g * GROUP + u)
+        def product(at, n=n, t=t, first=first, a_ref=a_ref, b_ref=b_ref):
+            e = live[n, at]
+            return index_c[t, e], block_product(a_ref[index_a[t, e] - first], b_ref[index_b[t, e]])
+
+        def several(g, carry, product=product):
+            for m, value in [product(g * GROUP + u) for u in range(GROUP)]:
+                c_ref[m] += value
             return carry
 
         def single(at, carry, add=add):
@@ -370,9 +374,12 @@
         def add(at, a_ref=held[n]):
             c_ref[plan[2, at]] += block_product(a_ref[plan[0, at]], b_ref[at])
 
-        def several(g, carry, begin=begin, add=add):
-            for u in range(GROUP):
-                add(begin + g * GROUP + u)
+        def product(at, a_ref=held[n]):
+            return plan[2, at], block_product(a_ref[plan[0, at]], b_ref[at])
+
+        def several(g, carry, begin=begin, product=product):
+            for m, value in [product(begin + g * GROUP + u) for u in range(GROUP)]:
+                c_ref[m] += value
             return carry
 
         def single(at, carry, add=add):
@@ -433,15 +440,18 @@
 def local(a_blocks, a_pick, a_place, b_blocks, b_pick, b_place, prod_a, prod_b, prod_c):
     flags = jnp.stack([lax.axis_index("row") % 2, lax.axis_index("col") % 2]).astype(jnp.int32)
     prods = (prod_a, prod_b, prod_c)
-    far_place = permute(a_place, lambda r, c: (r, c + AHEAD))
     outgoing = fill(lax.axis_size("col"), a_pick, b_pick, (*prods, flags), a_blocks, b_blocks)
-    outgoing, far_place, flags = together(outgoing, far_place, flags)
+    outgoing, flags = together(outgoing, flags)
     arrived = lax.all_to_all(outgoing, ("row", "col"), split_axis=0, concat_axis=0, tiled=True)
     width = arrived.shape[-1]
     half = width // 2
+    arrived, a_place = together(arrived, a_place)
+    far_place = permute(a_place, lambda r, c: (r, c + AHEAD))
     (b0,) = compact([b_place], [(1, 0, width)], arrived)
     arrived, b0 = together(arrived, b0)
-    up0, low3 = compact([a_place, far_place], [(0, 0, half), (0, half, half)], arrived)
+    (up0,) = compact([a_place], [(0, 0, half)], arrived)
+    arrived, far_place, up0 = together(arrived, far_place, up0)
+    (low3,) = compact([far_place], [(0, half, half)], arrived)
     up0, low3, flags = together(up0, low3, flags)
     core1, odd = flags[0] == 1, flags[1] == 1
 

time: 399 us -> 398 us (level)
  waiting for transfers between devices: 102 us -> 97.5 us
    ppermute x17, waiting for transfers between devices: 102 us -> 97.5 us  [permute(): return lax.ppermute(array, ('row', 'col'), pairs)]
    pallas_call x2 -> x3, Pallas kernels: 7.74 us -> 9.97 us  [compact(): pl.pallas_call(functools.partial(compact_kernel, tuple(parts)), out_shape...]
  transfers between devices with their start and end apart: 17 -> 17, of which waited for: 6 -> 7; matrix products, arithmetic and copies ran while one was open for 3% -> 3% of each run, Pallas kernels for 12% -> 11%
where the time goes in v6:
time: 398 us; the launch traced here: 396 us
  blocking collectives  199 us (50%)
  waiting for transfers between devices  97.5 us (24%)
  Pallas kernels  58.7 us (15%)
  starting transfers between devices  26.3 us (7%)
  other arithmetic  9.31 us (2%)
  local copies, waits for them, and re-layouts  4.83 us (1%)
    all_to_all x1, blocking collectives, local(): lax.all_to_all(outgoing, ('row', 'col'), split_axis=0, concat_axis=0, til...  199 us
    ppermute x17, waiting for transfers between devices, permute(): return lax.ppermute(array, ('row', 'col'), pairs)  97.5 us
    pallas_call x3, Pallas kernels, products(): pl.pallas_call(functools.partial(products_kernel, tuple(static), has_c),...  32.5 us
    ppermute x17, starting transfers between devices, permute(): return lax.ppermute(array, ('row', 'col'), pairs)  26.3 us
    pallas_call x3, Pallas kernels, compact(): pl.pallas_call(functools.partial(compact_kernel, tuple(parts)), out_shape...  9.97 us
  transfers between devices with their start and end apart: 17, of which 7 were waited for; matrix products, arithmetic and copies ran while one was open for 3% of the time, Pallas kernels for 11%

profile of v6, /device:TPU:0, one launch (start us, length us, event | category | flops | bytes accessed | tf_op | source)
XLA Modules:
  0.0 396.4 jit_solution(11561457350944280444)
XLA Ops:
  0.0 0.6 pad_add_fusion.flags
  0.6 6.1 %fill.1 = f32[128,2,128,128]{3,2,1,0:T(8,128)} custom-call(s32[128]{0:T(128)} %a_pick.1, s32[128]{0:T(128)} %b_pick.1, s32[4,64]{1,0:T(4,128)} %index_a.7, s32[4,64]{1,0:T(4,128)} %index_b.7, s32[4,64]{1,0:T(4,128)} %index_c.7, s32[2]{0:T(128)} %pad_add_fusion.flags, f32[56,128,128]{2,1,0:T(8,128)} %a_blocks.1, f32[56,128,128]{2,1,0:T(8,128)} %b_blocks.1), custom_call_target="tpu_custom_call" | custom-call | bytes 14680064 | tf_op jit(solution)/shard_map/fill/pallas_call | solution.py:74
  6.7 198.9 %all_to_all.5.refs_1_ = f32[128,2,128,128]{3,2,1,0:T(8,128)} all-to-all(f32[128,2,128,128]{3,2,1,0:T(8,128)} %fill.1), channel_id=1, replica_groups=mesh['row'=16,'col'=8] {'row','col'}, dimensions={0} | all-to-all | bytes 33554432 | tf_op jit(solution)/shard_map/all_to_all | solution.py:445
  205.7 3.9 compact.3.refs_8_.refs_9_.refs_2_
  209.5 0.5 collective-permute-start.3
  210.0 0.1 collective-permute-start.4
  210.1 2.9 collective-permute-start
  213.0 3.0 compact.4.refs_6_.refs_7_.refs_0_
  216.0 0.0 copy-start.4
  216.0 0.5 copy-done.4
  216.5 3.1 compact.5.refs_10_.refs_11_.refs_4_
  219.6 2.1 collective-permute-start.2
  221.7 1.2 collective-permute-start.1
  222.9 4.2 %plan.1 = s32[6,128]{1,0:T(8,128)} custom-call(s32[4,64]{1,0:T(4,128)} %index_a.7, s32[4,64]{1,0:T(4,128)} %index_b.7, s32[4,64]{1,0:T(4,128)} %index_c.7), custom_call_target="tpu_custom_call" | custom-call | tf_op jit(solution)/shard_map/plan/pallas_call | solution.py:316
  227.2 0.6 slice.51
  228.4 35.0 %collective-permute-done.2.refs_1_ = f32[56,64,128]{2,1,0:T(8,128)} collective-permute-done((f32[56,64,128]{2,1,0:T(8,128)}, f32[56,64,128]{2,1,0:T(8,128)}, u32[]{:S(2)}, u32[]{:S(2)}) %collective-permute-start.2) | collective-permute-done | bytes 1835040 | tf_op jit(solution)/shard_map/ppermute | solution.py:30
  263.4 1.9 fusion
  265.2 0.0 collective-permute-done.1.refs_4_
  265.3 1.5 fusion.1
  266.7 1.4 pad_maximum_fusion
  268.1 1.9 slice_select_fusion.5
  270.0 2.1 slice_select_fusion.4
  272.1 19.4 %collective-permute-done.3.refs_5_.refs_6_ = f32[56,128,128]{2,1,0:T(8,128)} collective-permute-done((f32[56,128,128]{2,1,0:T(8,128)}, f32[56,128,128]{2,1,0:T(8,128)}, u32[]{:S(2)}, u32[]{:S(2)}) %collective-permute-start.3) | collective-permute-done | bytes 3670048 | tf_op jit(solution)/shard_map/ppermute | solution.py:30
  291.5 1.7 collective-permute-start.5
  293.2 0.3 collective-permute-start.8
  293.5 4.2 %collective-permute-start.12 = (f32[56,128,128]{2,1,0:T(8,128)}, f32[56,128,128]{2,1,0:T(8,128)}, u32[]{:S(2)}, u32[]{:S(2)}) collective-permute-start(f32[56,128,128]{2,1,0:T(8,128)} %compact.3.refs_8_.refs_9_.refs_2_), channel_id=1, source_target_pairs={{32,8},{33,9},{34,10},{35,11},{36,12},{37,13},{38,14},{39,15},{48,... | collective-permute-start | bytes 11010056 | tf_op jit(solution)/shard_map/ppermute | solution.py:30
  297.7 25.4 %collective-permute-done.5.refs_0_ = f32[2,20,64,128]{3,2,1,0:T(8,128)S(1)} collective-permute-done((f32[2,20,64,128]{3,2,1,0:T(8,128)S(1)}, f32[2,20,64,128]{3,2,1,0:T(8,128)S(1)}, u32[]{:S(2)}, u32[]{:S(2)}) %collective-permute-start.5) | collective-permute-done | bytes 1310752 | tf_op jit(solution)/shard_map/ppermute | solution.py:30
  323.1 1.7 collective-permute-start.6
  324.8 1.2 slice_bitcast_fusion.2
  326.0 2.0 collective-permute-start.10
  328.0 1.2 collective-permute-start.11
  329.2 8.0 %products.3.refs_12_ = f32[64,128,128]{2,1,0:T(8,128)} custom-call(s32[2]{0:T(128)} %pad_add_fusion.flags, s32[4,64]{1,0:T(4,128)} %index_a.7, s32[4,64]{1,0:T(4,128)} %index_b.7, s32[4,64]{1,0:T(4,128)} %index_c.7, f32[2,20,64,128]{3,2,1,0:T(8,128)} %copy-done.1, f32[56,64,128]{2,1,0:T(8,128)} %collective-permute-done.2.refs_1_, ...), custom_call_target="tpu_custom_call" | custom-call | flops 805306368000 | bytes 8388608 | tf_op jit(solution)/shard_map/products/pallas_call | solution.py:258
  337.2 14.0 %collective-permute-done.8.refs_0_ = f32[2,20,64,128]{3,2,1,0:T(8,128)} collective-permute-done((f32[2,20,64,128]{3,2,1,0:T(8,128)}, f32[2,20,64,128]{3,2,1,0:T(8,128)}, u32[]{:S(2)}, u32[]{:S(2)}) %collective-permute-start.8) | collective-permute-done | bytes 1310752 | tf_op jit(solution)/shard_map/ppermute | solution.py:30
  351.3 1.7 collective-permute-start.7
  353.0 2.5 slice_bitcast_fusion
  355.5 0.0 collective-permute-done.10.refs_7_
  355.5 1.9 collective-permute-start.15
  357.4 0.0 collective-permute-done.11.refs_9_
  357.4 1.4 collective-permute-start.16
  358.7 13.0 %products.4.refs_13_ = f32[64,128,128]{2,1,0:T(8,128)} custom-call(s32[2]{0:T(128)} %pad_add_fusion.flags, s32[4,64]{1,0:T(4,128)} %index_a.7, s32[4,64]{1,0:T(4,128)} %index_b.7, s32[4,64]{1,0:T(4,128)} %index_c.7, f32[2,20,64,128]{3,2,1,0:T(8,128)} %collective-permute-done.8.refs_0_, ...), custom_call_target="tpu_custom_call", output_to_operand_aliasing={{}: (16, {})} | custom-call | flops 805306368000 | bytes 8388608 | tf_op jit(solution)/shard_map/products/pallas_call | solution.py:258
  371.7 1.7 collective-permute-done.7.refs_5_
  373.4 3.5 collective-permute-start.13
  376.9 0.0 collective-permute-start.14
  376.9 0.0 collective-permute-done.15.refs_8_
  376.9 11.5 %products.5.refs_7_ = f32[64,128,128]{2,1,0:T(8,128)} custom-call(s32[2]{0:T(128)} %pad_add_fusion.flags, s32[4,64]{1,0:T(4,128)} %index_a.7, s32[4,64]{1,0:T(4,128)} %index_b.7, s32[4,64]{1,0:T(4,128)} %index_c.7, f32[16,64,128]{2,1,0:T(8,128)} %collective-permute-done.6.refs_0_, ...), custom_call_target="tpu_custom_call", output_to_operand_aliasing={{}: (17, {})} | custom-call | flops 805306368000 | bytes 8388608 | tf_op jit(solution)/shard_map/products/pallas_call | solution.py:258
  388.4 0.1 collective-permute-done.13.refs_1_
  388.4 2.0 collective-permute-done.14.refs_3_
  390.5 5.9 %last_products.1 = f32[64,128,128]{2,1,0:T(8,128)} custom-call(s32[2]{0:T(128)} %pad_add_fusion.flags, s32[6,128]{1,0:T(8,128)} %plan.1, f32[56,64,128]{2,1,0:T(8,128)} %compact.4.refs_6_.refs_7_.refs_0_, f32[16,64,128]{2,1,0:T(8,128)} %collective-permute-done.13.refs_1_, ...), custom_call_target="tpu_custom_call", output_to_operand_aliasing={{}: (9, {})} | custom-call | flops 805306368000 | bytes 8388608 | tf_op jit(solution)/shard_map/last_products/pallas_call | solution.py:416
  (15 shorter events, 0.0 us)
Async XLA Ops:
  205.7 4.4 %copy-start.3 = (s32[56]{0:T(128)S(1)}, s32[56]{0:T(128)}, u32[]{:S(2)}) copy-start(s32[56]{0:T(128)} %refs_0_.2) | copy-start | bytes 676
  209.5 82.0 %collective-permute-start.3 = (f32[56,128,128]{2,1,0:T(8,128)}, f32[56,128,128]{2,1,0:T(8,128)}, u32[]{:S(2)}, u32[]{:S(2)}) collective-permute-start(f32[56,128,128]{2,1,0:T(8,128)} %compact.3.refs_8_.refs_9_.refs_2_), channel_id=1, source_target_pairs={{16,0},{17,1},{18,2},{19,3},{20,4},{21,5},{22,6},{23,7},{24,8},{25... | collective-permute-start | bytes 11010056 | tf_op jit(solution)/shard_map/ppermute | solution.py:30
  210.0 81.5 %collective-permute-start.4 = (f32[56,128,128]{2,1,0:T(8,128)}, f32[56,128,128]{2,1,0:T(8,128)}, u32[]{:S(2)}, u32[]{:S(2)}) collective-permute-start(f32[56,128,128]{2,1,0:T(8,128)} %compact.3.refs_8_.refs_9_.refs_2_), channel_id=1, source_target_pairs={{8,0},{9,1},{10,2},{11,3},{12,4},{13,5},{14,6},{15,7},{0,8},{1,9},... | collective-permute-start | bytes 11010056 | tf_op jit(solution)/shard_map/ppermute | solution.py:30
  210.1 5.9 %collective-permute-start = (s32[56]{0:T(128)S(1)}, s32[56]{0:T(128)S(1)}, u32[]{:S(2)}, u32[]{:S(2)}) collective-permute-start(s32[56]{0:T(128)S(1)} %copy-done.3), channel_id=1, source_target_pairs={{3,0},{4,1},{5,2},{6,3},{7,4},{0,5},{1,6},{2,7},{11,8},{12,9},{13,... | collective-permute-start | bytes 680 | tf_op jit(solution)/shard_map/ppermute | solution.py:30
  216.0 5.7 %copy-start = (f32[56,64,128]{2,1,0:T(8,128)S(1)}, f32[56,64,128]{2,1,0:T(8,128)}, u32[]{:S(2)}) copy-start(f32[56,64,128]{2,1,0:T(8,128)} %compact.4.refs_6_.refs_7_.refs_0_) | copy-start | bytes 5505028
  216.0 11.2 %copy-start.2 = (s32[2]{0:T(128)S(1)}, s32[2]{0:T(128)}, u32[]{:S(2)}) copy-start(s32[2]{0:T(128)} %pad_add_fusion.flags) | copy-start | bytes 28
  216.0 0.5 copy-start.4
  219.6 43.7 %collective-permute-start.2 = (f32[56,64,128]{2,1,0:T(8,128)}, f32[56,64,128]{2,1,0:T(8,128)}, u32[]{:S(2)}, u32[]{:S(2)}) collective-permute-start(f32[56,64,128]{2,1,0:T(8,128)} %compact.5.refs_10_.refs_11_.refs_4_), channel_id=1, source_target_pairs={{6,0},{7,1},{0,2},{1,3},{2,4},{3,5},{4,6},{5,7},{14,8},{15,9},{8,1... | collective-permute-start | bytes 5505032 | tf_op jit(solution)/shard_map/ppermute | solution.py:30
  221.7 43.5 %collective-permute-start.1 = (f32[56,64,128]{2,1,0:T(8,128)S(1)}, f32[56,64,128]{2,1,0:T(8,128)}, u32[]{:S(2)}, u32[]{:S(2)}) collective-permute-start(f32[56,64,128]{2,1,0:T(8,128)S(1)} %copy-done), channel_id=1, source_target_pairs={{2,0},{3,1},{4,2},{5,3},{6,4},{7,5},{0,6},{1,7},{10,8},{11,9},{12,... | collective-permute-start | bytes 5505032 | tf_op jit(solution)/shard_map/ppermute | solution.py:30
  291.5 36.5 %collective-permute-start.9 = (f32[56,128,128]{2,1,0:T(8,128)}, f32[56,128,128]{2,1,0:T(8,128)}, u32[]{:S(2)}, u32[]{:S(2)}) collective-permute-start(f32[56,128,128]{2,1,0:T(8,128)} %collective-permute-done.3.refs_5_.refs_6_), channel_id=1, source_target_pairs={{8,0},{9,1},{10,2},{11,3},{12,4},{13,5},{14,6},{15,7},{0,8},{1,9},... | collective-permute-start | bytes 11010056 | tf_op jit(solution)/shard_map/ppermute | solution.py:30
  291.5 31.6 %collective-permute-start.5 = (f32[2,20,64,128]{3,2,1,0:T(8,128)S(1)}, f32[2,20,64,128]{3,2,1,0:T(8,128)S(1)}, u32[]{:S(2)}, u32[]{:S(2)}) collective-permute-start(f32[2,20,64,128]{3,2,1,0:T(8,128)S(1)} %get-tuple-element.48), channel_id=1, source_target_pairs={{1,0},{0,1},{3,2},{2,3},{5,4},{4,5},{7,6},{6,7},{9,8},{8,9},{11,10... | collective-permute-start | bytes 3932168 | tf_op jit(solution)/shard_map/ppermute | solution.py:30
  293.2 58.1 %collective-permute-start.8 = (f32[2,20,64,128]{3,2,1,0:T(8,128)}, f32[2,20,64,128]{3,2,1,0:T(8,128)}, u32[]{:S(2)}, u32[]{:S(2)}) collective-permute-start(f32[2,20,64,128]{3,2,1,0:T(8,128)} %get-tuple-element.51), channel_id=1, source_target_pairs={{1,0},{0,1},{3,2},{2,3},{5,4},{4,5},{7,6},{6,7},{9,8},{8,9},{11,10... | collective-permute-start | bytes 3932168 | tf_op jit(solution)/shard_map/ppermute | solution.py:30
  293.5 65.2 %collective-permute-start.12 = (f32[56,128,128]{2,1,0:T(8,128)}, f32[56,128,128]{2,1,0:T(8,128)}, u32[]{:S(2)}, u32[]{:S(2)}) collective-permute-start(f32[56,128,128]{2,1,0:T(8,128)} %compact.3.refs_8_.refs_9_.refs_2_), channel_id=1, source_target_pairs={{32,8},{33,9},{34,10},{35,11},{36,12},{37,13},{38,14},{39,15},{48,... | collective-permute-start | bytes 11010056 | tf_op jit(solution)/shard_map/ppermute | solution.py:30
  323.1 6.1 %copy-start.1 = (f32[2,20,64,128]{3,2,1,0:T(8,128)}, f32[2,20,64,128]{3,2,1,0:T(8,128)S(1)}, u32[]{:S(2)}) copy-start(f32[2,20,64,128]{3,2,1,0:T(8,128)S(1)} %collective-permute-done.5.refs_0_) | copy-start | bytes 3932164
  323.1 48.6 %collective-permute-start.6 = (f32[16,64,128]{2,1,0:T(8,128)}, f32[16,64,128]{2,1,0:T(8,128)}, u32[]{:S(2)}, u32[]{:S(2)}) collective-permute-start(f32[16,64,128]{2,1,0:T(8,128)} %slice_select_fusion.5), channel_id=1, source_target_pairs={{1,0},{0,1},{3,2},{2,3},{5,4},{4,5},{7,6},{6,7},{9,8},{8,9},{11,10... | collective-permute-start | bytes 1572872 | tf_op jit(solution)/shard_map/ppermute | solution.py:30
  326.0 29.5 %collective-permute-start.10 = (f32[20,64,128]{2,1,0:T(8,128)}, f32[20,64,128]{2,1,0:T(8,128)}, u32[]{:S(2)}, u32[]{:S(2)}) collective-permute-start(f32[20,64,128]{2,1,0:T(8,128)} %get-tuple-element.68), channel_id=1, source_target_pairs={{6,0},{7,1},{0,2},{1,3},{2,4},{3,5},{4,6},{5,7},{14,8},{15,9},{8,1... | collective-permute-start | bytes 1966088 | tf_op jit(solution)/shard_map/ppermute | solution.py:30
  328.0 29.3 %collective-permute-start.11 = (f32[20,64,128]{2,1,0:T(8,128)}, f32[20,64,128]{2,1,0:T(8,128)}, u32[]{:S(2)}, u32[]{:S(2)}) collective-permute-start(f32[20,64,128]{2,1,0:T(8,128)} %get-tuple-element.67), channel_id=1, source_target_pairs={{2,0},{3,1},{4,2},{5,3},{6,4},{7,5},{0,6},{1,7},{10,8},{11,9},{12,... | collective-permute-start | bytes 1966088 | tf_op jit(solution)/shard_map/ppermute | solution.py:30
  351.3 22.1 %collective-permute-start.7 = (f32[16,64,128]{2,1,0:T(8,128)}, f32[16,64,128]{2,1,0:T(8,128)}, u32[]{:S(2)}, u32[]{:S(2)}) collective-permute-start(f32[16,64,128]{2,1,0:T(8,128)} %slice_select_fusion.4), channel_id=1, source_target_pairs={{1,0},{0,1},{3,2},{2,3},{5,4},{4,5},{7,6},{6,7},{9,8},{8,9},{11,10... | collective-permute-start | bytes 1572872 | tf_op jit(solution)/shard_map/ppermute | solution.py:30
  355.5 21.4 %collective-permute-start.15 = (f32[20,64,128]{2,1,0:T(8,128)}, f32[20,64,128]{2,1,0:T(8,128)}, u32[]{:S(2)}, u32[]{:S(2)}) collective-permute-start(f32[20,64,128]{2,1,0:T(8,128)} %get-tuple-element.66), channel_id=1, source_target_pairs={{6,0},{7,1},{0,2},{1,3},{2,4},{3,5},{4,6},{5,7},{14,8},{15,9},{8,1... | collective-permute-start | bytes 1966088 | tf_op jit(solution)/shard_map/ppermute | solution.py:30
  357.4 19.5 %collective-permute-start.16 = (f32[20,64,128]{2,1,0:T(8,128)}, f32[20,64,128]{2,1,0:T(8,128)}, u32[]{:S(2)}, u32[]{:S(2)}) collective-permute-start(f32[20,64,128]{2,1,0:T(8,128)} %get-tuple-element.65), channel_id=1, source_target_pairs={{2,0},{3,1},{4,2},{5,3},{6,4},{7,5},{0,6},{1,7},{10,8},{11,9},{12,... | collective-permute-start | bytes 1966088 | tf_op jit(solution)/shard_map/ppermute | solution.py:30
  373.4 15.1 %collective-permute-start.13 = (f32[16,64,128]{2,1,0:T(8,128)}, f32[16,64,128]{2,1,0:T(8,128)}, u32[]{:S(2)}, u32[]{:S(2)}) collective-permute-start(f32[16,64,128]{2,1,0:T(8,128)} %collective-permute-done.7.refs_5_), channel_id=1, source_target_pairs={{6,0},{7,1},{0,2},{1,3},{2,4},{3,5},{4,6},{5,7},{14,8},{15,9},{8,1... | collective-permute-start | bytes 1572872 | tf_op jit(solution)/shard_map/ppermute | solution.py:30
  376.9 13.6 %collective-permute-start.14 = (f32[16,64,128]{2,1,0:T(8,128)}, f32[16,64,128]{2,1,0:T(8,128)}, u32[]{:S(2)}, u32[]{:S(2)}) collective-permute-start(f32[16,64,128]{2,1,0:T(8,128)} %collective-permute-done.6.refs_0_), channel_id=1, source_target_pairs={{2,0},{3,1},{4,2},{5,3},{6,4},{7,5},{0,6},{1,7},{10,8},{11,9},{12,... | collective-permute-start | bytes 1572872 | tf_op jit(solution)/shard_map/ppermute | solution.py:30

commit v7 on v6

--- a/solution.py
+++ b/solution.py
@@ -11,7 +11,7 @@
 AHEAD = 3
 PIECES = 4
 SIZES = (20, 20, 16)
-GROUP = 4
+GROUPS = (8, 4, 2, 1)
 VMEM_LIMIT = 60 * 1024 * 1024
 
 ANY = pl.BlockSpec(memory_space=pl.ANY)
@@ -147,6 +147,20 @@
         preferred_element_type=jnp.float32,
     )
     return wide[:, :width] + wide[:, width:]
+
+
+def add_all(c_ref, product, count):
+    start = 0
+    for group in GROUPS:
+
+        def several(g, carry, group=group, start=start):
+            for m, value in [product(start + g * group + u) for u in range(group)]:
+                c_ref[m] += value
+            return carry
+
+        number = (count - start) // group
+        lax.fori_loop(0, number, several, 0)
+        start = start + number * group
 
 
 def rows_of(ref, spec):
@@ -206,26 +220,11 @@
         for copy in waits[n]:
             copy.wait()
 
-        def add(at, n=n, t=t, first=first, a_ref=a_ref, b_ref=b_ref):
-            e = live[n, at]
-            c_ref[index_c[t, e]] += block_product(a_ref[index_a[t, e] - first], b_ref[index_b[t, e]])
-
         def product(at, n=n, t=t, first=first, a_ref=a_ref, b_ref=b_ref):
             e = live[n, at]
             return index_c[t, e], block_product(a_ref[index_a[t, e] - first], b_ref[index_b[t, e]])
 
-        def several(g, carry, product=product):
-            for m, value in [product(g * GROUP + u) for u in range(GROUP)]:
-                c_ref[m] += value
-            return carry
-
-        def single(at, carry, add=add):
-            add(at)
-            return carry
-
-        groups = counts[n] // GROUP
-        lax.fori_loop(0, groups, several, 0)
-        lax.fori_loop(groups * GROUP, counts[n], single, 0)
+        add_all(c_ref, product, counts[n])
     out = pltpu.make_async_copy(c_ref, c_out, sem.at[len(jobs), 0])
     out.start()
     out.wait()
@@ -371,24 +370,10 @@
     for n in range(number):
         end = plan[5, n]
 
-        def add(at, a_ref=held[n]):
-            c_ref[plan[2, at]] += block_product(a_ref[plan[0, at]], b_ref[at])
-
         def product(at, a_ref=held[n]):
             return plan[2, at], block_product(a_ref[plan[0, at]], b_ref[at])
 
-        def several(g, carry, begin=begin, product=product):
-            for m, value in [product(begin + g * GROUP + u) for u in range(GROUP)]:
-                c_ref[m] += value
-            return carry
-
-        def single(at, carry, add=add):
-            add(at)
-            return carry
-
-        groups = (end - begin) // GROUP
-        lax.fori_loop(0, groups, several, 0)
-        lax.fori_loop(begin + groups * GROUP, end, single, 0)
+        add_all(c_ref, lambda at, begin=begin, product=product: product(begin + at), end - begin)
         begin = end
 
     def store(k, carry):

time: 398 us -> 397 us (level)
  transfers between devices with their start and end apart: 17 -> 17, of which waited for: 7 -> 7; matrix products, arithmetic and copies ran while one was open for 3% -> 3% of each run, Pallas kernels for 11% -> 10%
where the time goes in v7:
time: 397 us; the launch traced here: 396 us
  blocking collectives  199 us (50%)
  waiting for transfers between devices  98.8 us (25%)
  Pallas kernels  57.1 us (14%)
  starting transfers between devices  26.3 us (7%)
  other arithmetic  9.31 us (2%)
  local copies, waits for them, and re-layouts  4.83 us (1%)
    all_to_all x1, blocking collectives, local(): lax.all_to_all(outgoing, ('row', 'col'), split_axis=0, concat_axis=0, til...  199 us
    ppermute x17, waiting for transfers between devices, permute(): return lax.ppermute(array, ('row', 'col'), pairs)  98.8 us
    pallas_call x3, Pallas kernels, products(): pl.pallas_call(functools.partial(products_kernel, tuple(static), has_c),...  31.1 us
    ppermute x17, starting transfers between devices, permute(): return lax.ppermute(array, ('row', 'col'), pairs)  26.3 us
    pallas_call x3, Pallas kernels, compact(): pl.pallas_call(functools.partial(compact_kernel, tuple(parts)), out_shape...  9.97 us
  transfers between devices with their start and end apart: 17, of which 7 were waited for; matrix products, arithmetic and copies ran while one was open for 3% of the time, Pallas kernels for 10%

profile of v7, /device:TPU:0, one launch (start us, length us, event | category | flops | bytes accessed | tf_op | source)
XLA Modules:
  0.0 396.3 jit_solution(1605533030421675386)
XLA Ops:
  0.0 0.6 pad_add_fusion.flags
  0.6 6.0 %fill.1 = f32[128,2,128,128]{3,2,1,0:T(8,128)} custom-call(s32[128]{0:T(128)} %a_pick.1, s32[128]{0:T(128)} %b_pick.1, s32[4,64]{1,0:T(4,128)} %index_a.7, s32[4,64]{1,0:T(4,128)} %index_b.7, s32[4,64]{1,0:T(4,128)} %index_c.7, s32[2]{0:T(128)} %pad_add_fusion.flags, f32[56,128,128]{2,1,0:T(8,128)} %a_blocks.1, f32[56,128,128]{2,1,0:T(8,128)} %b_blocks.1), custom_call_target="tpu_custom_call" | custom-call | bytes 14680064 | tf_op jit(solution)/shard_map/fill/pallas_call | solution.py:74
  6.6 199.0 %all_to_all.5.refs_1_ = f32[128,2,128,128]{3,2,1,0:T(8,128)} all-to-all(f32[128,2,128,128]{3,2,1,0:T(8,128)} %fill.1), channel_id=1, replica_groups=mesh['row'=16,'col'=8] {'row','col'}, dimensions={0} | all-to-all | bytes 33554432 | tf_op jit(solution)/shard_map/all_to_all | solution.py:430
  205.6 3.9 compact.3.refs_8_.refs_9_.refs_2_
  209.5 0.5 collective-permute-start.3
  210.0 0.1 collective-permute-start.4
  210.1 2.9 collective-permute-start
  212.9 3.0 compact.4.refs_6_.refs_7_.refs_0_
  216.0 0.0 collective-permute-done.refs_0_
  216.0 0.0 copy-start.4
  216.0 0.5 copy-done.4
  216.5 3.1 compact.5.refs_10_.refs_11_.refs_4_
  219.6 2.1 collective-permute-start.2
  221.7 1.2 collective-permute-start.1
  222.9 4.2 %plan.1 = s32[6,128]{1,0:T(8,128)} custom-call(s32[4,64]{1,0:T(4,128)} %index_a.7, s32[4,64]{1,0:T(4,128)} %index_b.7, s32[4,64]{1,0:T(4,128)} %index_c.7), custom_call_target="tpu_custom_call" | custom-call | tf_op jit(solution)/shard_map/plan/pallas_call | solution.py:315
  227.2 0.6 slice.51
  228.4 35.0 %collective-permute-done.2.refs_1_ = f32[56,64,128]{2,1,0:T(8,128)} collective-permute-done((f32[56,64,128]{2,1,0:T(8,128)}, f32[56,64,128]{2,1,0:T(8,128)}, u32[]{:S(2)}, u32[]{:S(2)}) %collective-permute-start.2) | collective-permute-done | bytes 1835040 | tf_op jit(solution)/shard_map/ppermute | solution.py:30
  263.3 1.9 fusion
  265.2 1.5 fusion.1
  266.7 1.4 pad_maximum_fusion
  268.1 1.9 slice_select_fusion.5
  270.0 2.1 slice_select_fusion.4
  272.1 19.4 %collective-permute-done.3.refs_5_.refs_6_ = f32[56,128,128]{2,1,0:T(8,128)} collective-permute-done((f32[56,128,128]{2,1,0:T(8,128)}, f32[56,128,128]{2,1,0:T(8,128)}, u32[]{:S(2)}, u32[]{:S(2)}) %collective-permute-start.3) | collective-permute-done | bytes 3670048 | tf_op jit(solution)/shard_map/ppermute | solution.py:30
  291.5 0.0 collective-permute-done.4.refs_2_
  291.5 0.0 collective-permute-start.9
  291.5 1.7 collective-permute-start.5
  293.2 0.3 collective-permute-start.8
  293.5 4.2 %collective-permute-start.12 = (f32[56,128,128]{2,1,0:T(8,128)}, f32[56,128,128]{2,1,0:T(8,128)}, u32[]{:S(2)}, u32[]{:S(2)}) collective-permute-start(f32[56,128,128]{2,1,0:T(8,128)} %compact.3.refs_8_.refs_9_.refs_2_), channel_id=1, source_target_pairs={{32,8},{33,9},{34,10},{35,11},{36,12},{37,13},{38,14},{39,15},{48,... | collective-permute-start | bytes 11010056 | tf_op jit(solution)/shard_map/ppermute | solution.py:30
  297.7 25.4 %collective-permute-done.5.refs_0_ = f32[2,20,64,128]{3,2,1,0:T(8,128)S(1)} collective-permute-done((f32[2,20,64,128]{3,2,1,0:T(8,128)S(1)}, f32[2,20,64,128]{3,2,1,0:T(8,128)S(1)}, u32[]{:S(2)}, u32[]{:S(2)}) %collective-permute-start.5) | collective-permute-done | bytes 1310752 | tf_op jit(solution)/shard_map/ppermute | solution.py:30
  323.1 1.7 collective-permute-start.6
  324.7 1.2 slice_bitcast_fusion.2
  326.0 2.0 collective-permute-start.10
  328.0 0.0 collective-permute-done.9.refs_3_.refs_5_
  328.0 1.2 collective-permute-start.11
  329.2 8.1 %products.3.refs_12_ = f32[64,128,128]{2,1,0:T(8,128)} custom-call(s32[2]{0:T(128)} %pad_add_fusion.flags, s32[4,64]{1,0:T(4,128)} %index_a.7, s32[4,64]{1,0:T(4,128)} %index_b.7, s32[4,64]{1,0:T(4,128)} %index_c.7, f32[2,20,64,128]{3,2,1,0:T(8,128)} %copy-done.1, f32[56,64,128]{2,1,0:T(8,128)} %collective-permute-done.2.refs_1_, ...), custom_call_target="tpu_custom_call" | custom-call | flops 805306368000 | bytes 8388608 | tf_op jit(solution)/shard_map/products/pallas_call | solution.py:257
  337.3 13.9 %collective-permute-done.8.refs_0_ = f32[2,20,64,128]{3,2,1,0:T(8,128)} collective-permute-done((f32[2,20,64,128]{3,2,1,0:T(8,128)}, f32[2,20,64,128]{3,2,1,0:T(8,128)}, u32[]{:S(2)}, u32[]{:S(2)}) %collective-permute-start.8) | collective-permute-done | bytes 1310752 | tf_op jit(solution)/shard_map/ppermute | solution.py:30
  351.2 1.7 collective-permute-start.7
  352.9 2.5 slice_bitcast_fusion
  355.4 0.0 collective-permute-done.10.refs_7_
  355.4 1.9 collective-permute-start.15
  357.3 1.4 collective-permute-start.16
  358.7 11.7 %products.4.refs_13_ = f32[64,128,128]{2,1,0:T(8,128)} custom-call(s32[2]{0:T(128)} %pad_add_fusion.flags, s32[4,64]{1,0:T(4,128)} %index_a.7, s32[4,64]{1,0:T(4,128)} %index_b.7, s32[4,64]{1,0:T(4,128)} %index_c.7, f32[2,20,64,128]{3,2,1,0:T(8,128)} %collective-permute-done.8.refs_0_, ...), custom_call_target="tpu_custom_call", output_to_operand_aliasing={{}: (16, {})} | custom-call | flops 805306368000 | bytes 8388608 | tf_op jit(solution)/shard_map/products/pallas_call | solution.py:257
  370.4 3.0 collective-permute-done.7.refs_5_
  373.3 3.5 collective-permute-start.13
  376.8 11.3 %products.5.refs_7_ = f32[64,128,128]{2,1,0:T(8,128)} custom-call(s32[2]{0:T(128)} %pad_add_fusion.flags, s32[4,64]{1,0:T(4,128)} %index_a.7, s32[4,64]{1,0:T(4,128)} %index_b.7, s32[4,64]{1,0:T(4,128)} %index_c.7, f32[16,64,128]{2,1,0:T(8,128)} %collective-permute-done.6.refs_0_, ...), custom_call_target="tpu_custom_call", output_to_operand_aliasing={{}: (17, {})} | custom-call | flops 805306368000 | bytes 8388608 | tf_op jit(solution)/shard_map/products/pallas_call | solution.py:257
  388.2 0.2 collective-permute-done.13.refs_1_
  388.4 2.0 collective-permute-done.14.refs_3_
  390.4 5.7 %last_products.1 = f32[64,128,128]{2,1,0:T(8,128)} custom-call(s32[2]{0:T(128)} %pad_add_fusion.flags, s32[6,128]{1,0:T(8,128)} %plan.1, f32[56,64,128]{2,1,0:T(8,128)} %compact.4.refs_6_.refs_7_.refs_0_, f32[16,64,128]{2,1,0:T(8,128)} %collective-permute-done.13.refs_1_, ...), custom_call_target="tpu_custom_call", output_to_operand_aliasing={{}: (9, {})} | custom-call | flops 805306368000 | bytes 8388608 | tf_op jit(solution)/shard_map/last_products/pallas_call | solution.py:401
  (15 shorter events, 0.0 us)
Async XLA Ops:
  205.6 4.4 %copy-start.3 = (s32[56]{0:T(128)S(1)}, s32[56]{0:T(128)}, u32[]{:S(2)}) copy-start(s32[56]{0:T(128)} %refs_0_.2) | copy-start | bytes 676
  209.5 82.0 %collective-permute-start.3 = (f32[56,128,128]{2,1,0:T(8,128)}, f32[56,128,128]{2,1,0:T(8,128)}, u32[]{:S(2)}, u32[]{:S(2)}) collective-permute-start(f32[56,128,128]{2,1,0:T(8,128)} %compact.3.refs_8_.refs_9_.refs_2_), channel_id=1, source_target_pairs={{16,0},{17,1},{18,2},{19,3},{20,4},{21,5},{22,6},{23,7},{24,8},{25... | collective-permute-start | bytes 11010056 | tf_op jit(solution)/shard_map/ppermute | solution.py:30
  210.0 81.5 %collective-permute-start.4 = (f32[56,128,128]{2,1,0:T(8,128)}, f32[56,128,128]{2,1,0:T(8,128)}, u32[]{:S(2)}, u32[]{:S(2)}) collective-permute-start(f32[56,128,128]{2,1,0:T(8,128)} %compact.3.refs_8_.refs_9_.refs_2_), channel_id=1, source_target_pairs={{8,0},{9,1},{10,2},{11,3},{12,4},{13,5},{14,6},{15,7},{0,8},{1,9},... | collective-permute-start | bytes 11010056 | tf_op jit(solution)/shard_map/ppermute | solution.py:30
  210.1 5.9 %collective-permute-start = (s32[56]{0:T(128)S(1)}, s32[56]{0:T(128)S(1)}, u32[]{:S(2)}, u32[]{:S(2)}) collective-permute-start(s32[56]{0:T(128)S(1)} %copy-done.3), channel_id=1, source_target_pairs={{3,0},{4,1},{5,2},{6,3},{7,4},{0,5},{1,6},{2,7},{11,8},{12,9},{13,... | collective-permute-start | bytes 680 | tf_op jit(solution)/shard_map/ppermute | solution.py:30
  216.0 5.7 %copy-start = (f32[56,64,128]{2,1,0:T(8,128)S(1)}, f32[56,64,128]{2,1,0:T(8,128)}, u32[]{:S(2)}) copy-start(f32[56,64,128]{2,1,0:T(8,128)} %compact.4.refs_6_.refs_7_.refs_0_) | copy-start | bytes 5505028
  216.0 11.2 %copy-start.2 = (s32[2]{0:T(128)S(1)}, s32[2]{0:T(128)}, u32[]{:S(2)}) copy-start(s32[2]{0:T(128)} %pad_add_fusion.flags) | copy-start | bytes 28
  216.0 0.5 copy-start.4
  219.6 43.7 %collective-permute-start.2 = (f32[56,64,128]{2,1,0:T(8,128)}, f32[56,64,128]{2,1,0:T(8,128)}, u32[]{:S(2)}, u32[]{:S(2)}) collective-permute-start(f32[56,64,128]{2,1,0:T(8,128)} %compact.5.refs_10_.refs_11_.refs_4_), channel_id=1, source_target_pairs={{6,0},{7,1},{0,2},{1,3},{2,4},{3,5},{4,6},{5,7},{14,8},{15,9},{8,1... | collective-permute-start | bytes 5505032 | tf_op jit(solution)/shard_map/ppermute | solution.py:30
  221.7 43.5 %collective-permute-start.1 = (f32[56,64,128]{2,1,0:T(8,128)S(1)}, f32[56,64,128]{2,1,0:T(8,128)}, u32[]{:S(2)}, u32[]{:S(2)}) collective-permute-start(f32[56,64,128]{2,1,0:T(8,128)S(1)} %copy-done), channel_id=1, source_target_pairs={{2,0},{3,1},{4,2},{5,3},{6,4},{7,5},{0,6},{1,7},{10,8},{11,9},{12,... | collective-permute-start | bytes 5505032 | tf_op jit(solution)/shard_map/ppermute | solution.py:30
  291.5 36.5 %collective-permute-start.9 = (f32[56,128,128]{2,1,0:T(8,128)}, f32[56,128,128]{2,1,0:T(8,128)}, u32[]{:S(2)}, u32[]{:S(2)}) collective-permute-start(f32[56,128,128]{2,1,0:T(8,128)} %collective-permute-done.3.refs_5_.refs_6_), channel_id=1, source_target_pairs={{8,0},{9,1},{10,2},{11,3},{12,4},{13,5},{14,6},{15,7},{0,8},{1,9},... | collective-permute-start | bytes 11010056 | tf_op jit(solution)/shard_map/ppermute | solution.py:30
  291.5 31.6 %collective-permute-start.5 = (f32[2,20,64,128]{3,2,1,0:T(8,128)S(1)}, f32[2,20,64,128]{3,2,1,0:T(8,128)S(1)}, u32[]{:S(2)}, u32[]{:S(2)}) collective-permute-start(f32[2,20,64,128]{3,2,1,0:T(8,128)S(1)} %get-tuple-element.48), channel_id=1, source_target_pairs={{1,0},{0,1},{3,2},{2,3},{5,4},{4,5},{7,6},{6,7},{9,8},{8,9},{11,10... | collective-permute-start | bytes 3932168 | tf_op jit(solution)/shard_map/ppermute | solution.py:30
  293.2 58.1 %collective-permute-start.8 = (f32[2,20,64,128]{3,2,1,0:T(8,128)}, f32[2,20,64,128]{3,2,1,0:T(8,128)}, u32[]{:S(2)}, u32[]{:S(2)}) collective-permute-start(f32[2,20,64,128]{3,2,1,0:T(8,128)} %get-tuple-element.51), channel_id=1, source_target_pairs={{1,0},{0,1},{3,2},{2,3},{5,4},{4,5},{7,6},{6,7},{9,8},{8,9},{11,10... | collective-permute-start | bytes 3932168 | tf_op jit(solution)/shard_map/ppermute | solution.py:30
  293.5 65.2 %collective-permute-start.12 = (f32[56,128,128]{2,1,0:T(8,128)}, f32[56,128,128]{2,1,0:T(8,128)}, u32[]{:S(2)}, u32[]{:S(2)}) collective-permute-start(f32[56,128,128]{2,1,0:T(8,128)} %compact.3.refs_8_.refs_9_.refs_2_), channel_id=1, source_target_pairs={{32,8},{33,9},{34,10},{35,11},{36,12},{37,13},{38,14},{39,15},{48,... | collective-permute-start | bytes 11010056 | tf_op jit(solution)/shard_map/ppermute | solution.py:30
  323.1 6.1 %copy-start.1 = (f32[2,20,64,128]{3,2,1,0:T(8,128)}, f32[2,20,64,128]{3,2,1,0:T(8,128)S(1)}, u32[]{:S(2)}) copy-start(f32[2,20,64,128]{3,2,1,0:T(8,128)S(1)} %collective-permute-done.5.refs_0_) | copy-start | bytes 3932164
  323.1 47.3 %collective-permute-start.6 = (f32[16,64,128]{2,1,0:T(8,128)}, f32[16,64,128]{2,1,0:T(8,128)}, u32[]{:S(2)}, u32[]{:S(2)}) collective-permute-start(f32[16,64,128]{2,1,0:T(8,128)} %slice_select_fusion.5), channel_id=1, source_target_pairs={{1,0},{0,1},{3,2},{2,3},{5,4},{4,5},{7,6},{6,7},{9,8},{8,9},{11,10... | collective-permute-start | bytes 1572872 | tf_op jit(solution)/shard_map/ppermute | solution.py:30
  326.0 29.5 %collective-permute-start.10 = (f32[20,64,128]{2,1,0:T(8,128)}, f32[20,64,128]{2,1,0:T(8,128)}, u32[]{:S(2)}, u32[]{:S(2)}) collective-permute-start(f32[20,64,128]{2,1,0:T(8,128)} %get-tuple-element.68), channel_id=1, source_target_pairs={{6,0},{7,1},{0,2},{1,3},{2,4},{3,5},{4,6},{5,7},{14,8},{15,9},{8,1... | collective-permute-start | bytes 1966088 | tf_op jit(solution)/shard_map/ppermute | solution.py:30
  328.0 29.3 %collective-permute-start.11 = (f32[20,64,128]{2,1,0:T(8,128)}, f32[20,64,128]{2,1,0:T(8,128)}, u32[]{:S(2)}, u32[]{:S(2)}) collective-permute-start(f32[20,64,128]{2,1,0:T(8,128)} %get-tuple-element.67), channel_id=1, source_target_pairs={{2,0},{3,1},{4,2},{5,3},{6,4},{7,5},{0,6},{1,7},{10,8},{11,9},{12,... | collective-permute-start | bytes 1966088 | tf_op jit(solution)/shard_map/ppermute | solution.py:30
  351.2 22.1 %collective-permute-start.7 = (f32[16,64,128]{2,1,0:T(8,128)}, f32[16,64,128]{2,1,0:T(8,128)}, u32[]{:S(2)}, u32[]{:S(2)}) collective-permute-start(f32[16,64,128]{2,1,0:T(8,128)} %slice_select_fusion.4), channel_id=1, source_target_pairs={{1,0},{0,1},{3,2},{2,3},{5,4},{4,5},{7,6},{6,7},{9,8},{8,9},{11,10... | collective-permute-start | bytes 1572872 | tf_op jit(solution)/shard_map/ppermute | solution.py:30
  355.4 21.4 %collective-permute-start.15 = (f32[20,64,128]{2,1,0:T(8,128)}, f32[20,64,128]{2,1,0:T(8,128)}, u32[]{:S(2)}, u32[]{:S(2)}) collective-permute-start(f32[20,64,128]{2,1,0:T(8,128)} %get-tuple-element.66), channel_id=1, source_target_pairs={{6,0},{7,1},{0,2},{1,3},{2,4},{3,5},{4,6},{5,7},{14,8},{15,9},{8,1... | collective-permute-start | bytes 1966088 | tf_op jit(solution)/shard_map/ppermute | solution.py:30
  357.3 19.5 %collective-permute-start.16 = (f32[20,64,128]{2,1,0:T(8,128)}, f32[20,64,128]{2,1,0:T(8,128)}, u32[]{:S(2)}, u32[]{:S(2)}) collective-permute-start(f32[20,64,128]{2,1,0:T(8,128)} %get-tuple-element.65), channel_id=1, source_target_pairs={{2,0},{3,1},{4,2},{5,3},{6,4},{7,5},{0,6},{1,7},{10,8},{11,9},{12,... | collective-permute-start | bytes 1966088 | tf_op jit(solution)/shard_map/ppermute | solution.py:30
  373.3 15.1 %collective-permute-start.13 = (f32[16,64,128]{2,1,0:T(8,128)}, f32[16,64,128]{2,1,0:T(8,128)}, u32[]{:S(2)}, u32[]{:S(2)}) collective-permute-start(f32[16,64,128]{2,1,0:T(8,128)} %collective-permute-done.7.refs_5_), channel_id=1, source_target_pairs={{6,0},{7,1},{0,2},{1,3},{2,4},{3,5},{4,6},{5,7},{14,8},{15,9},{8,1... | collective-permute-start | bytes 1572872 | tf_op jit(solution)/shard_map/ppermute | solution.py:30
  376.8 13.6 %collective-permute-start.14 = (f32[16,64,128]{2,1,0:T(8,128)}, f32[16,64,128]{2,1,0:T(8,128)}, u32[]{:S(2)}, u32[]{:S(2)}) collective-permute-start(f32[16,64,128]{2,1,0:T(8,128)} %collective-permute-done.6.refs_0_), channel_id=1, source_target_pairs={{2,0},{3,1},{4,2},{5,3},{6,4},{7,5},{0,6},{1,7},{10,8},{11,9},{12,... | collective-permute-start | bytes 1572872 | tf_op jit(solution)/shard_map/ppermute | solution.py:30

commit v8 on v7

--- a/solution.py
+++ b/solution.py
@@ -9,7 +9,7 @@
 
 CBLK = 64
 AHEAD = 3
-PIECES = 4
+PIECES = 8
 SIZES = (20, 20, 16)
 GROUPS = (8, 4, 2, 1)
 VMEM_LIMIT = 60 * 1024 * 1024

time: 397 us -> 398 us (level)
  transfers between devices with their start and end apart: 17 -> 17, of which waited for: 7 -> 6; matrix products, arithmetic and copies ran while one was open for 3% -> 3% of each run, Pallas kernels for 10% -> 10%
where the time goes in v8:
time: 398 us; the launch traced here: 396 us
  blocking collectives  199 us (50%)
  waiting for transfers between devices  98.9 us (25%)
  Pallas kernels  56.7 us (14%)
  starting transfers between devices  26.3 us (7%)
  other arithmetic  9.31 us (2%)
  local copies, waits for them, and re-layouts  4.83 us (1%)
    all_to_all x1, blocking collectives, local(): lax.all_to_all(outgoing, ('row', 'col'), split_axis=0, concat_axis=0, til...  199 us
    ppermute x17, waiting for transfers between devices, permute(): return lax.ppermute(array, ('row', 'col'), pairs)  98.9 us
    pallas_call x3, Pallas kernels, products(): pl.pallas_call(functools.partial(products_kernel, tuple(static), has_c),...  31.1 us
    ppermute x17, starting transfers between devices, permute(): return lax.ppermute(array, ('row', 'col'), pairs)  26.3 us
    pallas_call x3, Pallas kernels, compact(): pl.pallas_call(functools.partial(compact_kernel, tuple(parts)), out_shape...  10.2 us
  transfers between devices with their start and end apart: 17, of which 6 were waited for; matrix products, arithmetic and copies ran while one was open for 3% of the time, Pallas kernels for 10%

profile of v8, /device:TPU:0, one launch (start us, length us, event | category | flops | bytes accessed | tf_op | source)
XLA Modules:
  0.0 396.0 jit_solution(892255039726186428)
XLA Ops:
  0.0 0.6 pad_add_fusion.flags
  0.6 6.1 %fill.1 = f32[128,2,128,128]{3,2,1,0:T(8,128)} custom-call(s32[128]{0:T(128)} %a_pick.1, s32[128]{0:T(128)} %b_pick.1, s32[4,64]{1,0:T(4,128)} %index_a.7, s32[4,64]{1,0:T(4,128)} %index_b.7, s32[4,64]{1,0:T(4,128)} %index_c.7, s32[2]{0:T(128)} %pad_add_fusion.flags, f32[56,128,128]{2,1,0:T(8,128)} %a_blocks.1, f32[56,128,128]{2,1,0:T(8,128)} %b_blocks.1), custom_call_target="tpu_custom_call" | custom-call | bytes 14680064 | tf_op jit(solution)/shard_map/fill/pallas_call | solution.py:74
  6.7 199.0 %all_to_all.5.refs_1_ = f32[128,2,128,128]{3,2,1,0:T(8,128)} all-to-all(f32[128,2,128,128]{3,2,1,0:T(8,128)} %fill.1), channel_id=1, replica_groups=mesh['row'=16,'col'=8] {'row','col'}, dimensions={0} | all-to-all | bytes 33554432 | tf_op jit(solution)/shard_map/all_to_all | solution.py:430
  205.7 4.1 %compact.3.refs_8_.refs_9_.refs_2_ = f32[56,128,128]{2,1,0:T(8,128)} custom-call(s32[56]{0:T(128)} %refs_0_.1, f32[128,2,128,128]{3,2,1,0:T(8,128)} %all_to_all.5.refs_1_), custom_call_target="tpu_custom_call" | custom-call | flops 99999997952 | bytes 16777216 | tf_op jit(solution)/shard_map/compact/pallas_call | solution.py:119
  209.8 0.5 collective-permute-start.3
  210.3 0.1 collective-permute-start.4
  210.4 2.9 collective-permute-start
  213.2 3.0 compact.4.refs_6_.refs_7_.refs_0_
  216.3 0.0 collective-permute-done.refs_0_
  216.3 0.0 copy-start.4
  216.3 0.5 copy-done.4
  216.8 3.1 compact.5.refs_10_.refs_11_.refs_4_
  219.9 2.1 collective-permute-start.2
  222.0 1.2 collective-permute-start.1
  223.2 4.2 %plan.1 = s32[6,128]{1,0:T(8,128)} custom-call(s32[4,64]{1,0:T(4,128)} %index_a.7, s32[4,64]{1,0:T(4,128)} %index_b.7, s32[4,64]{1,0:T(4,128)} %index_c.7), custom_call_target="tpu_custom_call" | custom-call | tf_op jit(solution)/shard_map/plan/pallas_call | solution.py:315
  227.5 0.6 slice.51
  228.7 34.9 %collective-permute-done.2.refs_1_ = f32[56,64,128]{2,1,0:T(8,128)} collective-permute-done((f32[56,64,128]{2,1,0:T(8,128)}, f32[56,64,128]{2,1,0:T(8,128)}, u32[]{:S(2)}, u32[]{:S(2)}) %collective-permute-start.2) | collective-permute-done | bytes 1835040 | tf_op jit(solution)/shard_map/ppermute | solution.py:30
  263.7 1.9 fusion
  265.5 1.5 fusion.1
  267.0 1.4 pad_maximum_fusion
  268.4 1.9 slice_select_fusion.5
  270.3 2.1 slice_select_fusion.4
  272.4 19.4 %collective-permute-done.3.refs_5_.refs_6_ = f32[56,128,128]{2,1,0:T(8,128)} collective-permute-done((f32[56,128,128]{2,1,0:T(8,128)}, f32[56,128,128]{2,1,0:T(8,128)}, u32[]{:S(2)}, u32[]{:S(2)}) %collective-permute-start.3) | collective-permute-done | bytes 3670048 | tf_op jit(solution)/shard_map/ppermute | solution.py:30
  291.8 1.7 collective-permute-start.5
  293.5 0.3 collective-permute-start.8
  293.8 4.2 %collective-permute-start.12 = (f32[56,128,128]{2,1,0:T(8,128)}, f32[56,128,128]{2,1,0:T(8,128)}, u32[]{:S(2)}, u32[]{:S(2)}) collective-permute-start(f32[56,128,128]{2,1,0:T(8,128)} %compact.3.refs_8_.refs_9_.refs_2_), channel_id=1, source_target_pairs={{32,8},{33,9},{34,10},{35,11},{36,12},{37,13},{38,14},{39,15},{48,... | collective-permute-start | bytes 11010056 | tf_op jit(solution)/shard_map/ppermute | solution.py:30
  298.0 25.4 %collective-permute-done.5.refs_0_ = f32[2,20,64,128]{3,2,1,0:T(8,128)S(1)} collective-permute-done((f32[2,20,64,128]{3,2,1,0:T(8,128)S(1)}, f32[2,20,64,128]{3,2,1,0:T(8,128)S(1)}, u32[]{:S(2)}, u32[]{:S(2)}) %collective-permute-start.5) | collective-permute-done | bytes 1310752 | tf_op jit(solution)/shard_map/ppermute | solution.py:30
  323.4 1.7 collective-permute-start.6
  325.0 1.2 slice_bitcast_fusion.2
  326.3 2.0 collective-permute-start.10
  328.3 1.2 collective-permute-start.11
  329.5 7.7 %products.3.refs_12_ = f32[64,128,128]{2,1,0:T(8,128)} custom-call(s32[2]{0:T(128)} %pad_add_fusion.flags, s32[4,64]{1,0:T(4,128)} %index_a.7, s32[4,64]{1,0:T(4,128)} %index_b.7, s32[4,64]{1,0:T(4,128)} %index_c.7, f32[2,20,64,128]{3,2,1,0:T(8,128)} %copy-done.1, f32[56,64,128]{2,1,0:T(8,128)} %collective-permute-done.2.refs_1_, ...), custom_call_target="tpu_custom_call" | custom-call | flops 805306368000 | bytes 8388608 | tf_op jit(solution)/shard_map/products/pallas_call | solution.py:257
  337.2 14.4 %collective-permute-done.8.refs_0_ = f32[2,20,64,128]{3,2,1,0:T(8,128)} collective-permute-done((f32[2,20,64,128]{3,2,1,0:T(8,128)}, f32[2,20,64,128]{3,2,1,0:T(8,128)}, u32[]{:S(2)}, u32[]{:S(2)}) %collective-permute-start.8) | collective-permute-done | bytes 1310752 | tf_op jit(solution)/shard_map/ppermute | solution.py:30
  351.6 1.7 collective-permute-start.7
  353.2 2.5 slice_bitcast_fusion
  355.7 0.0 collective-permute-done.10.refs_7_
  355.7 1.9 collective-permute-start.15
  357.6 0.0 collective-permute-done.11.refs_9_
  357.6 1.4 collective-permute-start.16
  359.0 11.8 %products.4.refs_13_ = f32[64,128,128]{2,1,0:T(8,128)} custom-call(s32[2]{0:T(128)} %pad_add_fusion.flags, s32[4,64]{1,0:T(4,128)} %index_a.7, s32[4,64]{1,0:T(4,128)} %index_b.7, s32[4,64]{1,0:T(4,128)} %index_c.7, f32[2,20,64,128]{3,2,1,0:T(8,128)} %collective-permute-done.8.refs_0_, ...), custom_call_target="tpu_custom_call", output_to_operand_aliasing={{}: (16, {})} | custom-call | flops 805306368000 | bytes 8388608 | tf_op jit(solution)/shard_map/products/pallas_call | solution.py:257
  370.8 0.0 collective-permute-done.6.refs_0_
  370.8 2.8 collective-permute-done.7.refs_5_
  373.6 3.5 collective-permute-start.13
  377.1 0.0 collective-permute-start.14
  377.2 11.6 %products.5.refs_7_ = f32[64,128,128]{2,1,0:T(8,128)} custom-call(s32[2]{0:T(128)} %pad_add_fusion.flags, s32[4,64]{1,0:T(4,128)} %index_a.7, s32[4,64]{1,0:T(4,128)} %index_b.7, s32[4,64]{1,0:T(4,128)} %index_c.7, f32[16,64,128]{2,1,0:T(8,128)} %collective-permute-done.6.refs_0_, ...), custom_call_target="tpu_custom_call", output_to_operand_aliasing={{}: (17, {})} | custom-call | flops 805306368000 | bytes 8388608 | tf_op jit(solution)/shard_map/products/pallas_call | solution.py:257
  388.7 0.0 collective-permute-done.13.refs_1_
  388.7 2.0 collective-permute-done.14.refs_3_
  390.8 5.1 %last_products.1 = f32[64,128,128]{2,1,0:T(8,128)} custom-call(s32[2]{0:T(128)} %pad_add_fusion.flags, s32[6,128]{1,0:T(8,128)} %plan.1, f32[56,64,128]{2,1,0:T(8,128)} %compact.4.refs_6_.refs_7_.refs_0_, f32[16,64,128]{2,1,0:T(8,128)} %collective-permute-done.13.refs_1_, ...), custom_call_target="tpu_custom_call", output_to_operand_aliasing={{}: (9, {})} | custom-call | flops 805306368000 | bytes 8388608 | tf_op jit(solution)/shard_map/last_products/pallas_call | solution.py:401
  (15 shorter events, 0.0 us)
Async XLA Ops:
  205.7 4.7 %copy-start.3 = (s32[56]{0:T(128)S(1)}, s32[56]{0:T(128)}, u32[]{:S(2)}) copy-start(s32[56]{0:T(128)} %refs_0_.2) | copy-start | bytes 676
  209.8 82.0 %collective-permute-start.3 = (f32[56,128,128]{2,1,0:T(8,128)}, f32[56,128,128]{2,1,0:T(8,128)}, u32[]{:S(2)}, u32[]{:S(2)}) collective-permute-start(f32[56,128,128]{2,1,0:T(8,128)} %compact.3.refs_8_.refs_9_.refs_2_), channel_id=1, source_target_pairs={{16,0},{17,1},{18,2},{19,3},{20,4},{21,5},{22,6},{23,7},{24,8},{25... | collective-permute-start | bytes 11010056 | tf_op jit(solution)/shard_map/ppermute | solution.py:30
  210.3 81.5 %collective-permute-start.4 = (f32[56,128,128]{2,1,0:T(8,128)}, f32[56,128,128]{2,1,0:T(8,128)}, u32[]{:S(2)}, u32[]{:S(2)}) collective-permute-start(f32[56,128,128]{2,1,0:T(8,128)} %compact.3.refs_8_.refs_9_.refs_2_), channel_id=1, source_target_pairs={{8,0},{9,1},{10,2},{11,3},{12,4},{13,5},{14,6},{15,7},{0,8},{1,9},... | collective-permute-start | bytes 11010056 | tf_op jit(solution)/shard_map/ppermute | solution.py:30
  210.4 5.9 %collective-permute-start = (s32[56]{0:T(128)S(1)}, s32[56]{0:T(128)S(1)}, u32[]{:S(2)}, u32[]{:S(2)}) collective-permute-start(s32[56]{0:T(128)S(1)} %copy-done.3), channel_id=1, source_target_pairs={{3,0},{4,1},{5,2},{6,3},{7,4},{0,5},{1,6},{2,7},{11,8},{12,9},{13,... | collective-permute-start | bytes 680 | tf_op jit(solution)/shard_map/ppermute | solution.py:30
  216.3 5.7 %copy-start = (f32[56,64,128]{2,1,0:T(8,128)S(1)}, f32[56,64,128]{2,1,0:T(8,128)}, u32[]{:S(2)}) copy-start(f32[56,64,128]{2,1,0:T(8,128)} %compact.4.refs_6_.refs_7_.refs_0_) | copy-start | bytes 5505028
  216.3 11.2 %copy-start.2 = (s32[2]{0:T(128)S(1)}, s32[2]{0:T(128)}, u32[]{:S(2)}) copy-start(s32[2]{0:T(128)} %pad_add_fusion.flags) | copy-start | bytes 28
  216.3 0.5 copy-start.4
  219.9 43.7 %collective-permute-start.2 = (f32[56,64,128]{2,1,0:T(8,128)}, f32[56,64,128]{2,1,0:T(8,128)}, u32[]{:S(2)}, u32[]{:S(2)}) collective-permute-start(f32[56,64,128]{2,1,0:T(8,128)} %compact.5.refs_10_.refs_11_.refs_4_), channel_id=1, source_target_pairs={{6,0},{7,1},{0,2},{1,3},{2,4},{3,5},{4,6},{5,7},{14,8},{15,9},{8,1... | collective-permute-start | bytes 5505032 | tf_op jit(solution)/shard_map/ppermute | solution.py:30
  222.0 43.5 %collective-permute-start.1 = (f32[56,64,128]{2,1,0:T(8,128)S(1)}, f32[56,64,128]{2,1,0:T(8,128)}, u32[]{:S(2)}, u32[]{:S(2)}) collective-permute-start(f32[56,64,128]{2,1,0:T(8,128)S(1)} %copy-done), channel_id=1, source_target_pairs={{2,0},{3,1},{4,2},{5,3},{6,4},{7,5},{0,6},{1,7},{10,8},{11,9},{12,... | collective-permute-start | bytes 5505032 | tf_op jit(solution)/shard_map/ppermute | solution.py:30
  291.8 36.5 %collective-permute-start.9 = (f32[56,128,128]{2,1,0:T(8,128)}, f32[56,128,128]{2,1,0:T(8,128)}, u32[]{:S(2)}, u32[]{:S(2)}) collective-permute-start(f32[56,128,128]{2,1,0:T(8,128)} %collective-permute-done.3.refs_5_.refs_6_), channel_id=1, source_target_pairs={{8,0},{9,1},{10,2},{11,3},{12,4},{13,5},{14,6},{15,7},{0,8},{1,9},... | collective-permute-start | bytes 11010056 | tf_op jit(solution)/shard_map/ppermute | solution.py:30
  291.8 31.6 %collective-permute-start.5 = (f32[2,20,64,128]{3,2,1,0:T(8,128)S(1)}, f32[2,20,64,128]{3,2,1,0:T(8,128)S(1)}, u32[]{:S(2)}, u32[]{:S(2)}) collective-permute-start(f32[2,20,64,128]{3,2,1,0:T(8,128)S(1)} %get-tuple-element.48), channel_id=1, source_target_pairs={{1,0},{0,1},{3,2},{2,3},{5,4},{4,5},{7,6},{6,7},{9,8},{8,9},{11,10... | collective-permute-start | bytes 3932168 | tf_op jit(solution)/shard_map/ppermute | solution.py:30
  293.5 58.1 %collective-permute-start.8 = (f32[2,20,64,128]{3,2,1,0:T(8,128)}, f32[2,20,64,128]{3,2,1,0:T(8,128)}, u32[]{:S(2)}, u32[]{:S(2)}) collective-permute-start(f32[2,20,64,128]{3,2,1,0:T(8,128)} %get-tuple-element.51), channel_id=1, source_target_pairs={{1,0},{0,1},{3,2},{2,3},{5,4},{4,5},{7,6},{6,7},{9,8},{8,9},{11,10... | collective-permute-start | bytes 3932168 | tf_op jit(solution)/shard_map/ppermute | solution.py:30
  293.8 65.2 %collective-permute-start.12 = (f32[56,128,128]{2,1,0:T(8,128)}, f32[56,128,128]{2,1,0:T(8,128)}, u32[]{:S(2)}, u32[]{:S(2)}) collective-permute-start(f32[56,128,128]{2,1,0:T(8,128)} %compact.3.refs_8_.refs_9_.refs_2_), channel_id=1, source_target_pairs={{32,8},{33,9},{34,10},{35,11},{36,12},{37,13},{38,14},{39,15},{48,... | collective-permute-start | bytes 11010056 | tf_op jit(solution)/shard_map/ppermute | solution.py:30
  323.4 6.1 %copy-start.1 = (f32[2,20,64,128]{3,2,1,0:T(8,128)}, f32[2,20,64,128]{3,2,1,0:T(8,128)S(1)}, u32[]{:S(2)}) copy-start(f32[2,20,64,128]{3,2,1,0:T(8,128)S(1)} %collective-permute-done.5.refs_0_) | copy-start | bytes 3932164
  323.4 47.5 %collective-permute-start.6 = (f32[16,64,128]{2,1,0:T(8,128)}, f32[16,64,128]{2,1,0:T(8,128)}, u32[]{:S(2)}, u32[]{:S(2)}) collective-permute-start(f32[16,64,128]{2,1,0:T(8,128)} %slice_select_fusion.5), channel_id=1, source_target_pairs={{1,0},{0,1},{3,2},{2,3},{5,4},{4,5},{7,6},{6,7},{9,8},{8,9},{11,10... | collective-permute-start | bytes 1572872 | tf_op jit(solution)/shard_map/ppermute | solution.py:30
  326.3 29.5 %collective-permute-start.10 = (f32[20,64,128]{2,1,0:T(8,128)}, f32[20,64,128]{2,1,0:T(8,128)}, u32[]{:S(2)}, u32[]{:S(2)}) collective-permute-start(f32[20,64,128]{2,1,0:T(8,128)} %get-tuple-element.68), channel_id=1, source_target_pairs={{6,0},{7,1},{0,2},{1,3},{2,4},{3,5},{4,6},{5,7},{14,8},{15,9},{8,1... | collective-permute-start | bytes 1966088 | tf_op jit(solution)/shard_map/ppermute | solution.py:30
  328.3 29.3 %collective-permute-start.11 = (f32[20,64,128]{2,1,0:T(8,128)}, f32[20,64,128]{2,1,0:T(8,128)}, u32[]{:S(2)}, u32[]{:S(2)}) collective-permute-start(f32[20,64,128]{2,1,0:T(8,128)} %get-tuple-element.67), channel_id=1, source_target_pairs={{2,0},{3,1},{4,2},{5,3},{6,4},{7,5},{0,6},{1,7},{10,8},{11,9},{12,... | collective-permute-start | bytes 1966088 | tf_op jit(solution)/shard_map/ppermute | solution.py:30
  351.6 22.1 %collective-permute-start.7 = (f32[16,64,128]{2,1,0:T(8,128)}, f32[16,64,128]{2,1,0:T(8,128)}, u32[]{:S(2)}, u32[]{:S(2)}) collective-permute-start(f32[16,64,128]{2,1,0:T(8,128)} %slice_select_fusion.4), channel_id=1, source_target_pairs={{1,0},{0,1},{3,2},{2,3},{5,4},{4,5},{7,6},{6,7},{9,8},{8,9},{11,10... | collective-permute-start | bytes 1572872 | tf_op jit(solution)/shard_map/ppermute | solution.py:30
  355.7 21.4 %collective-permute-start.15 = (f32[20,64,128]{2,1,0:T(8,128)}, f32[20,64,128]{2,1,0:T(8,128)}, u32[]{:S(2)}, u32[]{:S(2)}) collective-permute-start(f32[20,64,128]{2,1,0:T(8,128)} %get-tuple-element.66), channel_id=1, source_target_pairs={{6,0},{7,1},{0,2},{1,3},{2,4},{3,5},{4,6},{5,7},{14,8},{15,9},{8,1... | collective-permute-start | bytes 1966088 | tf_op jit(solution)/shard_map/ppermute | solution.py:30
  357.6 19.5 %collective-permute-start.16 = (f32[20,64,128]{2,1,0:T(8,128)}, f32[20,64,128]{2,1,0:T(8,128)}, u32[]{:S(2)}, u32[]{:S(2)}) collective-permute-start(f32[20,64,128]{2,1,0:T(8,128)} %get-tuple-element.65), channel_id=1, source_target_pairs={{2,0},{3,1},{4,2},{5,3},{6,4},{7,5},{0,6},{1,7},{10,8},{11,9},{12,... | collective-permute-start | bytes 1966088 | tf_op jit(solution)/shard_map/ppermute | solution.py:30
  373.6 15.1 %collective-permute-start.13 = (f32[16,64,128]{2,1,0:T(8,128)}, f32[16,64,128]{2,1,0:T(8,128)}, u32[]{:S(2)}, u32[]{:S(2)}) collective-permute-start(f32[16,64,128]{2,1,0:T(8,128)} %collective-permute-done.7.refs_5_), channel_id=1, source_target_pairs={{6,0},{7,1},{0,2},{1,3},{2,4},{3,5},{4,6},{5,7},{14,8},{15,9},{8,1... | collective-permute-start | bytes 1572872 | tf_op jit(solution)/shard_map/ppermute | solution.py:30
  377.1 13.6 %collective-permute-start.14 = (f32[16,64,128]{2,1,0:T(8,128)}, f32[16,64,128]{2,1,0:T(8,128)}, u32[]{:S(2)}, u32[]{:S(2)}) collective-permute-start(f32[16,64,128]{2,1,0:T(8,128)} %collective-permute-done.6.refs_0_), channel_id=1, source_target_pairs={{2,0},{3,1},{4,2},{5,3},{6,4},{7,5},{0,6},{1,7},{10,8},{11,9},{12,... | collective-permute-start | bytes 1572872 | tf_op jit(solution)/shard_map/ppermute | solution.py:30
